TPU v7x, 32 devices: a whole 2x2x4 slice. The times are simulated.
32 devices in a mesh: tm: 4 (over z), elem: 8 (over y, x, core).
Axes of the slice: x: 2, y: 2, z: 4, core: 2. Of those that a mesh axis runs over, the one named last changes fastest.
Arguments:
- state: float32 [16, 5, 8, 125, 128], P('tm', None, 'elem'), may hold values from -6 to 6
- metric_scale: float32 [8, 125, 128], P('elem'), may hold values from 0.1 to 0.4
- flux_jacobians: float32 [3, 5, 5], replicated, may hold values from -1.5 to 1.5, as said below
- preconditioner: float32 [16, 5, 5, 8, 128], P('tm', None, None, 'elem'), may hold values from -0.04 to 0.24
- inflow: float32 [16, 5, 8, 25], P('tm', None, 'elem'), may hold values from -6 to 6
Outputs:
- new_state: float32 [16, 5, 8, 125, 128], P('tm', None, 'elem')
- final_residual: float32 [16, 5, 8, 125, 128], P('tm', None, 'elem')
Inputs may be any that keep to these rules, and one draw needn't show every extreme that they name: `flux_jacobians`: symmetric in its last two dimensions.
All inputs are finite; a program needn't handle non-finite values.
Results may differ from a plain program's by a relative error of at most 0.0001.
Values sent between devices are 32-bit elements; how exact they have to be, the bound alone decides.
No kernel may reach another device: no remote copies, remote signals or barrier semaphores. Data moves between devices by JAX's collectives and lax.ppermute only.
A program may use at most 128 MiB of HBM per device.

v0:
```python
import math

import jax
import jax.numpy as jnp
import numpy as np
from jax import lax
from jax.sharding import PartitionSpec as P

NI = 16
PR = 8
PASSES = 3


precise = lax.Precision.HIGHEST


def passed_along(block, axis, distance):
    devices = range(lax.axis_size(axis))
    route = [((i - distance) % len(devices), i) for i in devices]
    return lax.ppermute(block, axis, route)


def gll_derivative():
    points = np.array([-1.0, -math.sqrt(3.0 / 7.0), 0.0, math.sqrt(3.0 / 7.0), 1.0])
    legendre = (35.0 * points**4 - 30.0 * points**2 + 3.0) / 8.0
    identity = np.eye(5, dtype=bool)
    spacing = np.where(identity, 1.0, points[:, None] - points[None, :])
    matrix = legendre[:, None] / legendre[None, :] / spacing
    corner = np.array([-5.0, 0.0, 0.0, 0.0, 5.0])[None, :]
    return np.where(identity, corner, matrix)


def spectral_rows(row_ids, col_ids, count):
    offset = row_ids[:, None] - col_ids[None, :]
    parity = 1.0 - 2.0 * jnp.remainder(offset, 2).astype(jnp.float32)
    angle = jnp.pi * offset.astype(jnp.float32) / count
    diagonal = offset == 0
    sine = jnp.where(diagonal, 1.0, jnp.sin(angle))
    return jnp.where(diagonal, 0.0, 0.5 * parity * jnp.cos(angle) / sine)


def mix_variables(matrix, values):
    parts = [values[:, column] for column in range(values.shape[1])]
    mixed = []
    for row_index in range(values.shape[1]):
        total = matrix[row_index, 0] * parts[0]
        for column in range(1, values.shape[1]):
            total = total + matrix[row_index, column] * parts[column]
        mixed.append(total)
    return jnp.stack(mixed, axis=1)


def derive_along(table, values, node_axis):
    parts = [lax.index_in_dim(values, column, node_axis, keepdims=False) for column in range(5)]
    result = []
    for row_index in range(5):
        total = None
        for column in range(5):
            weight = float(table[row_index, column])
            if weight != 0.0:
                term = weight * parts[column]
                total = term if total is None else total + term
        result.append(total)
    return jnp.stack(result, axis=node_axis)


def lift_faces(lows, highs, beyond_low, beyond_high, matrix, damping, node_axis):
    jump_high = beyond_high - highs
    jump_low = beyond_low - lows
    high_term = 0.5 * (mix_variables(matrix, jump_high) - damping * jump_high)
    low_term = -0.5 * (mix_variables(matrix, jump_low) + damping * jump_low)
    middle = jnp.zeros_like(lows)
    return jnp.stack([low_term, middle, middle, middle, high_term], axis=node_axis)


def spatial_residual(fields, metric, jacobians, damping, table, inflow_nodes, position, reflect):
    volume = None
    for direction in range(3):
        derived = derive_along(table, fields, 2 + direction)
        term = mix_variables(jacobians[direction], derived)
        volume = term if volume is None else volume + term
    circ_lows = fields[:, :, 0]
    circ_highs = fields[:, :, 4]
    from_next = passed_along(circ_lows, "elem", -PR)
    from_prev = passed_along(circ_highs, "elem", PR)
    surface = lift_faces(circ_lows, circ_highs, from_prev, from_next, jacobians[0], damping[0], 2)
    rad_lows = fields[:, :, :, 0]
    rad_highs = fields[:, :, :, 4]
    above = passed_along(rad_lows, "elem", -1)
    below = passed_along(rad_highs, "elem", 1)
    beyond_high = jnp.where(position == PR - 1, reflect * rad_highs, above)
    beyond_low = jnp.where(position == 0, reflect * rad_lows, below)
    surface = surface + lift_faces(
        rad_lows, rad_highs, beyond_low, beyond_high, jacobians[1], damping[1], 3
    )
    axial_lows = fields[:, :, :, :, 0]
    axial_highs = fields[:, :, :, :, 4]
    beyond_high = jnp.concatenate([axial_lows[..., 1:], axial_highs[..., -1:]], axis=4)
    beyond_low = jnp.concatenate([inflow_nodes, axial_highs[..., :-1]], axis=4)
    surface = surface + lift_faces(
        axial_lows, axial_highs, beyond_low, beyond_high, jacobians[2], damping[2], 4
    )
    return metric * (volume + 10.0 * surface)


def per_device(state, metric_scale, flux_jacobians, preconditioner, inflow):
    inst_dev = state.shape[0]
    variables = state.shape[1]
    axial_cells = state.shape[4]
    table = gll_derivative()
    damping = jnp.max(jnp.sum(jnp.abs(flux_jacobians), axis=2), axis=1)
    grid_shape = (inst_dev, variables, 5, 5, 5, axial_cells)
    metric = metric_scale.reshape(1, 1, 5, 5, 5, axial_cells)
    inflow_nodes = inflow.reshape(inst_dev, variables, 5, 5, 1)
    position = (lax.axis_index("elem") + PR // 2) % PR
    reflect = jnp.array([1.0, 1.0, -1.0, 1.0, 1.0], dtype=jnp.float32).reshape(
        1, variables, 1, 1, 1
    )
    my_rows = lax.axis_index("tm") * inst_dev + jnp.arange(inst_dev, dtype=jnp.int32)
    flattened = state.reshape(inst_dev, -1)
    row_ids = jnp.arange(lax.axis_size("tm") * inst_dev, dtype=jnp.int32)
    weights = spectral_rows(row_ids, my_rows, NI)
    spectral = lax.psum_scatter(
        jnp.dot(weights, flattened, precision=precise, preferred_element_type=jnp.float32),
        "tm",
        scatter_dimension=0,
        tiled=True,
    )
    spectral = spectral.reshape(grid_shape)

    def full_residual(current):
        return (
            spatial_residual(
                current, metric, flux_jacobians, damping, table, inflow_nodes, position, reflect
            )
            + spectral
        )

    iterate = state.reshape(grid_shape)
    for sweep_index in range(PASSES):
        residual = full_residual(iterate).reshape(inst_dev, variables, 125, axial_cells)
        parts = [residual[:, column] for column in range(variables)]
        updates = []
        for row_index in range(variables):
            total = preconditioner[:, row_index, 0] * parts[0]
            for column in range(1, variables):
                total = total + preconditioner[:, row_index, column] * parts[column]
            updates.append(total)
        update = jnp.stack(updates, axis=1)
        iterate = iterate - update.reshape(grid_shape)
    final_residual = full_residual(iterate)
    return (iterate.reshape(state.shape), final_residual.reshape(state.shape))


def solution(mesh):
    in_specs = (
        P("tm", None, "elem", None, None),
        P("elem", None, None),
        P(),
        P("tm", None, None, "elem", None),
        P("tm", None, "elem", None),
    )
    out_specs = (P("tm", None, "elem", None, None), P("tm", None, "elem", None, None))
    return jax.shard_map(
        per_device, mesh=mesh, in_specs=in_specs, out_specs=out_specs, check_vma=False
    )
```

profile of v0, /device:TPU:0, one launch (start us, length us, event | category | flops | bytes accessed | tf_op | source)
XLA Modules:
  0.0 757.3 jit_solution(18443264665343997203)
XLA Ops:
  7.2 4.5 reduce
  12.3 6.1 fusion.259
  28.1 3.4 collective-permute-start
  38.6 3.4 multiply_add_fusion.68
  43.6 3.3 multiply_add_fusion.78
  59.0 3.4 multiply_add_fusion.70
  63.1 3.4 multiply_add_fusion.69
  67.2 3.4 multiply_add_fusion.67
  70.6 3.4 multiply_add_fusion.66
  77.3 3.4 multiply_add_fusion.64
  80.7 3.4 multiply_add_fusion.77
  147.9 3.3 constant_dynamic-update-slice_fusion.46
  163.7 3.3 constant_dynamic-update-slice_fusion.41
  176.6 3.3 constant_dynamic-update-slice_fusion.52
  192.5 3.3 constant_dynamic-update-slice_fusion.57
  217.6 3.3 multiply_add_fusion.58
  220.9 3.4 multiply_add_fusion.57
  244.6 3.4 multiply_add_fusion.50
  248.0 3.4 multiply_add_fusion.49
  277.5 3.4 constant_dynamic-update-slice_fusion.122
  293.5 3.3 constant_dynamic-update-slice_fusion.127
  304.5 3.4 multiply_add_fusion.48
  307.9 6.5 multiply_add_fusion.44
  314.4 6.6 multiply_add_fusion.45
  363.2 3.3 constant_dynamic-update-slice_fusion.116
  379.7 3.3 constant_dynamic-update-slice_fusion.111
  396.7 3.3 multiply_add_fusion.38
  400.0 3.4 multiply_add_fusion.37
  424.2 3.4 multiply_add_fusion.30
  427.5 3.4 multiply_add_fusion.29
  453.3 3.3 constant_dynamic-update-slice_fusion.192
  464.0 3.4 multiply_add_fusion.28
  470.6 3.4 multiply_add_fusion.26
  477.2 3.3 multiply_add_fusion.24
  524.3 3.3 constant_dynamic-update-slice_fusion.186
  540.8 3.3 constant_dynamic-update-slice_fusion.181
  554.5 3.3 constant_dynamic-update-slice_fusion.197
  572.9 3.4 multiply_add_fusion.8
  579.6 3.4 multiply_add_fusion.6
  586.1 3.3 multiply_add_fusion.4
  590.8 3.3 multiply_add_fusion.18
  594.0 3.4 multiply_add_fusion.17
  617.8 3.4 multiply_add_fusion.10
  621.1 3.4 multiply_add_fusion.9
  688.4 3.3 constant_dynamic-update-slice_fusion.256
  704.9 3.3 constant_dynamic-update-slice_fusion.251
  718.6 3.4 constant_dynamic-update-slice_fusion.262
  734.6 3.3 constant_dynamic-update-slice_fusion.267
  (532 shorter events, 569.5 us)
Async XLA Ops:
  7.2 199.6 %all-reduce.3.cloned.1.call-start = ((), (), s32[]{:S(2)}) async-start(), calls=%async_computation | async-start | bytes 10240000
  20.9 84.3 %collective-permute-start.2 = (f32[4,5,5,5,128]{4,0,3,2,1:T(4,128)}, f32[4,5,5,5,128]{4,0,3,2,1:T(4,128)}, u32[]{:S(2)}, u32[]{:S(2)}) collective-permute-start(f32[4,5,5,5,128]{4,0,3,2,1:T(4,128)} %get-tuple-element.103), channel_id=1, source_target_pairs={{7,0},{0,1},{1,2},{2,3},{3,4},{4,5},{5,6},{6,7},{15,8},{8,9},{9,10... | collective-permute-start | bytes 768008 | tf_op jit(solution)/shard_map/ppermute | solution.py:20
  21.4 10.3 %copy-start.45 = (f32[3,5,5]{2,0,1:T(4,128)S(1)}, f32[3,5,5]{2,0,1:T(4,128)}, u32[]{:S(2)}) copy-start(f32[3,5,5]{2,0,1:T(4,128)} %param.8) | copy-start | bytes 904
  21.4 83.8 %collective-permute-start.3 = (f32[4,5,5,5,128]{4,0,3,2,1:T(4,128)}, f32[4,5,5,5,128]{4,0,3,2,1:T(4,128)}, u32[]{:S(2)}, u32[]{:S(2)}) collective-permute-start(f32[4,5,5,5,128]{4,0,3,2,1:T(4,128)} %get-tuple-element.104), channel_id=1, source_target_pairs={{1,0},{2,1},{3,2},{4,3},{5,4},{6,5},{7,6},{0,7},{9,8},{10,9},{11,1... | collective-permute-start | bytes 768008 | tf_op jit(solution)/shard_map/ppermute | solution.py:20
  25.1 80.1 %collective-permute-start.1 = (f32[4,5,5,5,128]{4,0,3,2,1:T(4,128)}, f32[4,5,5,5,128]{4,0,3,2,1:T(4,128)}, u32[]{:S(2)}, u32[]{:S(2)}) collective-permute-start(f32[4,5,5,5,128]{4,0,3,2,1:T(4,128)} %get-tuple-element.106), channel_id=1, source_target_pairs={{0,0},{1,1},{2,2},{3,3},{4,4},{5,5},{6,6},{7,7},{8,8},{9,9},{10,10... | collective-permute-start | bytes 768008 | tf_op jit(solution)/shard_map/ppermute | solution.py:20
  28.1 77.2 %collective-permute-start = (f32[4,5,5,5,128]{4,0,3,2,1:T(4,128)}, f32[4,5,5,5,128]{4,0,3,2,1:T(4,128)}, u32[]{:S(2)}, u32[]{:S(2)}) collective-permute-start(f32[4,5,5,5,128]{4,0,3,2,1:T(4,128)} %get-tuple-element.105), channel_id=1, source_target_pairs={{0,0},{1,1},{2,2},{3,3},{4,4},{5,5},{6,6},{7,7},{8,8},{9,9},{10,10... | collective-permute-start | bytes 768008 | tf_op jit(solution)/shard_map/ppermute | solution.py:20
  36.8 354.3 %copy-start.39 = (f32[4,1,1,1,128]{4,3,2,1,0:T(1,128)}, f32[4,1,1,1,128]{4,3,2,1,0:T(1,128)S(1)}, u32[]{:S(2)}) copy-start(f32[4,1,1,1,128]{4,3,2,1,0:T(1,128)S(1)} %get-tuple-element.144) | copy-start | bytes 6148
  36.8 354.3 %copy-start.41 = (f32[4,1,1,1,128]{4,3,2,1,0:T(1,128)}, f32[4,1,1,1,128]{4,3,2,1,0:T(1,128)S(1)}, u32[]{:S(2)}) copy-start(f32[4,1,1,1,128]{4,3,2,1,0:T(1,128)S(1)} %get-tuple-element.145) | copy-start | bytes 6148
  36.8 354.3 %copy-start.43 = (f32[4,1,1,1,128]{4,3,2,1,0:T(1,128)}, f32[4,1,1,1,128]{4,3,2,1,0:T(1,128)S(1)}, u32[]{:S(2)}) copy-start(f32[4,1,1,1,128]{4,3,2,1,0:T(1,128)S(1)} %get-tuple-element.146) | copy-start | bytes 6148
  43.6 4.2 copy-start
  67.2 3.4 copy-start.11
  77.2 3.5 copy-start.1
  80.7 7.4 copy-start.12
  92.7 5.4 copy-start.33
  96.0 2.9 copy-start.34
  96.0 4.3 copy-start.46
  98.9 4.9 copy-start.37
  98.9 4.9 copy-start.49
  98.9 6.1 copy-start.35
  101.4 3.9 copy-start.47
  206.8 2.1 copy-start.13
  208.9 2.9 copy-start.2
  251.3 17.7 %collective-permute-start.6 = (f32[4,5,5,5,128]{4,0,3,2,1:T(4,128)}, f32[4,5,5,5,128]{4,0,3,2,1:T(4,128)}, u32[]{:S(2)}, u32[]{:S(2)}) collective-permute-start(f32[4,5,5,5,128]{4,0,3,2,1:T(4,128)} %get-tuple-element.90), channel_id=1, source_target_pairs={{7,0},{0,1},{1,2},{2,3},{3,4},{4,5},{5,6},{6,7},{15,8},{8,9},{9,10... | collective-permute-start | bytes 768008 | tf_op jit(solution)/shard_map/ppermute | solution.py:20
  251.4 17.6 %collective-permute-start.7 = (f32[4,5,5,5,128]{4,0,3,2,1:T(4,128)}, f32[4,5,5,5,128]{4,0,3,2,1:T(4,128)}, u32[]{:S(2)}, u32[]{:S(2)}) collective-permute-start(f32[4,5,5,5,128]{4,0,3,2,1:T(4,128)} %get-tuple-element.91), channel_id=1, source_target_pairs={{1,0},{2,1},{3,2},{4,3},{5,4},{6,5},{7,6},{0,7},{9,8},{10,9},{11,1... | collective-permute-start | bytes 768008 | tf_op jit(solution)/shard_map/ppermute | solution.py:20
  255.0 14.0 %collective-permute-start.5 = (f32[4,5,5,5,128]{4,0,3,2,1:T(4,128)}, f32[4,5,5,5,128]{4,0,3,2,1:T(4,128)}, u32[]{:S(2)}, u32[]{:S(2)}) collective-permute-start(f32[4,5,5,5,128]{4,0,3,2,1:T(4,128)} %get-tuple-element.93), channel_id=1, source_target_pairs={{0,0},{1,1},{2,2},{3,3},{4,4},{5,5},{6,6},{7,7},{8,8},{9,9},{10,10... | collective-permute-start | bytes 768008 | tf_op jit(solution)/shard_map/ppermute | solution.py:20
  257.9 11.1 %collective-permute-start.4 = (f32[4,5,5,5,128]{4,0,3,2,1:T(4,128)}, f32[4,5,5,5,128]{4,0,3,2,1:T(4,128)}, u32[]{:S(2)}, u32[]{:S(2)}) collective-permute-start(f32[4,5,5,5,128]{4,0,3,2,1:T(4,128)} %get-tuple-element.92), channel_id=1, source_target_pairs={{0,0},{1,1},{2,2},{3,3},{4,4},{5,5},{6,6},{7,7},{8,8},{9,9},{10,10... | collective-permute-start | bytes 768008 | tf_op jit(solution)/shard_map/ppermute | solution.py:20
  262.9 2.2 copy-start.22
  277.5 25.6 %copy-start.10 = (f32[4,5,5,5,5,128]{5,0,3,2,4,1:T(4,128)S(1)}, f32[4,5,5,5,5,128]{5,0,3,2,4,1:T(4,128)}, u32[]{:S(2)}) copy-start(f32[4,5,5,5,5,128]{5,0,3,2,4,1:T(4,128)} %constant_dynamic-update-slice_fusion.91) | copy-start | bytes 3840004
  277.5 25.6 %copy-start.32 = (f32[4,5,5,5,1,1]{5,0,3,2,1,4:T(4,128)S(1)}, f32[4,5,5,5,1,1]{5,0,3,2,1,4:T(4,128)}, u32[]{:S(2)}) copy-start(f32[4,5,5,5,1,1]{5,0,3,2,1,4:T(4,128)} %copy.770) | copy-start | bytes 6004
  431.7 10.4 %copy-start.8 = (f32[4,5,5,5,128]{4,0,3,2,1:T(4,128)}, f32[4,5,5,5,128]{4,0,3,2,1:T(4,128)S(1)}, u32[]{:S(2)}) copy-start(f32[4,5,5,5,128]{4,0,3,2,1:T(4,128)S(1)} %get-tuple-element.63) | copy-start | bytes 768004
  431.7 13.7 %collective-permute-start.10 = (f32[4,5,5,5,128]{4,0,3,2,1:T(4,128)}, f32[4,5,5,5,128]{4,0,3,2,1:T(4,128)}, u32[]{:S(2)}, u32[]{:S(2)}) collective-permute-start(f32[4,5,5,5,128]{4,0,3,2,1:T(4,128)} %get-tuple-element.68), channel_id=1, source_target_pairs={{7,0},{0,1},{1,2},{2,3},{3,4},{4,5},{5,6},{6,7},{15,8},{8,9},{9,10... | collective-permute-start | bytes 768008 | tf_op jit(solution)/shard_map/ppermute | solution.py:20
  431.8 13.7 %collective-permute-start.11 = (f32[4,5,5,5,128]{4,0,3,2,1:T(4,128)}, f32[4,5,5,5,128]{4,0,3,2,1:T(4,128)}, u32[]{:S(2)}, u32[]{:S(2)}) collective-permute-start(f32[4,5,5,5,128]{4,0,3,2,1:T(4,128)} %get-tuple-element.69), channel_id=1, source_target_pairs={{1,0},{2,1},{3,2},{4,3},{5,4},{6,5},{7,6},{0,7},{9,8},{10,9},{11,1... | collective-permute-start | bytes 768008 | tf_op jit(solution)/shard_map/ppermute | solution.py:20
  434.4 46.3 %collective-permute-start.9 = (f32[4,5,5,5,128]{4,0,3,2,1:T(4,128)}, f32[4,5,5,5,128]{4,0,3,2,1:T(4,128)}, u32[]{:S(2)}, u32[]{:S(2)}) collective-permute-start(f32[4,5,5,5,128]{4,0,3,2,1:T(4,128)} %get-tuple-element.71), channel_id=1, source_target_pairs={{0,0},{1,1},{2,2},{3,3},{4,4},{5,5},{6,6},{7,7},{8,8},{9,9},{10,10... | collective-permute-start | bytes 768008 | tf_op jit(solution)/shard_map/ppermute | solution.py:20
  437.3 43.3 %collective-permute-start.8 = (f32[4,5,5,5,128]{4,0,3,2,1:T(4,128)}, f32[4,5,5,5,128]{4,0,3,2,1:T(4,128)}, u32[]{:S(2)}, u32[]{:S(2)}) collective-permute-start(f32[4,5,5,5,128]{4,0,3,2,1:T(4,128)} %get-tuple-element.70), channel_id=1, source_target_pairs={{0,0},{1,1},{2,2},{3,3},{4,4},{5,5},{6,6},{7,7},{8,8},{9,9},{10,10... | collective-permute-start | bytes 768008 | tf_op jit(solution)/shard_map/ppermute | solution.py:20
  565.9 1.8 copy-start.19
  624.5 19.7 %collective-permute-start.14 = (f32[4,5,5,5,128]{4,0,3,2,1:T(4,128)}, f32[4,5,5,5,128]{4,0,3,2,1:T(4,128)}, u32[]{:S(2)}, u32[]{:S(2)}) collective-permute-start(f32[4,5,5,5,128]{4,0,3,2,1:T(4,128)} %get-tuple-element.55), channel_id=1, source_target_pairs={{7,0},{0,1},{1,2},{2,3},{3,4},{4,5},{5,6},{6,7},{15,8},{8,9},{9,10... | collective-permute-start | bytes 768008 | tf_op jit(solution)/shard_map/ppermute | solution.py:20
  624.6 19.6 %collective-permute-start.15 = (f32[4,5,5,5,128]{4,0,3,2,1:T(4,128)}, f32[4,5,5,5,128]{4,0,3,2,1:T(4,128)}, u32[]{:S(2)}, u32[]{:S(2)}) collective-permute-start(f32[4,5,5,5,128]{4,0,3,2,1:T(4,128)} %get-tuple-element.56), channel_id=1, source_target_pairs={{1,0},{2,1},{3,2},{4,3},{5,4},{6,5},{7,6},{0,7},{9,8},{10,9},{11,1... | collective-permute-start | bytes 768008 | tf_op jit(solution)/shard_map/ppermute | solution.py:20
  628.0 16.2 %collective-permute-start.13 = (f32[4,5,5,5,128]{4,0,3,2,1:T(4,128)}, f32[4,5,5,5,128]{4,0,3,2,1:T(4,128)}, u32[]{:S(2)}, u32[]{:S(2)}) collective-permute-start(f32[4,5,5,5,128]{4,0,3,2,1:T(4,128)} %get-tuple-element.58), channel_id=1, source_target_pairs={{0,0},{1,1},{2,2},{3,3},{4,4},{5,5},{6,6},{7,7},{8,8},{9,9},{10,10... | collective-permute-start | bytes 768008 | tf_op jit(solution)/shard_map/ppermute | solution.py:20
  630.9 13.3 %collective-permute-start.12 = (f32[4,5,5,5,128]{4,0,3,2,1:T(4,128)}, f32[4,5,5,5,128]{4,0,3,2,1:T(4,128)}, u32[]{:S(2)}, u32[]{:S(2)}) collective-permute-start(f32[4,5,5,5,128]{4,0,3,2,1:T(4,128)} %get-tuple-element.57), channel_id=1, source_target_pairs={{0,0},{1,1},{2,2},{3,3},{4,4},{5,5},{6,6},{7,7},{8,8},{9,9},{10,10... | collective-permute-start | bytes 768008 | tf_op jit(solution)/shard_map/ppermute | solution.py:20
  634.2 2.3 copy-start.29
  635.4 1.9 copy-start.7
  635.4 2.2 copy-start.27
  641.8 2.4 copy-start.48
  718.6 25.5 %copy-start.30 = (f32[4,5,5,5,1,127]{5,0,3,2,1,4:T(4,128)S(1)}, f32[4,5,5,5,1,127]{5,0,3,2,1,4:T(4,128)}, u32[]{:S(2)}) copy-start(f32[4,5,5,5,1,127]{5,0,3,2,1,4:T(4,128)} %get-tuple-element.108) | copy-start | bytes 762004
  718.6 25.5 %copy-start.31 = (f32[4,5,5,5,1,1]{5,0,3,2,1,4:T(4,128)S(1)}, f32[4,5,5,5,1,1]{5,0,3,2,1,4:T(4,128)}, u32[]{:S(2)}) copy-start(f32[4,5,5,5,1,1]{5,0,3,2,1,4:T(4,128)} %copy.871) | copy-start | bytes 6004
  744.1 1.7 copy-start.17
  744.1 1.7 copy-start.21
  745.3 1.8 copy-start.15
  (19 other events, 21.7 us)
Sparse Core Ops, SparseCore 0:
  18.6 187.9 all-reduce.2
where the time goes:
time: 772 us; the launch traced here: 757 us
  other arithmetic  635 us (82%)
  local copies, waits for them, and re-layouts  63 us (8%)
  starting transfers between devices  35.5 us (5%)
  between operations  17.5 us (2%)
    unnamed x157, other arithmetic  322 us
    add x58, other arithmetic, mix_variables(): total = total + matrix[row_index, column] * parts[column]  196 us
    another operation x24, other arithmetic, mix_variables(): return jnp.stack(mixed, axis=1)  76 us
    ppermute x16, starting transfers between devices, passed_along(): return lax.ppermute(block, axis, route)  35.4 us
    unnamed x168, local copies, waits for them, and re-layouts  32.2 us
  transfers between devices with their start and end apart: 17, of which 0 were waited for; matrix products, arithmetic and copies ran while one was open for 30% of the time, Pallas kernels for 0%

commit v1 on v0

v1 whole, which is shorter than its diff:
```python
import math

import jax
import jax.numpy as jnp
import ml_dtypes
import numpy as np
from jax import lax
from jax.experimental import pallas as pl
from jax.experimental.pallas import tpu as pltpu
from jax.sharding import PartitionSpec as P

PR = 8
PASSES = 3
GROUPS = 2
ROWS = 128
FACE = 32
HIGH = 96

F32 = jnp.float32
BF16 = jnp.bfloat16


def gll_derivative():
    points = np.array([-1.0, -math.sqrt(3.0 / 7.0), 0.0, math.sqrt(3.0 / 7.0), 1.0])
    legendre = (35.0 * points**4 - 30.0 * points**2 + 3.0) / 8.0
    identity = np.eye(5, dtype=bool)
    spacing = np.where(identity, 1.0, points[:, None] - points[None, :])
    matrix = legendre[:, None] / legendre[None, :] / spacing
    corner = np.array([-5.0, 0.0, 0.0, 0.0, 5.0])[None, :]
    return np.where(identity, corner, matrix)


def coupling_value(offset, count):
    offset = offset % count
    if offset == 0:
        return 0.0
    angle = math.pi * offset / count
    return 0.5 * (-1.0) ** offset * math.cos(angle) / math.sin(angle)


def node_rows():
    rows = np.zeros(125, dtype=np.int64)
    free = list(range(25, HIGH)) + list(range(HIGH + 25, ROWS))
    for i in range(5):
        for j in range(5):
            for k in range(5):
                node = 25 * i + 5 * j + k
                if j == 0:
                    rows[node] = 5 * i + k
                elif j == 4:
                    rows[node] = HIGH + 5 * i + k
                else:
                    rows[node] = free.pop(0)
    return rows


def split_bf16(matrix):
    high = matrix.astype(np.float32).astype(ml_dtypes.bfloat16)
    low = (matrix - high.astype(np.float64)).astype(np.float32).astype(ml_dtypes.bfloat16)
    return high, low


def tables(own_circ):
    table = gll_derivative()
    eye = np.eye(5)
    first, last = np.diag([1.0, 0, 0, 0, 0]), np.diag([0, 0, 0, 0, 1.0])
    to_first, to_last = np.zeros((5, 5)), np.zeros((5, 5))
    to_first[0, 4] = 1.0
    to_last[4, 0] = 1.0

    def along(matrix, direction):
        parts = [eye, eye, eye]
        parts[direction] = matrix
        return np.kron(np.kron(parts[0], parts[1]), parts[2])

    rows = node_rows()
    order = np.zeros((ROWS, ROWS))
    order[rows, np.arange(125)] = 1.0

    def placed(matrix):
        return order[:, :125] @ matrix @ order[:, :125].T

    mix, damp = [], []
    for d in range(3):
        mix.append(placed(along(table - 5.0 * last + 5.0 * first, d)))
        damp.append(placed(along(5.0 * last + 5.0 * first, d)))
    if own_circ:
        mix[0] = mix[0] + placed(along(5.0 * to_last - 5.0 * to_first, 0))
        damp[0] = damp[0] + placed(along(-5.0 * to_last - 5.0 * to_first, 0))
    none = np.zeros((ROWS, ROWS))
    axial_mix = placed(along(5.0 * to_last - 5.0 * to_first, 2))
    axial_damp = placed(along(-5.0 * to_last - 5.0 * to_first, 2))
    fluxes = np.concatenate(
        [
            np.concatenate([mix[0], none], 1),
            np.concatenate([mix[1], none], 1),
            np.concatenate([mix[2], axial_mix], 1),
        ],
        0,
    )
    fluxes = np.stack(split_bf16(fluxes))
    dampers = np.stack(
        [
            np.concatenate([damp[0], none], 1),
            np.concatenate([damp[1], none], 1),
            np.concatenate([damp[2], axial_damp], 1),
        ]
    ).astype(np.float32)
    return order, fluxes, dampers


def lane_masks(lanes):
    rows = node_rows()
    k_first, k_last = rows[0::5], rows[4::5]
    masks = np.zeros((3, ROWS, lanes), dtype=np.float32)
    masks[0][k_last, 1:] = 1.0
    masks[1][k_first, :-1] = 1.0
    masks[2][k_last, -1] = 5.0
    return masks


def halves(values):
    high = values.astype(BF16)
    low = (values - high.astype(F32)).astype(BF16)
    return high, low


def dot32(a, b):
    return jnp.dot(a, b, preferred_element_type=F32)


def reorder(matrix, values, terms):
    total = None
    for _ in range(terms):
        part = values.astype(BF16)
        moved = dot32(matrix, part)
        total = moved if total is None else total + moved
        values = values - part.astype(F32)
    return total


def mixed(weights, parts):
    total = weights[0] * parts[0]
    for weight, part in zip(weights[1:], parts[1:]):
        total = total + weight * part
    return total


VMEM_LIMIT = 48 * 2**20


def call(kernel, outs, ins, in_spaces, out_spaces=None, scratch=(), flops=0, alias=None, name=None):
    out_spaces = out_spaces or ["v"] * len(outs)
    space = {"v": pltpu.VMEM, "s": pltpu.SMEM, "a": pl.ANY}
    nbytes = sum(int(np.prod(x.shape)) * x.dtype.itemsize for x in list(ins) + list(outs))
    return pl.pallas_call(
        kernel,
        out_shape=outs,
        in_specs=[pl.BlockSpec(memory_space=space[s]) for s in in_spaces],
        out_specs=[pl.BlockSpec(memory_space=space[s]) for s in out_spaces],
        scratch_shapes=list(scratch),
        input_output_aliases=alias or {},
        compiler_params=pltpu.CompilerParams(vmem_limit_bytes=VMEM_LIMIT),
        cost_estimate=pl.CostEstimate(flops=flops, bytes_accessed=nbytes, transcendentals=0),
        name=name,
    )(*ins)


def shape(*dims, dtype=F32):
    return jax.ShapeDtypeStruct(dims, dtype)


def per_device(state, metric_scale, flux_jacobians, preconditioner, inflow):
    inst, nv, _, nodes, lanes = state.shape
    n_tm = lax.axis_size("tm")
    n_elem = lax.axis_size("elem")
    count = inst * n_tm
    own_circ = n_elem == PR
    block = ROWS // n_tm
    groups = GROUPS if inst % GROUPS == 0 else 1
    per = inst // groups
    order, flux_table, damp_table = tables(own_circ)
    order_b = order.astype(ml_dtypes.bfloat16)
    back_b = np.ascontiguousarray(order.T).astype(ml_dtypes.bfloat16)
    masks = lane_masks(lanes)
    node_row = node_rows()
    inlet_table = np.zeros((ROWS, ROWS), dtype=np.float32)
    inlet_table[node_row[0::5], np.arange(25)] = 1.0

    damping = jnp.max(jnp.sum(jnp.abs(flux_jacobians), axis=2), axis=1)
    coef = jnp.concatenate([flux_jacobians.reshape(-1), damping])
    precond = preconditioner.reshape(inst, nv, nv, lanes)
    inlet = inflow.reshape(inst, nv, 25)
    inlet = jnp.stack(
        [
            -5.0
            * (
                sum(flux_jacobians[2, v, w] * inlet[:, w] for w in range(nv))
                + damping[2] * inlet[:, v]
            )
            for v in range(nv)
        ],
        axis=1,
    ).reshape(inst * nv, 25)
    inlet = jnp.pad(inlet, ((0, ROWS - inst * nv), (0, ROWS - 25)))

    def jac(ref, d, v, w):
        return ref[(d * nv + v) * nv + w]

    def damp(ref, d):
        return ref[3 * nv * nv + d]

    def pack_kernel(state_ref, *refs):
        outs, padded, sem = refs[:n_tm], refs[n_tm], refs[n_tm + 1]
        copies = []
        for n in range(inst):
            for v in range(nv):
                padded[n, v, pl.ds(ROWS - 8, 8), :] = jnp.zeros((8, lanes), F32)
        for n in range(inst):
            for v in range(nv):
                copies.append(
                    pltpu.make_async_copy(
                        state_ref.at[n, v, :, 0, :],
                        padded.at[n, v, pl.ds(0, nodes), :],
                        sem.at[n, v],
                    )
                )
        for copy in copies:
            copy.start()
        for copy in copies:
            copy.wait()
        me = lax.axis_index("tm")
        for d in range(n_tm):
            start = pl.multiple_of(lax.rem(me + d, n_tm) * block, block)
            for n in range(inst):
                for v in range(nv):
                    outs[d][n, v] = padded[n, v, pl.ds(start, block), :]

    piece = shape(inst, nv, block, lanes)
    packed = call(
        pack_kernel,
        [piece] * n_tm + [shape(inst, nv, ROWS, lanes)],
        [state.reshape(inst, nv, nodes, 1, lanes)],
        "a",
        scratch=[pltpu.SemaphoreType.DMA((inst, nv))],
        name="pack",
    )
    pieces, padded = packed[:n_tm], packed[n_tm]

    def along_tm(x, d):
        return lax.ppermute(x, "tm", [(i, (i + d) % n_tm) for i in range(n_tm)])

    def along_elem(x, d):
        return lax.ppermute(x, "elem", [(i, (i + d) % n_elem) for i in range(n_elem)])

    arrived = [pieces[0]] + [along_tm(pieces[d], d) for d in range(1, n_tm)]

    def prep_kernel(
        padded_ref, metric_ref, coef_ref, order_ref, flux_ref, damp_ref, inlet_ref, inlet_table_ref,
        x_ref, lo_ref, hi_ref, m_ref, mf_ref, lhs_ref, col_ref, buf, sem,
    ):
        buf[pl.ds(ROWS - 8, 8), :] = jnp.zeros((8, lanes), F32)
        copy = pltpu.make_async_copy(metric_ref.at[:, 0, :], buf.at[pl.ds(0, nodes), :], sem)
        copy.start()
        copy.wait()
        metric = reorder(order_ref[...], buf[...], 3)
        m_ref[...] = metric
        row = lax.broadcasted_iota(jnp.int32, (FACE, lanes), 0)
        mf_ref[0] = jnp.where(row < 25, metric[0:FACE], 0.0)
        mf_ref[1] = jnp.where(row < 25, metric[HIGH:ROWS], 0.0)
        for part in range(2):
            lhs_ref[part, 0 : 3 * ROWS, :] = flux_ref[part]
        total = damp(coef_ref, 0) * damp_ref[0]
        for d in range(1, 3):
            total = total + damp(coef_ref, d) * damp_ref[d]
        high, low = halves(total)
        lhs_ref[0, 3 * ROWS : 4 * ROWS, :] = high
        lhs_ref[1, 3 * ROWS : 4 * ROWS, :] = low
        cols = lax.dot_general(
            inlet_table_ref[...],
            inlet_ref[...],
            (((1,), (1,)), ((), ())),
            precision=lax.Precision.HIGHEST,
            preferred_element_type=F32,
        )
        col_ref[...] = metric[:, 0:1] * cols
        for n in range(inst):
            natural = jnp.concatenate([padded_ref[n, v] for v in range(nv)], axis=1)
            moved = reorder(order_ref[...], natural, 3)
            for v in range(nv):
                part = moved[:, v * lanes : (v + 1) * lanes]
                x_ref[n, v] = part
                lo_ref[n, v] = part[0:FACE]
                hi_ref[n, v] = part[HIGH:ROWS]

    x0, lo0, hi0, metric, metric_face, lhs, inlet_cols = call(
        prep_kernel,
        [
            shape(inst, nv, ROWS, lanes),
            shape(inst, nv, FACE, lanes),
            shape(inst, nv, FACE, lanes),
            shape(ROWS, lanes),
            shape(2, FACE, lanes),
            shape(2, 4 * ROWS, 2 * ROWS, dtype=BF16),
            shape(ROWS, ROWS),
        ],
        [
            padded,
            metric_scale.reshape(nodes, 1, lanes),
            coef,
            order_b,
            flux_table,
            damp_table,
            inlet,
            inlet_table,
        ],
        "vasvvvvv",
        scratch=[pltpu.VMEM((ROWS, lanes), F32), pltpu.SemaphoreType.DMA],
        name="prep",
    )

    def bulk(x, coef_ref, lhs_ref, masks_ref, metric_value):
        wide = jnp.concatenate(x, axis=1)
        shifted = jnp.concatenate(
            [
                pltpu.roll(part, 1, 1) * masks_ref[0] + pltpu.roll(part, lanes - 1, 1) * masks_ref[1]
                for part in x
            ],
            axis=1,
        )
        high, low = halves(jnp.concatenate([wide, shifted], axis=0))
        grads = dot32(lhs_ref[0], high) + dot32(lhs_ref[1], high) + dot32(lhs_ref[0], low)

        def grad(d, w):
            return grads[d * ROWS : (d + 1) * ROWS, w * lanes : (w + 1) * lanes]

        edge = [masks_ref[2] * part for part in x]
        parts = [grad(0, w) for w in range(nv)] + [grad(1, w) for w in range(nv)]
        parts = parts + [grad(2, w) + edge[w] for w in range(nv)]
        result = []
        for v in range(nv):
            weights = [jac(coef_ref, d, v, w) for d in range(3) for w in range(nv)]
            total = mixed(weights, parts) + grad(3, v) - damp(coef_ref, 2) * edge[v]
            result.append(metric_value * total)
        return result

    def whole(lo_ref, z_ref, hi_ref, n, at, v):
        return jnp.concatenate([lo_ref[n, v], z_ref[at, v, FACE:HIGH, :], hi_ref[n, v]], axis=0)

    bulk_flops = 2 * 3 * 4 * ROWS * 2 * ROWS * nv * lanes

    def advance(z, lo, hi, extra, first, size):
        def kernel(*refs):
            z_ref, lo_ref, hi_ref, m_ref, p_ref, coef_ref, lhs_ref, masks_ref = refs[:8]
            out_ref = refs[-1]
            metric_value = m_ref[...]

            def body(n, carry):
                x = [whole(lo_ref, z_ref, hi_ref, n, n, v) for v in range(nv)]
                res = bulk(x, coef_ref, lhs_ref, masks_ref, metric_value)
                if extra is not None:
                    res = [res[v] + refs[8][n, v] for v in range(nv)]
                for v in range(nv):
                    weights = [p_ref[first + n, v, pl.ds(w, 1), :] for w in range(nv)]
                    out_ref[n, v] = x[v] - mixed(weights, res)
                return carry

            lax.fori_loop(0, size, body, 0)

        ins = [z, lo, hi, metric, precond, coef, lhs, masks]
        ins = ins + ([] if extra is None else [extra])
        return call(
            kernel,
            [shape(size, nv, ROWS, lanes)],
            ins,
            "vvvvvsvv" + ("" if extra is None else "v"),
            flops=bulk_flops * size,
            name="advance",
        )[0]

    def face_terms(n, lo_ref, hi_ref, below_ref, above_ref, coef_ref, mf_ref):
        position = lax.rem(lax.axis_index("elem") + PR // 2, PR)
        low_w, high_w = [], []
        for v in range(nv):
            sign = -1.0 if v == 2 else 1.0
            low_w.append(jnp.where(position == 0, sign * lo_ref[n, v], below_ref[n, v]))
            high_w.append(jnp.where(position == PR - 1, sign * hi_ref[n, v], above_ref[n, v]))
        lows, highs = [], []
        for v in range(nv):
            weights = [jac(coef_ref, 1, v, w) for w in range(nv)]
            lows.append((mixed(weights, low_w) + damp(coef_ref, 1) * low_w[v]) * (-5.0 * mf_ref[0]))
            highs.append((mixed(weights, high_w) - damp(coef_ref, 1) * high_w[v]) * (5.0 * mf_ref[1]))
        return lows, highs

    def swap_faces(lo, hi):
        return along_elem(hi, 1), along_elem(lo, -1)

    def close_faces(z, lo, hi, below, above, first, size):
        def kernel(z_ref, lo_ref, hi_ref, below_ref, above_ref, coef_ref, mf_ref, p_ref, nlo_ref, nhi_ref):
            def body(n, carry):
                lows, highs = face_terms(n, lo_ref, hi_ref, below_ref, above_ref, coef_ref, mf_ref)
                for v in range(nv):
                    weights = [p_ref[first + n, v, pl.ds(w, 1), :] for w in range(nv)]
                    nlo_ref[n, v] = z_ref[n, v, 0:FACE, :] - mixed(weights, lows)
                    nhi_ref[n, v] = z_ref[n, v, HIGH:ROWS, :] - mixed(weights, highs)
                return carry

            lax.fori_loop(0, size, body, 0)

        return call(
            kernel,
            [shape(size, nv, FACE, lanes)] * 2,
            [z, lo, hi, below, above, coef, metric_face, precond],
            "vvvvvsvv",
            name="faces",
        )

    def circ_extra(z, lo, hi):
        x = jnp.concatenate([lo, z[:, :, FACE:HIGH], hi], axis=2)
        picks = np.zeros((2, 25, ROWS), dtype=np.float32)
        picks[0, np.arange(25), node_row[0:25]] = 1.0
        picks[1, np.arange(25), node_row[100:125]] = 1.0
        exact = lax.Precision.HIGHEST

        def picked(which):
            return jnp.einsum("pq,nvqa->nvpa", picks[which], x, precision=exact)

        def mix(values):
            return jnp.einsum("vw,nwqa->nvqa", flux_jacobians[0], values, precision=exact)

        def placed(which, values):
            return jnp.einsum("pq,nvpa->nvqa", picks[which], values, precision=exact)

        above, below = along_elem(picked(0), -PR), along_elem(picked(1), PR)
        high_term = 5.0 * (mix(above) - damping[0] * above)
        low_term = -5.0 * (mix(below) + damping[0] * below)
        return metric * (placed(1, high_term) + placed(0, low_term))

    below0, above0 = swap_faces(lo0, hi0)
    t0 = advance(x0, lo0, hi0, None if own_circ else circ_extra(x0, lo0, hi0), 0, inst)
    tlo, thi = close_faces(t0, lo0, hi0, below0, above0, 0, inst)

    half_pair = n_tm % 2 == 0

    def coupling_kernel(*refs):
        x_refs, outs = refs[:n_tm], refs[n_tm:]

        def weight(offset, sign):
            return 0.5 * (
                coupling_value(offset, count) + sign * coupling_value(offset + count // 2, count)
            )

        def emit(e, j, rows, v, value):
            outs[e * groups + j // per][j % per, v, rows, :] = value

        def body(step, carry):
            v, rows = step // (block // 8), pl.ds(pl.multiple_of((step % (block // 8)) * 8, 8), 8)
            x = [[x_refs[d][i, v, rows, :] for i in range(inst)] for d in range(n_tm)]
            if half_pair:
                half = n_tm // 2
                sums = [x[d][i] + x[d + half][i] for d in range(half) for i in range(inst)]
                diffs = [x[d][i] - x[d + half][i] for d in range(half) for i in range(inst)]
                for e in range(half):
                    for j in range(inst):
                        offsets = [inst * (e + d) + j - i for d in range(half) for i in range(inst)]
                        terms = [(weight(o, 1), s) for o, s in zip(offsets, sums)]
                        terms = [(c, s) for c, s in terms if abs(c) > 1e-12]
                        even = mixed([c for c, _ in terms], [s for _, s in terms])
                        terms = [(weight(o, -1), s) for o, s in zip(offsets, diffs)]
                        terms = [(c, s) for c, s in terms if abs(c) > 1e-12]
                        odd = mixed([c for c, _ in terms], [s for _, s in terms])
                        emit(e, j, rows, v, even + odd)
                        emit(e + half, j, rows, v, even - odd)
            else:
                for e in range(n_tm):
                    for j in range(inst):
                        terms = [
                            (coupling_value(inst * (e + d) + j - i, count), x[d][i])
                            for d in range(n_tm)
                            for i in range(inst)
                        ]
                        emit(e, j, rows, v, mixed([c for c, _ in terms], [s for _, s in terms]))
            return carry

        lax.fori_loop(0, nv * (block // 8), body, 0)

    coupled = call(
        coupling_kernel,
        [shape(per, nv, block, lanes)] * (n_tm * groups),
        arrived,
        "v" * n_tm,
        name="coupling",
    )
    spectral = [
        [coupled[g]] + [along_tm(coupled[e * groups + g], e) for e in range(1, n_tm)]
        for g in range(groups)
    ]

    def first_pass(parts, first):
        def kernel(*refs):
            part_refs = refs[:n_tm]
            t_ref, tlo_ref, thi_ref, p_ref, col_ref, order_ref = refs[n_tm : n_tm + 6]
            x_ref, lo_ref, hi_ref, s_ref, buf = refs[n_tm + 6 :]
            me = lax.axis_index("tm")
            for d in range(n_tm):
                start = pl.multiple_of(lax.rem(me - d + n_tm, n_tm) * block, block)
                for n in range(per):
                    for v in range(nv):
                        buf[n, v, pl.ds(start, block), :] = part_refs[d][n, v]
            lane = lax.broadcasted_iota(jnp.int32, (ROWS, lanes), 1)
            for n in range(per):
                natural = jnp.concatenate([buf[n, v] for v in range(nv)], axis=1)
                moved = reorder(order_ref[...], natural, 2)
                terms = []
                for v in range(nv):
                    c = (first + n) * nv + v
                    column = jnp.broadcast_to(col_ref[:, c : c + 1], (ROWS, lanes))
                    term = moved[:, v * lanes : (v + 1) * lanes] + jnp.where(lane == 0, column, 0.0)
                    s_ref[n, v] = term
                    terms.append(term)
                for v in range(nv):
                    weights = [p_ref[first + n, v, pl.ds(w, 1), :] for w in range(nv)]
                    x = whole(tlo_ref, t_ref, thi_ref, first + n, first + n, v) - mixed(weights, terms)
                    x_ref[n, v] = x
                    lo_ref[n, v] = x[0:FACE]
                    hi_ref[n, v] = x[HIGH:ROWS]

        return call(
            kernel,
            [
                shape(per, nv, ROWS, lanes),
                shape(per, nv, FACE, lanes),
                shape(per, nv, FACE, lanes),
                shape(per, nv, ROWS, lanes),
            ],
            list(parts) + [t0, tlo, thi, precond, inlet_cols, order_b],
            "v" * (n_tm + 6),
            scratch=[pltpu.VMEM((per, nv, ROWS, lanes), F32)],
            name="first_pass",
        )

    def write_out(moved_ref, out_ref, sem, first, work):
        copies = []
        for n in range(per):
            work(n)
            for v in range(nv):
                copy = pltpu.make_async_copy(
                    moved_ref.at[n, v, pl.ds(0, nodes), :], out_ref.at[first + n, v, :, 0, :], sem.at[n, v]
                )
                copy.start()
                copies.append(copy)
        for copy in copies:
            copy.wait()

    def last_bulk(z, lo, hi, extra, first, out):
        def kernel(*refs):
            z_ref, lo_ref, hi_ref, m_ref, coef_ref, lhs_ref, masks_ref, extra_ref, back_ref = refs[:9]
            r_ref, out_ref, buf, sem = refs[-4:]
            metric_value = m_ref[...]

            def work(n):
                x = [whole(lo_ref, z_ref, hi_ref, n, n, v) for v in range(nv)]
                moved = reorder(back_ref[...], jnp.concatenate(x, axis=1), 3)
                for v in range(nv):
                    buf[n, v] = moved[:, v * lanes : (v + 1) * lanes]

            def residual(n, carry):
                x = [whole(lo_ref, z_ref, hi_ref, n, n, v) for v in range(nv)]
                res = bulk(x, coef_ref, lhs_ref, masks_ref, metric_value)
                for v in range(nv):
                    r_ref[n, v] = res[v] + extra_ref[n, v]
                return carry

            lax.fori_loop(0, per, residual, 0)
            write_out(buf, out_ref, sem, first, work)

        ins = [z, lo, hi, metric, coef, lhs, masks, extra, back_b] + ([] if out is None else [out])
        return call(
            kernel,
            [shape(per, nv, ROWS, lanes), shape(inst, nv, nodes, 1, lanes)],
            ins,
            "vvvvsvvvv" + ("" if out is None else "a"),
            out_spaces="va",
            scratch=[pltpu.VMEM((per, nv, ROWS, lanes), F32), pltpu.SemaphoreType.DMA((per, nv))],
            flops=bulk_flops * per,
            alias=None if out is None else {9: 1},
            name="last_bulk",
        )

    def last_faces(r, lo, hi, below, above, first, out):
        def kernel(*refs):
            r_ref, lo_ref, hi_ref, below_ref, above_ref, coef_ref, mf_ref, back_ref = refs[:8]
            out_ref, buf, sem = refs[-3:]

            def work(n):
                lows, highs = face_terms(n, lo_ref, hi_ref, below_ref, above_ref, coef_ref, mf_ref)
                full = [
                    jnp.concatenate(
                        [
                            r_ref[n, v, 0:FACE, :] + lows[v],
                            r_ref[n, v, FACE:HIGH, :],
                            r_ref[n, v, HIGH:ROWS, :] + highs[v],
                        ],
                        axis=0,
                    )
                    for v in range(nv)
                ]
                moved = reorder(back_ref[...], jnp.concatenate(full, axis=1), 2)
                for v in range(nv):
                    buf[n, v] = moved[:, v * lanes : (v + 1) * lanes]

            write_out(buf, out_ref, sem, first, work)

        ins = [r, lo, hi, below, above, coef, metric_face, back_b] + ([] if out is None else [out])
        return call(
            kernel,
            [shape(inst, nv, nodes, 1, lanes)],
            ins,
            "vvvvvsvv" + ("" if out is None else "a"),
            out_spaces="a",
            scratch=[pltpu.VMEM((per, nv, ROWS, lanes), F32), pltpu.SemaphoreType.DMA((per, nv))],
            alias=None if out is None else {8: 0},
            name="last_faces",
        )[0]

    new_state, final_residual = None, None
    for g in range(groups):
        first = g * per
        z, lo, hi, spec = first_pass(spectral[g], first)
        for sweep in range(PASSES):
            below, above = swap_faces(lo, hi)
            extra = spec if own_circ else spec + circ_extra(z, lo, hi)
            if sweep < PASSES - 1:
                z = advance(z, lo, hi, extra, first, per)
                lo, hi = close_faces(z, lo, hi, below, above, first, per)
            else:
                res, new_state = last_bulk(z, lo, hi, extra, first, new_state)
                final_residual = last_faces(res, lo, hi, below, above, first, final_residual)
    return (new_state.reshape(state.shape), final_residual.reshape(state.shape))


def solution(mesh):
    in_specs = (
        P("tm", None, "elem", None, None),
        P("elem", None, None),
        P(),
        P("tm", None, None, "elem", None),
        P("tm", None, "elem", None),
    )
    out_specs = (P("tm", None, "elem", None, None), P("tm", None, "elem", None, None))
    return jax.shard_map(
        per_device, mesh=mesh, in_specs=in_specs, out_specs=out_specs, check_vma=False
    )
```

time: 772 us -> 111 us (0.14); the launches traced: 757 us -> 110 us
  other arithmetic: 635 us -> 19 us
  local copies, waits for them, and re-layouts: 63 us -> 4.28 us
  Pallas kernels: 0 us -> 41.7 us
  between operations: 17.5 us -> 1.17 us
  waiting for transfers between devices: 0.08 us -> 12.5 us
    unnamed x157 -> x4, other arithmetic: 322 us -> 15.1 us
    add x63 -> x0, other arithmetic: 203 us -> none  [the longest x58 196 us: mix_variables(): total = total + matrix[row_index, column] * parts[column]]
    another operation x55 -> x1, other arithmetic: 94.6 us -> 3.78 us  [per_device(): jnp.stack([-5.0 * (sum((flux_jacobians[2, v, w] * inlet[:, w] for w in ra...]
    pallas_call x0 -> x19, Pallas kernels: none -> 41.7 us  [call(): pl.pallas_call(kernel, out_shape=outs, in_specs=[pl.BlockSpec(memory_spac...]
    unnamed x168 -> x25, local copies, waits for them, and re-layouts: 32.2 us -> 2.19 us
    ppermute x16 -> x23, waiting for transfers between devices: 0.04 us -> 12.5 us  [the longest x9 11.1 us: along_tm(): return lax.ppermute(x, 'tm', [(i, (i + d) % n_tm) for i in range(n_tm)])]
    sub x9 -> x0, other arithmetic: 10.6 us -> none  [the longest x4 7.43 us: lift_faces(): jump_low = beyond_low - lows]
    slice x22 -> x3, local copies, waits for them, and re-layouts: 10.6 us -> 1.98 us  [the longest x2 1.38 us: per_device(): flux_jacobians[2, v, w] * inlet[:, w]]
  transfers between devices with their start and end apart: 17 -> 23, of which waited for: 0 -> 4; matrix products, arithmetic and copies ran while one was open for 30% -> 19% of each run, Pallas kernels for 0% -> 34%
where the time goes in v1:
time: 111 us; the launch traced here: 110 us
  Pallas kernels  41.7 us (38%)
  starting transfers between devices  31.2 us (28%)
  other arithmetic  19 us (17%)
  waiting for transfers between devices  12.5 us (11%)
  local copies, waits for them, and re-layouts  4.28 us (4%)
  between operations  1.17 us (1%)
    pallas_call x19, Pallas kernels, call(): pl.pallas_call(kernel, out_shape=outs, in_specs=[pl.BlockSpec(memory_spac...  41.7 us
    ppermute x14, starting transfers between devices, along_elem(): lax.ppermute(x, 'elem', [(i, (i + d) % n_elem) for i in range(n_elem)])  18.8 us
    unnamed x4, other arithmetic  15.1 us
    ppermute x9, starting transfers between devices, along_tm(): return lax.ppermute(x, 'tm', [(i, (i + d) % n_tm) for i in range(n_tm)])  12.4 us
    ppermute x9, waiting for transfers between devices, along_tm(): return lax.ppermute(x, 'tm', [(i, (i + d) % n_tm) for i in range(n_tm)])  11.1 us
    another operation x1, other arithmetic, per_device(): jnp.stack([-5.0 * (sum((flux_jacobians[2, v, w] * inlet[:, w] for w in ra...  3.78 us
  transfers between devices with their start and end apart: 23, of which 4 were waited for; matrix products, arithmetic and copies ran while one was open for 19% of the time, Pallas kernels for 34%

profile of v1, /device:TPU:0, one launch (start us, length us, event | category | flops | bytes accessed | tf_op | source)
XLA Modules:
  0.0 109.9 jit_solution(8209604920840552627)
XLA Ops:
  0.6 1.3 %copy-done = f32[4,5,1,125,128]{4,2,3,1,0:T(1,128)S(1)} copy-done((f32[4,5,1,125,128]{4,2,3,1,0:T(1,128)S(1)}, f32[4,5,1,125,128]{4,2,3,1,0:T(1,128)}, u32[]{:S(2)}) %copy-start) | copy-done | bytes 1280024
  2.0 2.8 %pack.1 = (f32[4,5,32,128]{3,2,1,0:T(8,128)S(1)}, f32[4,5,32,128]{3,2,1,0:T(8,128)}, f32[4,5,32,128]{3,2,1,0:T(8,128)}, f32[4,5,32,128]{3,2,1,0:T(8,128)}, f32[4,5,128,128]{3,2,1,0:T(8,128)S(1)}) custom-call(f32[4,5,125,1,128]{4,3,2,1,0:T(1,128)S(1)} %bitcast.36), custom_call_target="tpu_custom_call" | custom-call | bytes 3901440 | tf_op jit(solution)/shard_map/pack/pallas_call | solution.py:156
  4.8 3.1 %collective-permute-start = (f32[4,5,32,128]{3,2,1,0:T(8,128)}, f32[4,5,32,128]{3,2,1,0:T(8,128)S(1)}, u32[]{:S(2)}, u32[]{:S(2)}) collective-permute-start(f32[4,5,32,128]{3,2,1,0:T(8,128)} %get-tuple-element.45), channel_id=1, source_target_pairs={{0,8},{8,16},{16,24},{24,0},{1,9},{9,17},{17,25},{25,1},{2,10},{10... | collective-permute-start | bytes 983048 | tf_op jit(solution)/shard_map/ppermute | solution.py:251
  7.9 2.6 %collective-permute-start.1 = (f32[4,5,32,128]{3,2,1,0:T(8,128)}, f32[4,5,32,128]{3,2,1,0:T(8,128)S(1)}, u32[]{:S(2)}, u32[]{:S(2)}) collective-permute-start(f32[4,5,32,128]{3,2,1,0:T(8,128)} %get-tuple-element.46), channel_id=1, source_target_pairs={{0,16},{8,24},{16,0},{24,8},{1,17},{9,25},{17,1},{25,9},{2,18},{10... | collective-permute-start | bytes 983048 | tf_op jit(solution)/shard_map/ppermute | solution.py:251
  10.5 1.3 %collective-permute-start.2 = (f32[4,5,32,128]{3,2,1,0:T(8,128)}, f32[4,5,32,128]{3,2,1,0:T(8,128)S(1)}, u32[]{:S(2)}, u32[]{:S(2)}) collective-permute-start(f32[4,5,32,128]{3,2,1,0:T(8,128)} %get-tuple-element.47), channel_id=1, source_target_pairs={{0,24},{8,0},{16,8},{24,16},{1,25},{9,1},{17,9},{25,17},{2,26},{10... | collective-permute-start | bytes 983048 | tf_op jit(solution)/shard_map/ppermute | solution.py:251
  11.9 0.7 fusion
  12.6 0.7 fusion.1
  13.3 0.6 slice.132
  13.9 3.8 %constant_dynamic-update-slice_fusion.4 = f32[4,5,25]{2,0,1:T(4,128)S(1)} fusion(f32[4,5,25]{2,0,1:T(4,128)S(1)} %bitcast.40, f32[]{:T(128)} %bitcast.8, f32[]{:T(128)} %bitcast.7, f32[]{:T(128)} %bitcast.6, f32[]{:T(128)} %bitcast.5, f32[]{:T(128)} %bitcast.4, f32[]{:T(128)} %bitcast.2), kind=kLoop, calls=%fused_computation.5 | loop fusion | flops 1199 | bytes 4072
  17.7 3.8 %constant_dynamic-update-slice_fusion.3 = f32[4,5,25]{2,0,1:T(4,128)S(1)} fusion(f32[4,5,25]{2,0,1:T(4,128)S(1)} %constant_dynamic-update-slice_fusion.4, f32[4,5,25]{2,0,1:T(4,128)S(1)} %bitcast.41, f32[]{:T(128)} %bitcast.13, f32[]{:T(128)} %bitcast.12, f32[]{:T(128)} %bitcast.11, f32[]{:T(128)} %bitcast.10, f32[]{:T(128)} %bitcast.9, f32[]{:T(128)} %bitcast.8), kind=kLoop, calls=%fused_computation.4 | loop fusion | flops 1200 | bytes 12312
  21.5 3.7 %constant_dynamic-update-slice_fusion.2 = f32[4,5,25]{2,0,1:T(4,128)S(1)} fusion(f32[4,5,25]{2,0,1:T(4,128)S(1)} %constant_dynamic-update-slice_fusion.3, f32[4,5,25]{2,0,1:T(4,128)S(1)} %bitcast.42, f32[]{:T(128)} %bitcast.18, f32[]{:T(128)} %bitcast.17, f32[]{:T(128)} %bitcast.16, f32[]{:T(128)} %bitcast.15, f32[]{:T(128)} %bitcast.14, f32[]{:T(128)} %bitcast.8), kind=kLoop, calls=%fused_computation.3 | loop fusion | flops 1200 | bytes 12312
  25.2 3.8 %constant_dynamic-update-slice_fusion.1 = f32[4,5,25]{2,0,1:T(4,128)S(1)} fusion(f32[4,5,25]{2,0,1:T(4,128)S(1)} %constant_dynamic-update-slice_fusion.2, f32[4,5,25]{2,0,1:T(4,128)S(1)} %bitcast.43, f32[]{:T(128)} %bitcast.23, f32[]{:T(128)} %bitcast.22, f32[]{:T(128)} %bitcast.21, f32[]{:T(128)} %bitcast.20, f32[]{:T(128)} %bitcast.19, f32[]{:T(128)} %bitcast.8), kind=kLoop, calls=%fused_computation.2 | loop fusion | flops 1200 | bytes 12312
  29.0 3.8 %constant_dynamic-update-slice_fusion = f32[4,5,25]{2,0,1:T(4,128)S(1)} fusion(f32[4,5,25]{2,0,1:T(4,128)S(1)} %constant_dynamic-update-slice_fusion.1, f32[4,5,25]{2,0,1:T(4,128)S(1)} %bitcast.44, f32[]{:T(128)} %bitcast.28, f32[]{:T(128)} %bitcast.27, f32[]{:T(128)} %bitcast.26, f32[]{:T(128)} %bitcast.25, f32[]{:T(128)} %bitcast.24, f32[]{:T(128)} %bitcast.8), kind=kLoop, calls=%fused_computation.1 | loop fusion | flops 1200 | bytes 12312 | tf_op jit(solution)/shard_map/stack | solution.py:194
  33.0 0.8 copy-done.7
  33.9 1.5 %prep.1 = (f32[4,5,128,128]{3,2,1,0:T(8,128)S(1)}, f32[4,5,32,128]{3,2,1,0:T(8,128)S(1)}, f32[4,5,32,128]{3,2,1,0:T(8,128)S(1)}, f32[128,128]{1,0:T(8,128)S(1)},...) custom-call(f32[4,5,128,128]{3,2,1,0:T(8,128)S(1)} %get-tuple-element.52.padded_ref, ...), custom_call_target="tpu_custom_call" | custom-call | bytes 4979512 | tf_op jit(solution)/shard_map/prep/pallas_call | solution.py:156
  35.4 2.6 %collective-permute-start.7 = (f32[4,5,32,128]{3,2,1,0:T(8,128)S(1)}, f32[4,5,32,128]{3,2,1,0:T(8,128)S(1)}, u32[]{:S(2)}, u32[]{:S(2)}) collective-permute-start(f32[4,5,32,128]{3,2,1,0:T(8,128)S(1)} %get-tuple-element.54.refs_1_.lo_ref), channel_id=1, source_target_pairs={{0,7},{1,0},{2,1},{3,2},{4,3},{5,4},{6,5},{7,6},{8,15},{9,8},{10,9... | collective-permute-start | bytes 983048 | tf_op jit(solution)/shard_map/ppermute | solution.py:254
  38.1 0.9 coupling.1
  39.0 1.5 %collective-permute-start.3 = (f32[2,5,32,128]{3,2,1,0:T(8,128)S(1)}, f32[2,5,32,128]{3,2,1,0:T(8,128)S(1)}, u32[]{:S(2)}, u32[]{:S(2)}) collective-permute-start(f32[2,5,32,128]{3,2,1,0:T(8,128)S(1)} %get-tuple-element.49), channel_id=1, source_target_pairs={{0,8},{8,16},{16,24},{24,0},{1,9},{9,17},{17,25},{25,1},{2,10},{10... | collective-permute-start | bytes 491528 | tf_op jit(solution)/shard_map/ppermute | solution.py:251
  40.5 1.7 %collective-permute-start.4 = (f32[2,5,32,128]{3,2,1,0:T(8,128)S(1)}, f32[2,5,32,128]{3,2,1,0:T(8,128)S(1)}, u32[]{:S(2)}, u32[]{:S(2)}) collective-permute-start(f32[2,5,32,128]{3,2,1,0:T(8,128)S(1)} %get-tuple-element.50), channel_id=1, source_target_pairs={{0,16},{8,24},{16,0},{24,8},{1,17},{9,25},{17,1},{25,9},{2,18},{10... | collective-permute-start | bytes 491528 | tf_op jit(solution)/shard_map/ppermute | solution.py:251
  42.1 0.9 collective-permute-start.5
  43.0 1.4 %collective-permute-done.6.below_ref = f32[4,5,32,128]{3,2,1,0:T(8,128)S(1)} collective-permute-done((f32[4,5,32,128]{3,2,1,0:T(8,128)S(1)}, f32[4,5,32,128]{3,2,1,0:T(8,128)S(1)}, u32[]{:S(2)}, u32[]{:S(2)}) %collective-permute-start.6) | collective-permute-done | bytes 327712 | tf_op jit(solution)/shard_map/ppermute | solution.py:254
  44.4 0.7 collective-permute-start.12
  45.1 0.4 collective-permute-start.13
  45.5 2.5 %collective-permute-done.3.refs_1_ = f32[2,5,32,128]{3,2,1,0:T(8,128)S(1)} collective-permute-done((f32[2,5,32,128]{3,2,1,0:T(8,128)S(1)}, f32[2,5,32,128]{3,2,1,0:T(8,128)S(1)}, u32[]{:S(2)}, u32[]{:S(2)}) %collective-permute-start.3) | collective-permute-done | bytes 163872 | tf_op jit(solution)/shard_map/ppermute | solution.py:251
  48.3 5.8 %advance.5.z_ref.refs_4_ = f32[4,5,128,128]{3,2,1,0:T(8,128)S(1)} custom-call(f32[4,5,128,128]{3,2,1,0:T(8,128)S(1)} %get-tuple-element.53.refs_0_, f32[4,5,32,128]{3,2,1,0:T(8,128)S(1)} %get-tuple-element.54.refs_1_.lo_ref, f32[4,5,32,128]{3,2,1,0:T(8,128)S(1)} %get-tuple-element.55.refs_2_.hi_ref, f32[128,128]{1,0:T(8,128)S(1)} %get-tuple-element.56.refs_3_, ...), custom_call_target="tpu_custom_call" | custom-call | flops 2013265920 | bytes 4114744 | tf_op jit(solution)/shard_map/advance/pallas_call | solution.py:156
  54.1 1.1 %faces.5 = (f32[4,5,32,128]{3,2,1,0:T(8,128)S(1)}, f32[4,5,32,128]{3,2,1,0:T(8,128)S(1)}) custom-call(f32[4,5,128,128]{3,2,1,0:T(8,128)S(1)} %advance.5.z_ref.refs_4_, f32[4,5,32,128]{3,2,1,0:T(8,128)S(1)} %get-tuple-element.54.refs_1_.lo_ref, f32[4,5,32,128]{3,2,1,0:T(8,128)S(1)} %get-tuple-element.55.refs_2_.hi_ref, ...), custom_call_target="tpu_custom_call" | custom-call | bytes 3361080 | tf_op jit(solution)/shard_map/faces/pallas_call | solution.py:156
  55.2 2.8 %collective-permute-done.4.refs_2_ = f32[2,5,32,128]{3,2,1,0:T(8,128)S(1)} collective-permute-done((f32[2,5,32,128]{3,2,1,0:T(8,128)S(1)}, f32[2,5,32,128]{3,2,1,0:T(8,128)S(1)}, u32[]{:S(2)}, u32[]{:S(2)}) %collective-permute-start.4) | collective-permute-done | bytes 163872 | tf_op jit(solution)/shard_map/ppermute | solution.py:251
  58.0 0.6 first_pass.2
  58.7 2.6 %collective-permute-start.9 = (f32[2,5,32,128]{3,2,1,0:T(8,128)S(1)}, f32[2,5,32,128]{3,2,1,0:T(8,128)S(1)}, u32[]{:S(2)}, u32[]{:S(2)}) collective-permute-start(f32[2,5,32,128]{3,2,1,0:T(8,128)S(1)} %get-tuple-element.63.refs_1_.lo_ref), channel_id=1, source_target_pairs={{0,7},{1,0},{2,1},{3,2},{4,3},{5,4},{6,5},{7,6},{8,15},{9,8},{10,9... | collective-permute-start | bytes 491528 | tf_op jit(solution)/shard_map/ppermute | solution.py:254
  61.3 5.7 %collective-permute-done.13.refs_2_ = f32[2,5,32,128]{3,2,1,0:T(8,128)S(1)} collective-permute-done((f32[2,5,32,128]{3,2,1,0:T(8,128)S(1)}, f32[2,5,32,128]{3,2,1,0:T(8,128)S(1)}, u32[]{:S(2)}, u32[]{:S(2)}) %collective-permute-start.13) | collective-permute-done | bytes 163872 | tf_op jit(solution)/shard_map/ppermute | solution.py:251
  67.1 0.6 first_pass.3
  67.7 2.6 %collective-permute-start.16 = (f32[2,5,32,128]{3,2,1,0:T(8,128)S(1)}, f32[2,5,32,128]{3,2,1,0:T(8,128)S(1)}, u32[]{:S(2)}, u32[]{:S(2)}) collective-permute-start(f32[2,5,32,128]{3,2,1,0:T(8,128)S(1)} %get-tuple-element.75.refs_1_.lo_ref), channel_id=1, source_target_pairs={{0,7},{1,0},{2,1},{3,2},{4,3},{5,4},{6,5},{7,6},{8,15},{9,8},{10,9... | collective-permute-start | bytes 491528 | tf_op jit(solution)/shard_map/ppermute | solution.py:254
  70.4 3.2 %advance.6.z_ref.refs_0_ = f32[2,5,128,128]{3,2,1,0:T(8,128)S(1)} custom-call(f32[2,5,128,128]{3,2,1,0:T(8,128)S(1)} %get-tuple-element.62.refs_0_, f32[2,5,32,128]{3,2,1,0:T(8,128)S(1)} %get-tuple-element.63.refs_1_.lo_ref, f32[2,5,32,128]{3,2,1,0:T(8,128)S(1)} %get-tuple-element.64.refs_2_.hi_ref, f32[128,128]{1,0:T(8,128)S(1)} %get-tuple-element.56.refs_3_, ...), custom_call_target="tpu_custom_call" | custom-call | flops 1006632960 | bytes 3131704 | tf_op jit(solution)/shard_map/advance/pallas_call | solution.py:156
  73.6 3.2 %advance.8.z_ref.refs_0_ = f32[2,5,128,128]{3,2,1,0:T(8,128)S(1)} custom-call(f32[2,5,128,128]{3,2,1,0:T(8,128)S(1)} %get-tuple-element.74.refs_0_, f32[2,5,32,128]{3,2,1,0:T(8,128)S(1)} %get-tuple-element.75.refs_1_.lo_ref, f32[2,5,32,128]{3,2,1,0:T(8,128)S(1)} %get-tuple-element.76.refs_2_.hi_ref, f32[128,128]{1,0:T(8,128)S(1)} %get-tuple-element.56.refs_3_, ...), custom_call_target="tpu_custom_call" | custom-call | flops 1006632960 | bytes 3131704 | tf_op jit(solution)/shard_map/advance/pallas_call | solution.py:156
  76.8 0.8 faces.6
  77.7 2.6 %collective-permute-start.11 = (f32[2,5,32,128]{3,2,1,0:T(8,128)S(1)}, f32[2,5,32,128]{3,2,1,0:T(8,128)S(1)}, u32[]{:S(2)}, u32[]{:S(2)}) collective-permute-start(f32[2,5,32,128]{3,2,1,0:T(8,128)S(1)} %get-tuple-element.66.refs_1_.lo_ref), channel_id=1, source_target_pairs={{0,7},{1,0},{2,1},{3,2},{4,3},{5,4},{6,5},{7,6},{8,15},{9,8},{10,9... | collective-permute-start | bytes 491528 | tf_op jit(solution)/shard_map/ppermute | solution.py:254
  80.4 0.8 faces.8
  81.3 2.6 %collective-permute-start.18 = (f32[2,5,32,128]{3,2,1,0:T(8,128)S(1)}, f32[2,5,32,128]{3,2,1,0:T(8,128)S(1)}, u32[]{:S(2)}, u32[]{:S(2)}) collective-permute-start(f32[2,5,32,128]{3,2,1,0:T(8,128)S(1)} %get-tuple-element.78.refs_1_.lo_ref), channel_id=1, source_target_pairs={{0,7},{1,0},{2,1},{3,2},{4,3},{5,4},{6,5},{7,6},{8,15},{9,8},{10,9... | collective-permute-start | bytes 491528 | tf_op jit(solution)/shard_map/ppermute | solution.py:254
  83.9 3.2 %advance.7.z_ref.refs_0_ = f32[2,5,128,128]{3,2,1,0:T(8,128)S(1)} custom-call(f32[2,5,128,128]{3,2,1,0:T(8,128)S(1)} %advance.6.z_ref.refs_0_, f32[2,5,32,128]{3,2,1,0:T(8,128)S(1)} %get-tuple-element.66.refs_1_.lo_ref, f32[2,5,32,128]{3,2,1,0:T(8,128)S(1)} %get-tuple-element.67.refs_2_.hi_ref, f32[128,128]{1,0:T(8,128)S(1)} %get-tuple-element.56.refs_3_, ...), custom_call_target="tpu_custom_call" | custom-call | flops 1006632960 | bytes 3131704 | tf_op jit(solution)/shard_map/advance/pallas_call | solution.py:156
  87.1 3.2 %advance.9.z_ref.refs_0_ = f32[2,5,128,128]{3,2,1,0:T(8,128)S(1)} custom-call(f32[2,5,128,128]{3,2,1,0:T(8,128)S(1)} %advance.8.z_ref.refs_0_, f32[2,5,32,128]{3,2,1,0:T(8,128)S(1)} %get-tuple-element.78.refs_1_.lo_ref, f32[2,5,32,128]{3,2,1,0:T(8,128)S(1)} %get-tuple-element.79.refs_2_.hi_ref, f32[128,128]{1,0:T(8,128)S(1)} %get-tuple-element.56.refs_3_, ...), custom_call_target="tpu_custom_call" | custom-call | flops 1006632960 | bytes 3131704 | tf_op jit(solution)/shard_map/advance/pallas_call | solution.py:156
  90.4 0.8 faces.7
  91.3 2.6 %collective-permute-start.20 = (f32[2,5,32,128]{3,2,1,0:T(8,128)S(1)}, f32[2,5,32,128]{3,2,1,0:T(8,128)S(1)}, u32[]{:S(2)}, u32[]{:S(2)}) collective-permute-start(f32[2,5,32,128]{3,2,1,0:T(8,128)S(1)} %get-tuple-element.68.refs_1_), channel_id=1, source_target_pairs={{0,7},{1,0},{2,1},{3,2},{4,3},{5,4},{6,5},{7,6},{8,15},{9,8},{10,9... | collective-permute-start | bytes 491528 | tf_op jit(solution)/shard_map/ppermute | solution.py:254
  93.9 0.8 faces.9
  94.8 2.6 %collective-permute-start.22 = (f32[2,5,32,128]{3,2,1,0:T(8,128)S(1)}, f32[2,5,32,128]{3,2,1,0:T(8,128)S(1)}, u32[]{:S(2)}, u32[]{:S(2)}) collective-permute-start(f32[2,5,32,128]{3,2,1,0:T(8,128)S(1)} %get-tuple-element.80.refs_1_), channel_id=1, source_target_pairs={{0,7},{1,0},{2,1},{3,2},{4,3},{5,4},{6,5},{7,6},{8,15},{9,8},{10,9... | collective-permute-start | bytes 491528 | tf_op jit(solution)/shard_map/ppermute | solution.py:254
  97.5 4.3 %last_bulk.2 = (f32[2,5,128,128]{3,2,1,0:T(8,128)S(1)}, f32[4,5,125,1,128]{4,3,2,1,0:T(1,128)}) custom-call(f32[2,5,128,128]{3,2,1,0:T(8,128)S(1)} %advance.9.z_ref.refs_0_, f32[2,5,32,128]{3,2,1,0:T(8,128)S(1)} %get-tuple-element.80.refs_1_, f32[2,5,32,128]{3,2,1,0:T(8,128)S(1)} %get-tuple-element.81.refs_2_, f32[128,128]{1,0:T(8,128)S(1)} %get-tuple-element.56.refs_3_, ...), custom_call_target="tpu_custom_call" | custom-call | flops 1006632960 | bytes 4393272 | tf_op jit(solution)/shard_map/last_bulk/pallas_call | solution.py:156
  101.8 4.3 %last_bulk.3 = (f32[2,5,128,128]{3,2,1,0:T(8,128)S(1)}, f32[4,5,125,1,128]{4,3,2,1,0:T(1,128)}) custom-call(f32[2,5,128,128]{3,2,1,0:T(8,128)S(1)} %advance.7.z_ref.refs_0_, f32[2,5,32,128]{3,2,1,0:T(8,128)S(1)} %get-tuple-element.68.refs_1_, f32[2,5,32,128]{3,2,1,0:T(8,128)S(1)} %get-tuple-element.69.refs_2_, ...), custom_call_target="tpu_custom_call", output_to_operand_aliasing={{1}: (9, {})} | custom-call | flops 1006632960 | bytes 5673272 | tf_op jit(solution)/shard_map/last_bulk/pallas_call | solution.py:156
  106.0 1.8 %last_faces.2.refs_8_ = f32[4,5,125,1,128]{4,3,2,1,0:T(1,128)} custom-call(f32[2,5,128,128]{3,2,1,0:T(8,128)S(1)} %get-tuple-element.85.refs_0_, f32[2,5,32,128]{3,2,1,0:T(8,128)S(1)} %get-tuple-element.80.refs_1_, f32[2,5,32,128]{3,2,1,0:T(8,128)S(1)} %get-tuple-element.81.refs_2_, f32[2,5,32,128]{3,2,1,0:T(8,128)S(1)} %collective-permute-done.21.refs_3_, ...), custom_call_target="tpu_custom_call" | custom-call | bytes 2656568 | tf_op jit(solution)/shard_map/last_faces/pallas_call | solution.py:156
  107.9 1.8 %last_faces.3 = f32[4,5,125,1,128]{4,3,2,1,0:T(1,128)} custom-call(f32[2,5,128,128]{3,2,1,0:T(8,128)S(1)} %get-tuple-element.84.refs_0_, f32[2,5,32,128]{3,2,1,0:T(8,128)S(1)} %get-tuple-element.68.refs_1_, f32[2,5,32,128]{3,2,1,0:T(8,128)S(1)} %get-tuple-element.69.refs_2_, ...), custom_call_target="tpu_custom_call", output_to_operand_aliasing={{}: (8, {})} | custom-call | bytes 3936568 | tf_op jit(solution)/shard_map/last_faces/pallas_call | solution.py:156
  (58 shorter events, 1.0 us)
Async XLA Ops:
  0.6 1.3 %copy-start = (f32[4,5,1,125,128]{4,2,3,1,0:T(1,128)S(1)}, f32[4,5,1,125,128]{4,2,3,1,0:T(1,128)}, u32[]{:S(2)}) copy-start(f32[4,5,1,125,128]{4,2,3,1,0:T(1,128)} %param.11) | copy-start | bytes 3840004
  1.9 9.9 %copy-start.8 = (f32[3,5,5]{2,0,1:T(4,128)S(1)}, f32[3,5,5]{2,0,1:T(4,128)}, u32[]{:S(2)}) copy-start(f32[3,5,5]{2,0,1:T(4,128)} %param.13) | copy-start | bytes 904
  1.9 11.4 %copy-start.10 = (f32[4,5,1,25]{3,2,1,0:T(1,128)S(1)}, f32[4,5,1,25]{3,2,1,0:T(1,128)}, u32[]{:S(2)}) copy-start(f32[4,5,1,25]{3,2,1,0:T(1,128)} %param.15) | copy-start | bytes 6004
  1.9 31.1 %copy-start.1 = (bf16[2,384,256]{2,1,0:T(8,128)(2,1)S(1)}, bf16[2,384,256]{2,1,0:T(8,128)(2,1)}, u32[]{:S(2)}) copy-start(bf16[2,384,256]{2,1,0:T(8,128)(2,1)} %constant.21.clone.flux_ref) | copy-start | bytes 1179652
  1.9 31.1 %copy-start.2 = (f32[3,128,256]{2,1,0:T(8,128)S(1)}, f32[3,128,256]{2,1,0:T(8,128)}, u32[]{:S(2)}) copy-start(f32[3,128,256]{2,1,0:T(8,128)} %constant.22.clone.damp_ref) | copy-start | bytes 1179652
  1.9 31.1 %copy-start.4 = (bf16[128,128]{1,0:T(8,128)(2,1)S(1)}, bf16[128,128]{1,0:T(8,128)(2,1)}, u32[]{:S(2)}) copy-start(bf16[128,128]{1,0:T(8,128)(2,1)} %constant.20.clone.order_ref.refs_9_) | copy-start | bytes 98308
  2.0 31.0 %copy-start.6 = (f32[128,128]{1,0:T(8,128)S(1)}, f32[128,128]{1,0:T(8,128)}, u32[]{:S(2)}) copy-start(f32[128,128]{1,0:T(8,128)} %constant.23.clone.inlet_table_ref) | copy-start | bytes 196612
  4.8 33.2 %collective-permute-start = (f32[4,5,32,128]{3,2,1,0:T(8,128)}, f32[4,5,32,128]{3,2,1,0:T(8,128)S(1)}, u32[]{:S(2)}, u32[]{:S(2)}) collective-permute-start(f32[4,5,32,128]{3,2,1,0:T(8,128)} %get-tuple-element.45), channel_id=1, source_target_pairs={{0,8},{8,16},{16,24},{24,0},{1,9},{9,17},{17,25},{25,1},{2,10},{10... | collective-permute-start | bytes 983048 | tf_op jit(solution)/shard_map/ppermute | solution.py:251
  7.9 30.2 %collective-permute-start.1 = (f32[4,5,32,128]{3,2,1,0:T(8,128)}, f32[4,5,32,128]{3,2,1,0:T(8,128)S(1)}, u32[]{:S(2)}, u32[]{:S(2)}) collective-permute-start(f32[4,5,32,128]{3,2,1,0:T(8,128)} %get-tuple-element.46), channel_id=1, source_target_pairs={{0,16},{8,24},{16,0},{24,8},{1,17},{9,25},{17,1},{25,9},{2,18},{10... | collective-permute-start | bytes 983048 | tf_op jit(solution)/shard_map/ppermute | solution.py:251
  10.5 27.6 %collective-permute-start.2 = (f32[4,5,32,128]{3,2,1,0:T(8,128)}, f32[4,5,32,128]{3,2,1,0:T(8,128)S(1)}, u32[]{:S(2)}, u32[]{:S(2)}) collective-permute-start(f32[4,5,32,128]{3,2,1,0:T(8,128)} %get-tuple-element.47), channel_id=1, source_target_pairs={{0,24},{8,0},{16,8},{24,16},{1,25},{9,1},{17,9},{25,17},{2,26},{10... | collective-permute-start | bytes 983048 | tf_op jit(solution)/shard_map/ppermute | solution.py:251
  33.0 0.8 copy-start.7
  33.8 6.6 %copy-start.9 = (f32[4,5,5,1,128]{4,3,2,1,0:T(1,128)S(1)}, f32[4,5,5,1,128]{4,3,2,1,0:T(1,128)}, u32[]{:S(2)}) copy-start(f32[4,5,5,1,128]{4,3,2,1,0:T(1,128)} %param.14) | copy-start | bytes 153604
  35.3 13.0 %copy-start.5 = (f32[3,128,128]{2,1,0:T(8,128)S(1)}, f32[3,128,128]{2,1,0:T(8,128)}, u32[]{:S(2)}) copy-start(f32[3,128,128]{2,1,0:T(8,128)} %constant.24.clone.refs_7_.refs_6_) | copy-start | bytes 589828
  35.4 9.1 %collective-permute-start.6 = (f32[4,5,32,128]{3,2,1,0:T(8,128)S(1)}, f32[4,5,32,128]{3,2,1,0:T(8,128)S(1)}, u32[]{:S(2)}, u32[]{:S(2)}) collective-permute-start(f32[4,5,32,128]{3,2,1,0:T(8,128)S(1)} %get-tuple-element.55.refs_2_.hi_ref), channel_id=1, source_target_pairs={{0,1},{1,2},{2,3},{3,4},{4,5},{5,6},{6,7},{7,0},{8,9},{9,10},{10,1... | collective-permute-start | bytes 983048 | tf_op jit(solution)/shard_map/ppermute | solution.py:254
  35.4 9.7 %collective-permute-start.7 = (f32[4,5,32,128]{3,2,1,0:T(8,128)S(1)}, f32[4,5,32,128]{3,2,1,0:T(8,128)S(1)}, u32[]{:S(2)}, u32[]{:S(2)}) collective-permute-start(f32[4,5,32,128]{3,2,1,0:T(8,128)S(1)} %get-tuple-element.54.refs_1_.lo_ref), channel_id=1, source_target_pairs={{0,7},{1,0},{2,1},{3,2},{4,3},{5,4},{6,5},{7,6},{8,15},{9,8},{10,9... | collective-permute-start | bytes 983048 | tf_op jit(solution)/shard_map/ppermute | solution.py:254
  39.0 9.1 %collective-permute-start.3 = (f32[2,5,32,128]{3,2,1,0:T(8,128)S(1)}, f32[2,5,32,128]{3,2,1,0:T(8,128)S(1)}, u32[]{:S(2)}, u32[]{:S(2)}) collective-permute-start(f32[2,5,32,128]{3,2,1,0:T(8,128)S(1)} %get-tuple-element.49), channel_id=1, source_target_pairs={{0,8},{8,16},{16,24},{24,0},{1,9},{9,17},{17,25},{25,1},{2,10},{10... | collective-permute-start | bytes 491528 | tf_op jit(solution)/shard_map/ppermute | solution.py:251
  40.5 17.5 %collective-permute-start.4 = (f32[2,5,32,128]{3,2,1,0:T(8,128)S(1)}, f32[2,5,32,128]{3,2,1,0:T(8,128)S(1)}, u32[]{:S(2)}, u32[]{:S(2)}) collective-permute-start(f32[2,5,32,128]{3,2,1,0:T(8,128)S(1)} %get-tuple-element.50), channel_id=1, source_target_pairs={{0,16},{8,24},{16,0},{24,8},{1,17},{9,25},{17,1},{25,9},{2,18},{10... | collective-permute-start | bytes 491528 | tf_op jit(solution)/shard_map/ppermute | solution.py:251
  42.1 15.9 %collective-permute-start.5 = (f32[2,5,32,128]{3,2,1,0:T(8,128)S(1)}, f32[2,5,32,128]{3,2,1,0:T(8,128)S(1)}, u32[]{:S(2)}, u32[]{:S(2)}) collective-permute-start(f32[2,5,32,128]{3,2,1,0:T(8,128)S(1)} %get-tuple-element.51), channel_id=1, source_target_pairs={{0,24},{8,0},{16,8},{24,16},{1,25},{9,1},{17,9},{25,17},{2,26},{10... | collective-permute-start | bytes 491528 | tf_op jit(solution)/shard_map/ppermute | solution.py:251
  44.4 16.9 %collective-permute-start.12 = (f32[2,5,32,128]{3,2,1,0:T(8,128)S(1)}, f32[2,5,32,128]{3,2,1,0:T(8,128)S(1)}, u32[]{:S(2)}, u32[]{:S(2)}) collective-permute-start(f32[2,5,32,128]{3,2,1,0:T(8,128)S(1)} %get-tuple-element.71), channel_id=1, source_target_pairs={{0,8},{8,16},{16,24},{24,0},{1,9},{9,17},{17,25},{25,1},{2,10},{10... | collective-permute-start | bytes 491528 | tf_op jit(solution)/shard_map/ppermute | solution.py:251
  45.1 22.0 %collective-permute-start.13 = (f32[2,5,32,128]{3,2,1,0:T(8,128)S(1)}, f32[2,5,32,128]{3,2,1,0:T(8,128)S(1)}, u32[]{:S(2)}, u32[]{:S(2)}) collective-permute-start(f32[2,5,32,128]{3,2,1,0:T(8,128)S(1)} %get-tuple-element.72), channel_id=1, source_target_pairs={{0,16},{8,24},{16,0},{24,8},{1,17},{9,25},{17,1},{25,9},{2,18},{10... | collective-permute-start | bytes 491528 | tf_op jit(solution)/shard_map/ppermute | solution.py:251
  48.1 19.0 %collective-permute-start.14 = (f32[2,5,32,128]{3,2,1,0:T(8,128)S(1)}, f32[2,5,32,128]{3,2,1,0:T(8,128)S(1)}, u32[]{:S(2)}, u32[]{:S(2)}) collective-permute-start(f32[2,5,32,128]{3,2,1,0:T(8,128)S(1)} %get-tuple-element.73), channel_id=1, source_target_pairs={{0,24},{8,0},{16,8},{24,16},{1,25},{9,1},{17,9},{25,17},{2,26},{10... | collective-permute-start | bytes 491528 | tf_op jit(solution)/shard_map/ppermute | solution.py:251
  58.6 18.1 %collective-permute-start.8 = (f32[2,5,32,128]{3,2,1,0:T(8,128)S(1)}, f32[2,5,32,128]{3,2,1,0:T(8,128)S(1)}, u32[]{:S(2)}, u32[]{:S(2)}) collective-permute-start(f32[2,5,32,128]{3,2,1,0:T(8,128)S(1)} %get-tuple-element.64.refs_2_.hi_ref), channel_id=1, source_target_pairs={{0,1},{1,2},{2,3},{3,4},{4,5},{5,6},{6,7},{7,0},{8,9},{9,10},{10,1... | collective-permute-start | bytes 491528 | tf_op jit(solution)/shard_map/ppermute | solution.py:254
  58.7 18.1 %collective-permute-start.9 = (f32[2,5,32,128]{3,2,1,0:T(8,128)S(1)}, f32[2,5,32,128]{3,2,1,0:T(8,128)S(1)}, u32[]{:S(2)}, u32[]{:S(2)}) collective-permute-start(f32[2,5,32,128]{3,2,1,0:T(8,128)S(1)} %get-tuple-element.63.refs_1_.lo_ref), channel_id=1, source_target_pairs={{0,7},{1,0},{2,1},{3,2},{4,3},{5,4},{6,5},{7,6},{8,15},{9,8},{10,9... | collective-permute-start | bytes 491528 | tf_op jit(solution)/shard_map/ppermute | solution.py:254
  67.7 12.7 %collective-permute-start.15 = (f32[2,5,32,128]{3,2,1,0:T(8,128)S(1)}, f32[2,5,32,128]{3,2,1,0:T(8,128)S(1)}, u32[]{:S(2)}, u32[]{:S(2)}) collective-permute-start(f32[2,5,32,128]{3,2,1,0:T(8,128)S(1)} %get-tuple-element.76.refs_2_.hi_ref), channel_id=1, source_target_pairs={{0,1},{1,2},{2,3},{3,4},{4,5},{5,6},{6,7},{7,0},{8,9},{9,10},{10,1... | collective-permute-start | bytes 491528 | tf_op jit(solution)/shard_map/ppermute | solution.py:254
  67.7 12.6 %collective-permute-start.16 = (f32[2,5,32,128]{3,2,1,0:T(8,128)S(1)}, f32[2,5,32,128]{3,2,1,0:T(8,128)S(1)}, u32[]{:S(2)}, u32[]{:S(2)}) collective-permute-start(f32[2,5,32,128]{3,2,1,0:T(8,128)S(1)} %get-tuple-element.75.refs_1_.lo_ref), channel_id=1, source_target_pairs={{0,7},{1,0},{2,1},{3,2},{4,3},{5,4},{6,5},{7,6},{8,15},{9,8},{10,9... | collective-permute-start | bytes 491528 | tf_op jit(solution)/shard_map/ppermute | solution.py:254
  77.7 12.7 %collective-permute-start.10 = (f32[2,5,32,128]{3,2,1,0:T(8,128)S(1)}, f32[2,5,32,128]{3,2,1,0:T(8,128)S(1)}, u32[]{:S(2)}, u32[]{:S(2)}) collective-permute-start(f32[2,5,32,128]{3,2,1,0:T(8,128)S(1)} %get-tuple-element.67.refs_2_.hi_ref), channel_id=1, source_target_pairs={{0,1},{1,2},{2,3},{3,4},{4,5},{5,6},{6,7},{7,0},{8,9},{9,10},{10,1... | collective-permute-start | bytes 491528 | tf_op jit(solution)/shard_map/ppermute | solution.py:254
  77.7 12.6 %collective-permute-start.11 = (f32[2,5,32,128]{3,2,1,0:T(8,128)S(1)}, f32[2,5,32,128]{3,2,1,0:T(8,128)S(1)}, u32[]{:S(2)}, u32[]{:S(2)}) collective-permute-start(f32[2,5,32,128]{3,2,1,0:T(8,128)S(1)} %get-tuple-element.66.refs_1_.lo_ref), channel_id=1, source_target_pairs={{0,7},{1,0},{2,1},{3,2},{4,3},{5,4},{6,5},{7,6},{8,15},{9,8},{10,9... | collective-permute-start | bytes 491528 | tf_op jit(solution)/shard_map/ppermute | solution.py:254
  81.2 12.7 %collective-permute-start.17 = (f32[2,5,32,128]{3,2,1,0:T(8,128)S(1)}, f32[2,5,32,128]{3,2,1,0:T(8,128)S(1)}, u32[]{:S(2)}, u32[]{:S(2)}) collective-permute-start(f32[2,5,32,128]{3,2,1,0:T(8,128)S(1)} %get-tuple-element.79.refs_2_.hi_ref), channel_id=1, source_target_pairs={{0,1},{1,2},{2,3},{3,4},{4,5},{5,6},{6,7},{7,0},{8,9},{9,10},{10,1... | collective-permute-start | bytes 491528 | tf_op jit(solution)/shard_map/ppermute | solution.py:254
  81.3 12.7 %collective-permute-start.18 = (f32[2,5,32,128]{3,2,1,0:T(8,128)S(1)}, f32[2,5,32,128]{3,2,1,0:T(8,128)S(1)}, u32[]{:S(2)}, u32[]{:S(2)}) collective-permute-start(f32[2,5,32,128]{3,2,1,0:T(8,128)S(1)} %get-tuple-element.78.refs_1_.lo_ref), channel_id=1, source_target_pairs={{0,7},{1,0},{2,1},{3,2},{4,3},{5,4},{6,5},{7,6},{8,15},{9,8},{10,9... | collective-permute-start | bytes 491528 | tf_op jit(solution)/shard_map/ppermute | solution.py:254
  90.3 7.1 %copy-start.3 = (bf16[128,128]{1,0:T(8,128)(2,1)S(1)}, bf16[128,128]{1,0:T(8,128)(2,1)}, u32[]{:S(2)}) copy-start(bf16[128,128]{1,0:T(8,128)(2,1)} %constant.25.clone.refs_8_.refs_7_) | copy-start | bytes 98308
  91.2 16.7 %collective-permute-start.19 = (f32[2,5,32,128]{3,2,1,0:T(8,128)S(1)}, f32[2,5,32,128]{3,2,1,0:T(8,128)S(1)}, u32[]{:S(2)}, u32[]{:S(2)}) collective-permute-start(f32[2,5,32,128]{3,2,1,0:T(8,128)S(1)} %get-tuple-element.69.refs_2_), channel_id=1, source_target_pairs={{0,1},{1,2},{2,3},{3,4},{4,5},{5,6},{6,7},{7,0},{8,9},{9,10},{10,1... | collective-permute-start | bytes 491528 | tf_op jit(solution)/shard_map/ppermute | solution.py:254
  91.3 16.6 %collective-permute-start.20 = (f32[2,5,32,128]{3,2,1,0:T(8,128)S(1)}, f32[2,5,32,128]{3,2,1,0:T(8,128)S(1)}, u32[]{:S(2)}, u32[]{:S(2)}) collective-permute-start(f32[2,5,32,128]{3,2,1,0:T(8,128)S(1)} %get-tuple-element.68.refs_1_), channel_id=1, source_target_pairs={{0,7},{1,0},{2,1},{3,2},{4,3},{5,4},{6,5},{7,6},{8,15},{9,8},{10,9... | collective-permute-start | bytes 491528 | tf_op jit(solution)/shard_map/ppermute | solution.py:254
  94.8 11.3 %collective-permute-start.21 = (f32[2,5,32,128]{3,2,1,0:T(8,128)S(1)}, f32[2,5,32,128]{3,2,1,0:T(8,128)S(1)}, u32[]{:S(2)}, u32[]{:S(2)}) collective-permute-start(f32[2,5,32,128]{3,2,1,0:T(8,128)S(1)} %get-tuple-element.81.refs_2_), channel_id=1, source_target_pairs={{0,1},{1,2},{2,3},{3,4},{4,5},{5,6},{6,7},{7,0},{8,9},{9,10},{10,1... | collective-permute-start | bytes 491528 | tf_op jit(solution)/shard_map/ppermute | solution.py:254
  94.8 11.2 %collective-permute-start.22 = (f32[2,5,32,128]{3,2,1,0:T(8,128)S(1)}, f32[2,5,32,128]{3,2,1,0:T(8,128)S(1)}, u32[]{:S(2)}, u32[]{:S(2)}) collective-permute-start(f32[2,5,32,128]{3,2,1,0:T(8,128)S(1)} %get-tuple-element.80.refs_1_), channel_id=1, source_target_pairs={{0,7},{1,0},{2,1},{3,2},{4,3},{5,4},{6,5},{7,6},{8,15},{9,8},{10,9... | collective-permute-start | bytes 491528 | tf_op jit(solution)/shard_map/ppermute | solution.py:254

commit v2 on v1

v2 whole, which is shorter than its diff:
```python
import math

import jax
import jax.numpy as jnp
import ml_dtypes
import numpy as np
from jax import lax
from jax.experimental import pallas as pl
from jax.experimental.pallas import tpu as pltpu
from jax.sharding import PartitionSpec as P

PR = 8
PASSES = 3
GROUPS = 2
ROWS = 128
FACE = 32
HIGH = 96

F32 = jnp.float32
BF16 = jnp.bfloat16


def gll_derivative():
    points = np.array([-1.0, -math.sqrt(3.0 / 7.0), 0.0, math.sqrt(3.0 / 7.0), 1.0])
    legendre = (35.0 * points**4 - 30.0 * points**2 + 3.0) / 8.0
    identity = np.eye(5, dtype=bool)
    spacing = np.where(identity, 1.0, points[:, None] - points[None, :])
    matrix = legendre[:, None] / legendre[None, :] / spacing
    corner = np.array([-5.0, 0.0, 0.0, 0.0, 5.0])[None, :]
    return np.where(identity, corner, matrix)


def coupling_value(offset, count):
    offset = offset % count
    if offset == 0:
        return 0.0
    angle = math.pi * offset / count
    return 0.5 * (-1.0) ** offset * math.cos(angle) / math.sin(angle)


FIRST = ((8, 16), (24, 40), (104, 112))
LAST = ((16, 24), (40, 56), (112, 120))
ENDS = 64


def node_rows():
    rows = np.zeros((5, 5, 5), dtype=np.int64)
    face_rest = list(range(0, 11)) + [16, 17, 18, 24]
    rest = [40] + list(range(56, HIGH)) + list(range(HIGH + 25, ROWS))
    face_used, used = 0, 0
    for i in range(5):
        for k in range(5):
            if k in (0, 4):
                local = (11 if k == 0 else 19) + i
            else:
                local = face_rest[face_used]
                face_used += 1
            rows[i, 0, k], rows[i, 4, k] = local, HIGH + local
            for j in range(1, 4):
                if k in (0, 4):
                    rows[i, j, k] = (25 if k == 0 else 41) + 3 * i + j - 1
                else:
                    rows[i, j, k] = rest[used]
                    used += 1
    return rows.reshape(125)


def end_rows():
    return [r for part in (FIRST, LAST) for a, b in part for r in range(a, b)]


def tables(own_circ):
    table = gll_derivative()
    eye = np.eye(5)
    first, last = np.diag([1.0, 0, 0, 0, 0]), np.diag([0, 0, 0, 0, 1.0])
    to_first, to_last = np.zeros((5, 5)), np.zeros((5, 5))
    to_first[0, 4] = 1.0
    to_last[4, 0] = 1.0

    def along(matrix, direction):
        parts = [eye, eye, eye]
        parts[direction] = matrix
        return np.kron(np.kron(parts[0], parts[1]), parts[2])

    rows = node_rows()
    order = np.zeros((ROWS, ROWS))
    order[rows, np.arange(125)] = 1.0

    def placed(matrix):
        return order[:, :125] @ matrix @ order[:, :125].T

    mix, damp = [], []
    for d in range(3):
        mix.append(placed(along(table - 5.0 * last + 5.0 * first, d)))
        damp.append(placed(along(5.0 * last + 5.0 * first, d)))
    if own_circ:
        mix[0] = mix[0] + placed(along(5.0 * to_last - 5.0 * to_first, 0))
        damp[0] = damp[0] + placed(along(-5.0 * to_last - 5.0 * to_first, 0))
    ends = end_rows()
    axial_mix = placed(along(5.0 * to_last - 5.0 * to_first, 2))[:, ends]
    axial_damp = placed(along(-5.0 * to_last - 5.0 * to_first, 2))[:, ends]
    none = np.zeros((ROWS, ENDS))

    def pair(matrix):
        return [np.concatenate([matrix, none], 1), np.concatenate([none, matrix], 1)]

    fluxes = np.stack(mix + pair(axial_mix)).astype(np.float32)
    dampers = np.stack(damp + pair(axial_damp)).astype(np.float32)
    return order, fluxes, dampers


def halves(values):
    high = values.astype(BF16)
    low = (values - high.astype(F32)).astype(BF16)
    return high, low


def dot32(a, b):
    return jnp.dot(a, b, preferred_element_type=F32)


def reorder(matrix, values, terms):
    total = None
    for _ in range(terms):
        part = values.astype(BF16)
        moved = dot32(matrix, part)
        total = moved if total is None else total + moved
        values = values - part.astype(F32)
    return total


def mixed(weights, parts):
    total = weights[0] * parts[0]
    for weight, part in zip(weights[1:], parts[1:]):
        total = total + weight * part
    return total


VMEM_LIMIT = 20 * 2**20
VMEM_ALONE = 56 * 2**20


def call(kernel, outs, ins, in_spaces, out_spaces=None, scratch=(), flops=0, alias=None, name=None, limit=VMEM_LIMIT):
    out_spaces = out_spaces or ["v"] * len(outs)
    space = {"v": pltpu.VMEM, "s": pltpu.SMEM, "a": pl.ANY, "h": pltpu.HBM}
    nbytes = sum(int(np.prod(x.shape)) * x.dtype.itemsize for x in list(ins) + list(outs))
    return pl.pallas_call(
        kernel,
        out_shape=outs,
        in_specs=[pl.BlockSpec(memory_space=space[s]) for s in in_spaces],
        out_specs=[pl.BlockSpec(memory_space=space[s]) for s in out_spaces],
        scratch_shapes=list(scratch),
        input_output_aliases=alias or {},
        compiler_params=pltpu.CompilerParams(vmem_limit_bytes=limit),
        cost_estimate=pl.CostEstimate(flops=flops, bytes_accessed=nbytes, transcendentals=0),
        name=name,
    )(*ins)


def shape(*dims, dtype=F32):
    return jax.ShapeDtypeStruct(dims, dtype)


def per_device(state, metric_scale, flux_jacobians, preconditioner, inflow):
    inst, nv, _, nodes, lanes = state.shape
    n_tm = lax.axis_size("tm")
    n_elem = lax.axis_size("elem")
    count = inst * n_tm
    own_circ = n_elem == PR
    block = ROWS // n_tm
    groups = GROUPS if inst % GROUPS == 0 else 1
    per = inst // groups
    order, flux_table, damp_table = tables(own_circ)
    order_b = order.astype(ml_dtypes.bfloat16)
    back_b = np.ascontiguousarray(order.T).astype(ml_dtypes.bfloat16)
    pairs = (nv + 1) // 2
    depth = nv * ROWS + pairs * 2 * ENDS
    node_row = node_rows()
    inlet_table = np.zeros((ROWS, ROWS), dtype=np.float32)
    inlet_table[node_row[0::5], np.arange(25)] = 1.0

    damping = jnp.max(jnp.sum(jnp.abs(flux_jacobians), axis=2), axis=1)
    coef = jnp.concatenate([flux_jacobians.reshape(-1), damping])
    precond = preconditioner.reshape(inst, nv, nv, lanes)
    inlet = jnp.pad(inflow.reshape(inst * nv, 25), ((0, ROWS - inst * nv), (0, ROWS - 25)))
    mix_index = np.full((ROWS, ROWS), -1, dtype=np.int32)
    for n in range(inst):
        for v in range(nv):
            for w in range(nv):
                mix_index[n * nv + w, n * nv + v] = v * nv + w

    def jac(ref, d, v, w):
        return ref[(d * nv + v) * nv + w]

    def damp(ref, d):
        return ref[3 * nv * nv + d]

    state_rows = state.reshape(inst, nv, nodes, 1, lanes)
    starts = [min(q * block, nodes - block) for q in range(n_tm)]
    spectral_order = np.zeros((ROWS, ROWS))
    for q in range(n_tm):
        for r in range(block):
            if starts[q] + r >= q * block:
                spectral_order[:, q * block + r] = order[:, starts[q] + r]

    def pack_kernel(state_ref, *refs):
        outs, sem = refs[:n_tm], refs[n_tm]
        me = lax.axis_index("tm")
        copies = []
        for d in range(n_tm):
            start = jnp.minimum(lax.rem(me + d, n_tm) * block, nodes - block)
            for n in range(inst):
                for v in range(nv):
                    copies.append(
                        pltpu.make_async_copy(
                            state_ref.at[n, v, pl.ds(start, block), 0, :], outs[d].at[n, v], sem.at[d, n, v]
                        )
                    )
        for copy in copies:
            copy.start()
        for copy in copies:
            copy.wait()

    piece = shape(inst, nv, block, lanes)
    pieces = call(
        pack_kernel,
        [piece] * n_tm,
        [state_rows],
        "h",
        scratch=[pltpu.SemaphoreType.DMA((n_tm, inst, nv))],
        name="pack",
        limit=VMEM_ALONE,
    )

    def after(x, *before):
        return lax.optimization_barrier((x, *before))[0]

    def along_tm(x, d):
        return lax.ppermute(x, "tm", [(i, (i + d) % n_tm) for i in range(n_tm)])

    def along_elem(x, d):
        return lax.ppermute(x, "elem", [(i, (i + d) % n_elem) for i in range(n_elem)])

    arrived = [pieces[0]] + [None] * (n_tm - 1)
    for d in sorted(range(1, n_tm), key=lambda d: abs(2 * d - n_tm)):
        arrived[d] = along_tm(pieces[d], d)

    def prep_kernel(
        state_ref, metric_ref, coef_ref, order_ref, flux_ref, damp_ref, inlet_ref, inlet_table_ref, mix_ref, p_ref,
        x_ref, lo_ref, hi_ref, m_ref, mf_ref, lhs_ref, col_ref, fc_ref, pc_ref, padded_ref, buf, sem,
    ):
        buf[pl.ds(ROWS - 8, 8), :] = jnp.zeros((8, lanes), F32)
        padded_ref[:, :, pl.ds(ROWS - 8, 8), :] = jnp.zeros((inst, nv, 8, lanes), F32)
        copies = [
            pltpu.make_async_copy(metric_ref.at[:, 0, :], buf.at[pl.ds(0, nodes), :], sem.at[0]),
        ]
        for n in range(inst):
            for v in range(nv):
                copies.append(
                    pltpu.make_async_copy(
                        state_ref.at[n, v, :, 0, :],
                        padded_ref.at[n, v, pl.ds(0, nodes), :],
                        sem.at[1 + n * nv + v],
                    )
                )
        for copy in copies:
            copy.start()
        for copy in copies:
            copy.wait()
        metric = reorder(order_ref[...], buf[...], 3)
        m_ref[...] = metric
        row = lax.broadcasted_iota(jnp.int32, (FACE, lanes), 0)
        mf_ref[0] = jnp.where(row < 25, metric[0:FACE], 0.0)
        mf_ref[1] = jnp.where(row < 25, metric[HIGH:ROWS], 0.0)
        for v in range(nv):
            for w in range(nv):
                value, own = jac(coef_ref, 1, v, w), damp(coef_ref, 1) if v == w else 0.0
                fc_ref[0, v, pl.ds(w, 1), :] = jnp.full((1, lanes), -5.0 * (value + own), F32)
                fc_ref[1, v, pl.ds(w, 1), :] = jnp.full((1, lanes), 5.0 * (value - own), F32)
        for side in range(2):
            tables_of = [fc_ref[side, u] for u in range(nv)]
            for n in range(inst):
                for v in range(nv):
                    weights = [p_ref[n, v, pl.ds(u, 1), :] for u in range(nv)]
                    pc_ref[side, n, v] = mixed(weights, tables_of)
        for v in range(nv):
            rows = pl.ds(v * ROWS, ROWS)
            for w in range(nv):
                total = mixed([jac(coef_ref, d, v, w) for d in range(3)], [flux_ref[d] for d in range(3)])
                if v == w:
                    for d in range(3):
                        total = total + damp(coef_ref, d) * damp_ref[d]
                high, low = halves(total)
                at = w * ROWS
                lhs_ref[rows, pl.ds(at, ROWS)] = high
                lhs_ref[rows, pl.ds(depth + at, ROWS)] = low
            for c in range(pairs):
                total = jac(coef_ref, 2, v, 2 * c) * flux_ref[3]
                if 2 * c + 1 < nv:
                    total = total + jac(coef_ref, 2, v, 2 * c + 1) * flux_ref[4]
                if v // 2 == c:
                    total = total + damp(coef_ref, 2) * damp_ref[3 + v % 2]
                high, low = halves(total)
                at = nv * ROWS + c * 2 * ENDS
                lhs_ref[rows, pl.ds(at, 2 * ENDS)] = high
                lhs_ref[rows, pl.ds(depth + at, 2 * ENDS)] = low
        cols = lax.dot_general(
            inlet_table_ref[...],
            inlet_ref[...],
            (((1,), (1,)), ((), ())),
            precision=lax.Precision.HIGHEST,
            preferred_element_type=F32,
        )
        blend = jnp.zeros((ROWS, ROWS), F32)
        for v in range(nv):
            for w in range(nv):
                value = jac(coef_ref, 2, v, w)
                if v == w:
                    value = value + damp(coef_ref, 2)
                blend = jnp.where(mix_ref[...] == v * nv + w, -5.0 * value, blend)
        cols = jnp.dot(cols, blend, precision=lax.Precision.HIGHEST, preferred_element_type=F32)
        col_ref[...] = metric[:, 0:1] * cols
        for n in range(inst):
            natural = jnp.concatenate([padded_ref[n, v] for v in range(nv)], axis=1)
            moved = reorder(order_ref[...], natural, 3)
            for v in range(nv):
                part = moved[:, v * lanes : (v + 1) * lanes]
                x_ref[n, v] = part
                lo_ref[n, v] = part[0:FACE]
                hi_ref[n, v] = part[HIGH:ROWS]

    x0, lo0, hi0, metric, metric_face, lhs, inlet_cols, face_coef, face_update = call(
        prep_kernel,
        [
            shape(inst, nv, ROWS, lanes),
            shape(inst, nv, FACE, lanes),
            shape(inst, nv, FACE, lanes),
            shape(ROWS, lanes),
            shape(2, FACE, lanes),
            shape(nv * ROWS, 2 * depth, dtype=BF16),
            shape(ROWS, ROWS),
            shape(2, nv, nv, lanes),
            shape(2, inst, nv, nv, lanes),
        ],
        [
            state_rows,
            metric_scale.reshape(nodes, 1, lanes),
            coef,
            order_b,
            flux_table,
            damp_table,
            inlet,
            inlet_table,
            mix_index,
            precond,
        ],
        "hhsvvvvvvv",
        scratch=[
            pltpu.VMEM((inst, nv, ROWS, lanes), F32),
            pltpu.VMEM((ROWS, lanes), F32),
            pltpu.SemaphoreType.DMA((1 + inst * nv,)),
        ],
        name="prep",
    )

    def bulk(xs, lhs_ref):
        cols = []
        lane = lax.broadcasted_iota(jnp.int32, (ENDS // 2, lanes), 1)
        for x in xs:
            ends = []
            for part in x:
                first = jnp.concatenate([part[a:b] for a, b in FIRST], axis=0)
                last = jnp.concatenate([part[a:b] for a, b in LAST], axis=0)
                ends.append(jnp.where(lane == lanes - 1, last, pltpu.roll(first, lanes - 1, 1)))
                ends.append(jnp.where(lane == 0, 0.0, pltpu.roll(last, 1, 1)))
            if nv % 2:
                ends.append(jnp.zeros((ENDS, lanes), F32))
            cols.append(jnp.concatenate(list(x) + ends, axis=0))
        high, low = halves(jnp.concatenate(cols, axis=1) if len(cols) > 1 else cols[0])
        both = dot32(lhs_ref[...], jnp.concatenate([high, high], axis=0))
        return both + dot32(lhs_ref[:, 0:depth], low)

    def block_of(result, n, v):
        return result[v * ROWS : (v + 1) * ROWS, n * lanes : (n + 1) * lanes]

    def whole(lo_ref, z_ref, hi_ref, n, at, v):
        return jnp.concatenate([lo_ref[n, v], z_ref[at, v, FACE:HIGH, :], hi_ref[n, v]], axis=0)

    bulk_flops = 2 * 3 * depth * nv * ROWS * lanes

    def advance(z, lo, hi, extra, first, size):
        def kernel(*refs):
            z_ref, lo_ref, hi_ref, m_ref, p_ref, lhs_ref = refs[:6]
            out_ref = refs[-1]
            metric_value = m_ref[...]
            for at in range(0, size, 2):
                ids = list(range(at, min(at + 2, size)))
                xs = [[whole(lo_ref, z_ref, hi_ref, n, n, v) for v in range(nv)] for n in ids]
                result = bulk(xs, lhs_ref)
                for m, n in enumerate(ids):
                    res = [metric_value * block_of(result, m, v) for v in range(nv)]
                    if extra is not None:
                        res = [res[v] + refs[6][n, v] for v in range(nv)]
                    for v in range(nv):
                        weights = [p_ref[first + n, v, pl.ds(w, 1), :] for w in range(nv)]
                        out_ref[n, v] = xs[m][v] - mixed(weights, res)

        ins = [z, lo, hi, metric, precond, lhs]
        ins = ins + ([] if extra is None else [extra])
        return call(
            kernel,
            [shape(size, nv, ROWS, lanes)],
            ins,
            "vvvvvv" + ("" if extra is None else "v"),
            flops=bulk_flops * size,
            name="advance",
        )[0]

    def face_terms(n, lo_ref, hi_ref, below_ref, above_ref, table_of, mf_ref):
        position = lax.rem(lax.axis_index("elem") + PR // 2, PR)
        low_w, high_w = [], []
        for v in range(nv):
            sign = -1.0 if v == 2 else 1.0
            low_w.append(jnp.where(position == 0, sign * lo_ref[n, v], below_ref[n, v]))
            high_w.append(jnp.where(position == PR - 1, sign * hi_ref[n, v], above_ref[n, v]))
        lows, highs = [], []
        for v in range(nv):
            lows.append(mf_ref[0] * mixed([table_of(0, v, w) for w in range(nv)], low_w))
            highs.append(mf_ref[1] * mixed([table_of(1, v, w) for w in range(nv)], high_w))
        return lows, highs

    def swap_faces(lo, hi):
        return along_elem(hi, 1), along_elem(lo, -1)

    def close_faces(z, lo, hi, below, above, first, size):
        def kernel(z_ref, lo_ref, hi_ref, below_ref, above_ref, mf_ref, pc_ref, nlo_ref, nhi_ref):
            for n in range(size):

                def table_of(side, v, w, n=n):
                    return pc_ref[side, first + n, v, pl.ds(w, 1), :]

                lows, highs = face_terms(n, lo_ref, hi_ref, below_ref, above_ref, table_of, mf_ref)
                for v in range(nv):
                    nlo_ref[n, v] = z_ref[n, v, 0:FACE, :] - lows[v]
                    nhi_ref[n, v] = z_ref[n, v, HIGH:ROWS, :] - highs[v]

        return call(
            kernel,
            [shape(size, nv, FACE, lanes)] * 2,
            [z, lo, hi, below, above, metric_face, face_update],
            "v" * 7,
            name="faces",
        )

    def circ_extra(z, lo, hi):
        x = jnp.concatenate([lo, z[:, :, FACE:HIGH], hi], axis=2)
        picks = np.zeros((2, 25, ROWS), dtype=np.float32)
        picks[0, np.arange(25), node_row[0:25]] = 1.0
        picks[1, np.arange(25), node_row[100:125]] = 1.0
        exact = lax.Precision.HIGHEST

        def picked(which):
            return jnp.einsum("pq,nvqa->nvpa", picks[which], x, precision=exact)

        def mix(values):
            return jnp.einsum("vw,nwqa->nvqa", flux_jacobians[0], values, precision=exact)

        def placed(which, values):
            return jnp.einsum("pq,nvpa->nvqa", picks[which], values, precision=exact)

        above, below = along_elem(picked(0), -PR), along_elem(picked(1), PR)
        high_term = 5.0 * (mix(above) - damping[0] * above)
        low_term = -5.0 * (mix(below) + damping[0] * below)
        return metric * (placed(1, high_term) + placed(0, low_term))

    below0, above0 = swap_faces(lo0, hi0)
    t0 = advance(x0, lo0, hi0, None if own_circ else circ_extra(x0, lo0, hi0), 0, inst)
    tlo, thi = close_faces(t0, lo0, hi0, below0, above0, 0, inst)

    half_pair = n_tm % 2 == 0

    def weight(offset, sign):
        return 0.5 * (coupling_value(offset, count) + sign * coupling_value(offset + count // 2, count))

    def weighted(terms):
        terms = [(c, x) for c, x in terms if abs(c) > 1e-12]
        return mixed([c for c, _ in terms], [x for _, x in terms])

    def coupling_kernel(*refs):
        x_refs, outs = refs[:n_tm], refs[n_tm:]

        def body(step, carry):
            v, rows = step // (block // 8), pl.ds(pl.multiple_of((step % (block // 8)) * 8, 8), 8)
            x = [[x_refs[d][i, v, rows, :] for i in range(inst)] for d in range(n_tm)]
            if half_pair:
                half = n_tm // 2
                sources = [(d, i) for d in range(half) for i in range(inst)]
                sums = [x[d][i] + x[d + half][i] for d, i in sources]
                diffs = [x[d][i] - x[d + half][i] for d, i in sources]
                for e in range(half):
                    for j in range(inst):
                        offsets = [inst * (e + d) + j - i for d, i in sources]
                        even = weighted([(weight(o, 1), s) for o, s in zip(offsets, sums)])
                        odd = weighted([(weight(o, -1), s) for o, s in zip(offsets, diffs)])
                        outs[e * groups + j // per][j % per, v, rows, :] = even + odd
                        outs[(e + half) * groups + j // per][j % per, v, rows, :] = even - odd
            else:
                sources = [(d, i) for d in range(n_tm) for i in range(inst)]
                for e in range(n_tm):
                    for j in range(inst):
                        offsets = [inst * (e + d) + j - i for d, i in sources]
                        outs[e * groups + j // per][j % per, v, rows, :] = weighted(
                            [(coupling_value(o, count), x[d][i]) for o, (d, i) in zip(offsets, sources)]
                        )
            return carry

        lax.fori_loop(0, nv * (block // 8), body, 0)

    coupled = call(
        coupling_kernel,
        [shape(per, nv, block, lanes)] * (n_tm * groups),
        arrived,
        "v" * n_tm,
        name="coupling",
    )
    spectral = [[coupled[g]] + [None] * (n_tm - 1) for g in range(groups)]
    for g in range(groups):
        for e in sorted(range(1, n_tm), key=lambda e: abs(2 * e - n_tm)):
            spectral[g][e] = along_tm(coupled[e * groups + g], e)

    def first_pass(parts, first):
        def kernel(*refs):
            part_refs = refs[:n_tm]
            t_ref, tlo_ref, thi_ref, p_ref, col_ref, order_ref = refs[n_tm : n_tm + 6]
            x_ref, lo_ref, hi_ref, s_ref, buf = refs[n_tm + 6 :]
            me = lax.axis_index("tm")
            for d in range(n_tm):
                start = pl.multiple_of(lax.rem(me - d + n_tm, n_tm) * block, block)
                for n in range(per):
                    for v in range(nv):
                        buf[n, v, pl.ds(start, block), :] = part_refs[d][n, v]
            lane = lax.broadcasted_iota(jnp.int32, (ROWS, lanes), 1)
            for n in range(per):
                natural = jnp.concatenate([buf[n, v] for v in range(nv)], axis=1)
                moved = reorder(order_ref[...], natural, 2)
                terms = []
                for v in range(nv):
                    c = (first + n) * nv + v
                    column = jnp.broadcast_to(col_ref[:, c : c + 1], (ROWS, lanes))
                    term = moved[:, v * lanes : (v + 1) * lanes] + jnp.where(lane == 0, column, 0.0)
                    s_ref[n, v] = term
                    terms.append(term)
                for v in range(nv):
                    weights = [p_ref[first + n, v, pl.ds(w, 1), :] for w in range(nv)]
                    x = whole(tlo_ref, t_ref, thi_ref, first + n, first + n, v) - mixed(weights, terms)
                    x_ref[n, v] = x
                    lo_ref[n, v] = x[0:FACE]
                    hi_ref[n, v] = x[HIGH:ROWS]

        return call(
            kernel,
            [
                shape(per, nv, ROWS, lanes),
                shape(per, nv, FACE, lanes),
                shape(per, nv, FACE, lanes),
                shape(per, nv, ROWS, lanes),
            ],
            list(parts) + [t0, tlo, thi, precond, inlet_cols, spectral_order.astype(ml_dtypes.bfloat16)],
            "v" * (n_tm + 6),
            scratch=[pltpu.VMEM((per, nv, ROWS, lanes), F32)],
            name="first_pass",
        )

    def write_out(moved_ref, out_ref, sem, first, work, meanwhile=None):
        copies = []
        for n in range(per):
            work(n)
            for v in range(nv):
                copy = pltpu.make_async_copy(
                    moved_ref.at[n, v, pl.ds(0, nodes), :], out_ref.at[first + n, v, :, 0, :], sem.at[n, v]
                )
                copy.start()
                copies.append(copy)
        if meanwhile is not None:
            meanwhile()
        for copy in copies:
            copy.wait()

    def last_bulk(z, lo, hi, extra, first, out):
        def kernel(*refs):
            z_ref, lo_ref, hi_ref, m_ref, lhs_ref, extra_ref, back_ref = refs[:7]
            r_ref, out_ref, buf, sem = refs[-4:]
            metric_value = m_ref[...]

            def work(n):
                x = [whole(lo_ref, z_ref, hi_ref, n, n, v) for v in range(nv)]
                moved = reorder(back_ref[...], jnp.concatenate(x, axis=1), 3)
                for v in range(nv):
                    buf[n, v] = moved[:, v * lanes : (v + 1) * lanes]

            def residual():
                for at in range(0, per, 2):
                    ids = list(range(at, min(at + 2, per)))
                    xs = [[whole(lo_ref, z_ref, hi_ref, n, n, v) for v in range(nv)] for n in ids]
                    result = bulk(xs, lhs_ref)
                    for m, n in enumerate(ids):
                        for v in range(nv):
                            r_ref[n, v] = metric_value * block_of(result, m, v) + extra_ref[n, v]

            write_out(buf, out_ref, sem, first, work, residual)

        ins = [z, lo, hi, metric, lhs, extra, back_b] + ([] if out is None else [out])
        return call(
            kernel,
            [shape(per, nv, ROWS, lanes), shape(inst, nv, nodes, 1, lanes)],
            ins,
            "vvvvvvv" + ("" if out is None else "a"),
            out_spaces="va",
            scratch=[pltpu.VMEM((per, nv, ROWS, lanes), F32), pltpu.SemaphoreType.DMA((per, nv))],
            flops=bulk_flops * per,
            alias=None if out is None else {7: 1},
            name="last_bulk",
        )

    def last_faces(r, lo, hi, below, above, first, out):
        def kernel(*refs):
            r_ref, lo_ref, hi_ref, below_ref, above_ref, mf_ref, fc_ref, back_ref = refs[:8]
            out_ref, buf, sem = refs[-3:]

            def table_of(side, v, w):
                return fc_ref[side, v, pl.ds(w, 1), :]

            def work(n):
                lows, highs = face_terms(n, lo_ref, hi_ref, below_ref, above_ref, table_of, mf_ref)
                full = [
                    jnp.concatenate(
                        [
                            r_ref[n, v, 0:FACE, :] + lows[v],
                            r_ref[n, v, FACE:HIGH, :],
                            r_ref[n, v, HIGH:ROWS, :] + highs[v],
                        ],
                        axis=0,
                    )
                    for v in range(nv)
                ]
                moved = reorder(back_ref[...], jnp.concatenate(full, axis=1), 2)
                for v in range(nv):
                    buf[n, v] = moved[:, v * lanes : (v + 1) * lanes]

            write_out(buf, out_ref, sem, first, work)

        ins = [r, lo, hi, below, above, metric_face, face_coef, back_b] + ([] if out is None else [out])
        return call(
            kernel,
            [shape(inst, nv, nodes, 1, lanes)],
            ins,
            "vvvvvvvv" + ("" if out is None else "a"),
            out_spaces="a",
            scratch=[pltpu.VMEM((per, nv, ROWS, lanes), F32), pltpu.SemaphoreType.DMA((per, nv))],
            alias=None if out is None else {8: 0},
            name="last_faces",
        )[0]

    new_state, final_residual = None, None
    chains, last = [None] * groups, None

    def begin(g):
        parts = spectral[g] if last is None else [after(spectral[g][0], last)] + spectral[g][1:]
        z, lo, hi, spec = first_pass(parts, g * per)
        chains[g] = (z, lo, hi, swap_faces(lo, hi), spec)
        return lo

    def local_part(g, count_done):
        nonlocal new_state
        z, lo, hi, swapped, spec = chains[g]
        extra = after(spec if own_circ else spec + circ_extra(z, lo, hi), last)
        if count_done < PASSES - 1:
            z = advance(z, lo, hi, extra, g * per, per)
        else:
            z, new_state = last_bulk(z, lo, hi, extra, g * per, new_state)
        chains[g] = (z, lo, hi, swapped, spec)
        return z

    def face_part(g, count_done):
        nonlocal final_residual
        z, lo, hi, (below, above), spec = chains[g]
        z = after(z, last)
        if count_done < PASSES - 1:
            lo, hi = close_faces(z, lo, hi, below, above, g * per, per)
            chains[g] = (z, lo, hi, swap_faces(lo, hi), spec)
            return lo
        final_residual = last_faces(z, lo, hi, below, above, g * per, final_residual)
        return final_residual

    for g in range(groups - 1):
        last = begin(g)
        last = local_part(g, 0)
    last = begin(groups - 1)
    for count_done in range(PASSES):
        for g in range(groups - 1):
            last = face_part(g, count_done)
        last = local_part(groups - 1, count_done)
        last = face_part(groups - 1, count_done)
        if count_done < PASSES - 1:
            for g in range(groups - 1):
                last = local_part(g, count_done + 1)
    return (new_state.reshape(state.shape), final_residual.reshape(state.shape))


def solution(mesh):
    in_specs = (
        P("tm", None, "elem", None, None),
        P("elem", None, None),
        P(),
        P("tm", None, None, "elem", None),
        P("tm", None, "elem", None),
    )
    out_specs = (P("tm", None, "elem", None, None), P("tm", None, "elem", None, None))
    return jax.shard_map(
        per_device, mesh=mesh, in_specs=in_specs, out_specs=out_specs, check_vma=False
    )
```

time: 111 us -> 95.3 us (0.86)
  other arithmetic: 19 us -> 1.66 us
  Pallas kernels: 41.7 us -> 25.3 us
  waiting for transfers between devices: 12.5 us -> 26.1 us
  starting transfers between devices: 31.2 us -> 34.8 us
  local copies, waits for them, and re-layouts: 4.28 us -> 5.9 us
    pallas_call x19, Pallas kernels: 41.7 us -> 25.3 us  [call(): pl.pallas_call(kernel, out_shape=outs, in_specs=[pl.BlockSpec(memory_spac...]
    unnamed x4 -> x1, other arithmetic: 15.1 us -> 0.78 us
    ppermute x9, waiting for transfers between devices: 11.1 us -> 22.1 us  [along_tm(): return lax.ppermute(x, 'tm', [(i, (i + d) % n_tm) for i in range(n_tm)])]
    ppermute x9, starting transfers between devices: 12.4 us -> 20 us  [along_tm(): return lax.ppermute(x, 'tm', [(i, (i + d) % n_tm) for i in range(n_tm)])]
    ppermute x14, starting transfers between devices: 18.8 us -> 14.8 us  [along_elem(): lax.ppermute(x, 'elem', [(i, (i + d) % n_elem) for i in range(n_elem)])]
    another operation x1 -> x0, other arithmetic: 3.78 us -> none  [per_device(): jnp.stack([-5.0 * (sum((flux_jacobians[2, v, w] * inlet[:, w] for w in ra...]
    unnamed x25 -> x22, local copies, waits for them, and re-layouts: 2.19 us -> 5.8 us
    ppermute x14, waiting for transfers between devices: 1.42 us -> 4.03 us  [along_elem(): lax.ppermute(x, 'elem', [(i, (i + d) % n_elem) for i in range(n_elem)])]
  transfers between devices with their start and end apart: 23 -> 23, of which waited for: 4 -> 11; matrix products, arithmetic and copies ran while one was open for 19% -> 3% of each run, Pallas kernels for 34% -> 22%
where the time goes in v2:
time: 95.3 us; the launch traced here: 94.8 us
  starting transfers between devices  34.8 us (37%)
  waiting for transfers between devices  26.1 us (27%)
  Pallas kernels  25.3 us (27%)
  local copies, waits for them, and re-layouts  5.9 us (6%)
  other arithmetic  1.66 us (2%)
  between operations  1.07 us (1%)
    pallas_call x19, Pallas kernels, call(): pl.pallas_call(kernel, out_shape=outs, in_specs=[pl.BlockSpec(memory_spac...  25.3 us
    ppermute x9, waiting for transfers between devices, along_tm(): return lax.ppermute(x, 'tm', [(i, (i + d) % n_tm) for i in range(n_tm)])  22.1 us
    ppermute x9, starting transfers between devices, along_tm(): return lax.ppermute(x, 'tm', [(i, (i + d) % n_tm) for i in range(n_tm)])  20 us
    ppermute x14, starting transfers between devices, along_elem(): lax.ppermute(x, 'elem', [(i, (i + d) % n_elem) for i in range(n_elem)])  14.8 us
    unnamed x22, local copies, waits for them, and re-layouts  5.8 us
    ppermute x14, waiting for transfers between devices, along_elem(): lax.ppermute(x, 'elem', [(i, (i + d) % n_elem) for i in range(n_elem)])  4.03 us
  transfers between devices with their start and end apart: 23, of which 11 were waited for; matrix products, arithmetic and copies ran while one was open for 3% of the time, Pallas kernels for 22%

profile of v2, /device:TPU:0, one launch (start us, length us, event | category | flops | bytes accessed | tf_op | source)
XLA Modules:
  0.0 94.8 jit_solution(11489671183276171035)
XLA Ops:
  0.7 3.1 %pack.1 = (f32[4,5,32,128]{3,2,1,0:T(8,128)}, f32[4,5,32,128]{3,2,1,0:T(8,128)}, f32[4,5,32,128]{3,2,1,0:T(8,128)}, f32[4,5,32,128]{3,2,1,0:T(8,128)}) custom-call(f32[4,5,125,1,128]{4,3,2,1,0:T(1,128)} %bitcast.7), custom_call_target="tpu_custom_call" | custom-call | bytes 2590720 | tf_op jit(solution)/shard_map/pack/pallas_call | solution.py:147
  3.8 3.1 %collective-permute-start = (f32[4,5,32,128]{3,2,1,0:T(8,128)}, f32[4,5,32,128]{3,2,1,0:T(8,128)S(1)}, u32[]{:S(2)}, u32[]{:S(2)}) collective-permute-start(f32[4,5,32,128]{3,2,1,0:T(8,128)} %get-tuple-element.54), channel_id=1, source_target_pairs={{0,8},{8,16},{16,24},{24,0},{1,9},{9,17},{17,25},{25,1},{2,10},{10... | collective-permute-start | bytes 983048 | tf_op jit(solution)/shard_map/ppermute | solution.py:239
  6.9 2.6 %collective-permute-start.1 = (f32[4,5,32,128]{3,2,1,0:T(8,128)}, f32[4,5,32,128]{3,2,1,0:T(8,128)S(1)}, u32[]{:S(2)}, u32[]{:S(2)}) collective-permute-start(f32[4,5,32,128]{3,2,1,0:T(8,128)} %get-tuple-element.55), channel_id=1, source_target_pairs={{0,16},{8,24},{16,0},{24,8},{1,17},{9,25},{17,1},{25,9},{2,18},{10... | collective-permute-start | bytes 983048 | tf_op jit(solution)/shard_map/ppermute | solution.py:239
  9.5 1.3 %collective-permute-start.2 = (f32[4,5,32,128]{3,2,1,0:T(8,128)}, f32[4,5,32,128]{3,2,1,0:T(8,128)S(1)}, u32[]{:S(2)}, u32[]{:S(2)}) collective-permute-start(f32[4,5,32,128]{3,2,1,0:T(8,128)} %get-tuple-element.56), channel_id=1, source_target_pairs={{0,24},{8,0},{16,8},{24,16},{1,25},{9,1},{17,9},{25,17},{2,26},{10... | collective-permute-start | bytes 983048 | tf_op jit(solution)/shard_map/ppermute | solution.py:239
  10.8 0.8 abs_reduce_fusion
  11.6 0.7 copy.28
  12.3 0.8 copy.40
  13.2 0.8 reduce
  14.2 1.0 %copy-done.4 = f32[5,128,128]{2,1,0:T(8,128)S(1)} copy-done((f32[5,128,128]{2,1,0:T(8,128)S(1)}, f32[5,128,128]{2,1,0:T(8,128)}, u32[]{:S(2)}) %copy-start.4) | copy-done | bytes 327704
  15.1 0.8 copy-done.6
  16.0 0.8 copy-done.7
  16.8 0.8 copy-done.8
  17.6 0.8 copy-done.9
  18.4 5.2 %prep.1 = (f32[4,5,128,128]{3,2,1,0:T(8,128)S(1)}, f32[4,5,32,128]{3,2,1,0:T(8,128)S(1)}, f32[4,5,32,128]{3,2,1,0:T(8,128)S(1)}, f32[128,128]{1,0:T(8,128)S(1)},...) custom-call(f32[4,5,125,1,128]{4,3,2,1,0:T(1,128)S(1)} %bitcast.8, ...), custom_call_target="tpu_custom_call" | custom-call | bytes 7159608 | tf_op jit(solution)/shard_map/prep/pallas_call | solution.py:147
  23.7 2.6 %collective-permute-start.7 = (f32[4,5,32,128]{3,2,1,0:T(8,128)S(1)}, f32[4,5,32,128]{3,2,1,0:T(8,128)S(1)}, u32[]{:S(2)}, u32[]{:S(2)}) collective-permute-start(f32[4,5,32,128]{3,2,1,0:T(8,128)S(1)} %get-tuple-element.63.refs_1_.lo_ref), channel_id=1, source_target_pairs={{0,7},{1,0},{2,1},{3,2},{4,3},{5,4},{6,5},{7,6},{8,15},{9,8},{10,9... | collective-permute-start | bytes 983048 | tf_op jit(solution)/shard_map/ppermute | solution.py:242
  26.4 4.6 %collective-permute-done.1.refs_2_ = f32[4,5,32,128]{3,2,1,0:T(8,128)S(1)} collective-permute-done((f32[4,5,32,128]{3,2,1,0:T(8,128)}, f32[4,5,32,128]{3,2,1,0:T(8,128)S(1)}, u32[]{:S(2)}, u32[]{:S(2)}) %collective-permute-start.1) | collective-permute-done | bytes 327712 | tf_op jit(solution)/shard_map/ppermute | solution.py:239
  31.0 0.9 coupling.1
  31.9 7.5 %collective-permute-start.3 = (f32[2,5,32,128]{3,2,1,0:T(8,128)S(1)}, f32[2,5,32,128]{3,2,1,0:T(8,128)S(1)}, u32[]{:S(2)}, u32[]{:S(2)}) collective-permute-start(f32[2,5,32,128]{3,2,1,0:T(8,128)S(1)} %get-tuple-element.59), channel_id=1, source_target_pairs={{0,8},{8,16},{16,24},{24,0},{1,9},{9,17},{17,25},{25,1},{2,10},{10... | collective-permute-start | bytes 491528 | tf_op jit(solution)/shard_map/ppermute | solution.py:239
  39.4 1.6 %collective-permute-start.4 = (f32[2,5,32,128]{3,2,1,0:T(8,128)S(1)}, f32[2,5,32,128]{3,2,1,0:T(8,128)S(1)}, u32[]{:S(2)}, u32[]{:S(2)}) collective-permute-start(f32[2,5,32,128]{3,2,1,0:T(8,128)S(1)} %get-tuple-element.60), channel_id=1, source_target_pairs={{0,16},{8,24},{16,0},{24,8},{1,17},{9,25},{17,1},{25,9},{2,18},{10... | collective-permute-start | bytes 491528 | tf_op jit(solution)/shard_map/ppermute | solution.py:239
  41.0 0.9 collective-permute-start.5
  41.9 1.9 %collective-permute-start.10 = (f32[2,5,32,128]{3,2,1,0:T(8,128)S(1)}, f32[2,5,32,128]{3,2,1,0:T(8,128)S(1)}, u32[]{:S(2)}, u32[]{:S(2)}) collective-permute-start(f32[2,5,32,128]{3,2,1,0:T(8,128)S(1)} %get-tuple-element.80), channel_id=1, source_target_pairs={{0,24},{8,0},{16,8},{24,16},{1,25},{9,1},{17,9},{25,17},{2,26},{10... | collective-permute-start | bytes 491528 | tf_op jit(solution)/shard_map/ppermute | solution.py:239
  43.9 1.4 %collective-permute-done.3.refs_1_ = f32[2,5,32,128]{3,2,1,0:T(8,128)S(1)} collective-permute-done((f32[2,5,32,128]{3,2,1,0:T(8,128)S(1)}, f32[2,5,32,128]{3,2,1,0:T(8,128)S(1)}, u32[]{:S(2)}, u32[]{:S(2)}) %collective-permute-start.3) | collective-permute-done | bytes 163872 | tf_op jit(solution)/shard_map/ppermute | solution.py:239
  45.3 1.0 %collective-permute-start.9 = (f32[2,5,32,128]{3,2,1,0:T(8,128)S(1)}, f32[2,5,32,128]{3,2,1,0:T(8,128)S(1)}, u32[]{:S(2)}, u32[]{:S(2)}) collective-permute-start(f32[2,5,32,128]{3,2,1,0:T(8,128)S(1)} %get-tuple-element.79), channel_id=1, source_target_pairs={{0,16},{8,24},{16,0},{24,8},{1,17},{9,25},{17,1},{25,9},{2,18},{10... | collective-permute-start | bytes 491528 | tf_op jit(solution)/shard_map/ppermute | solution.py:239
  46.3 2.7 %advance.5.z_ref.refs_4_ = f32[4,5,128,128]{3,2,1,0:T(8,128)S(1)} custom-call(f32[4,5,128,128]{3,2,1,0:T(8,128)S(1)} %get-tuple-element.62.refs_0_, f32[4,5,32,128]{3,2,1,0:T(8,128)S(1)} %get-tuple-element.63.refs_1_.lo_ref, f32[4,5,32,128]{3,2,1,0:T(8,128)S(1)} %get-tuple-element.64.refs_2_.hi_ref, f32[128,128]{1,0:T(8,128)S(1)} %get-tuple-element.65.refs_3_, ...), custom_call_target="tpu_custom_call" | custom-call | flops 2013265920 | bytes 6014976 | tf_op jit(solution)/shard_map/advance/pallas_call | solution.py:147
  49.3 1.6 %collective-permute-done.4.refs_2_ = f32[2,5,32,128]{3,2,1,0:T(8,128)S(1)} collective-permute-done((f32[2,5,32,128]{3,2,1,0:T(8,128)S(1)}, f32[2,5,32,128]{3,2,1,0:T(8,128)S(1)}, u32[]{:S(2)}, u32[]{:S(2)}) %collective-permute-start.4) | collective-permute-done | bytes 163872 | tf_op jit(solution)/shard_map/ppermute | solution.py:239
  51.0 1.0 %collective-permute-done.5.refs_3_ = f32[2,5,32,128]{3,2,1,0:T(8,128)S(1)} collective-permute-done((f32[2,5,32,128]{3,2,1,0:T(8,128)S(1)}, f32[2,5,32,128]{3,2,1,0:T(8,128)S(1)}, u32[]{:S(2)}, u32[]{:S(2)}) %collective-permute-start.5) | collective-permute-done | bytes 163872 | tf_op jit(solution)/shard_map/ppermute | solution.py:239
  51.9 0.6 first_pass.2
  52.5 1.1 %collective-permute-start.12 = (f32[2,5,32,128]{3,2,1,0:T(8,128)S(1)}, f32[2,5,32,128]{3,2,1,0:T(8,128)S(1)}, u32[]{:S(2)}, u32[]{:S(2)}) collective-permute-start(f32[2,5,32,128]{3,2,1,0:T(8,128)S(1)} %get-tuple-element.73.refs_1_.lo_ref), channel_id=1, source_target_pairs={{0,7},{1,0},{2,1},{3,2},{4,3},{5,4},{6,5},{7,6},{8,15},{9,8},{10,9... | collective-permute-start | bytes 491528 | tf_op jit(solution)/shard_map/ppermute | solution.py:242
  53.6 1.4 %advance.6.z_ref.refs_0_ = f32[2,5,128,128]{3,2,1,0:T(8,128)S(1)} custom-call(f32[2,5,128,128]{3,2,1,0:T(8,128)S(1)} %get-tuple-element.72.refs_0_, f32[2,5,32,128]{3,2,1,0:T(8,128)S(1)} %get-tuple-element.73.refs_1_.lo_ref, f32[2,5,32,128]{3,2,1,0:T(8,128)S(1)} %get-tuple-element.74.refs_2_.hi_ref, f32[128,128]{1,0:T(8,128)S(1)} %get-tuple-element.65.refs_3_, ...), custom_call_target="tpu_custom_call" | custom-call | flops 1006632960 | bytes 5031936 | tf_op jit(solution)/shard_map/advance/pallas_call | solution.py:147
  55.0 0.7 collective-permute-done.10.refs_3_
  55.7 3.7 %collective-permute-done.8.refs_1_ = f32[2,5,32,128]{3,2,1,0:T(8,128)S(1)} collective-permute-done((f32[2,5,32,128]{3,2,1,0:T(8,128)S(1)}, f32[2,5,32,128]{3,2,1,0:T(8,128)S(1)}, u32[]{:S(2)}, u32[]{:S(2)}) %collective-permute-start.8) | collective-permute-done | bytes 163872 | tf_op jit(solution)/shard_map/ppermute | solution.py:239
  59.4 9.0 %collective-permute-done.9.refs_2_ = f32[2,5,32,128]{3,2,1,0:T(8,128)S(1)} collective-permute-done((f32[2,5,32,128]{3,2,1,0:T(8,128)S(1)}, f32[2,5,32,128]{3,2,1,0:T(8,128)S(1)}, u32[]{:S(2)}, u32[]{:S(2)}) %collective-permute-start.9) | collective-permute-done | bytes 163872 | tf_op jit(solution)/shard_map/ppermute | solution.py:239
  68.4 0.6 first_pass.3
  69.1 2.6 %collective-permute-start.14 = (f32[2,5,32,128]{3,2,1,0:T(8,128)S(1)}, f32[2,5,32,128]{3,2,1,0:T(8,128)S(1)}, u32[]{:S(2)}, u32[]{:S(2)}) collective-permute-start(f32[2,5,32,128]{3,2,1,0:T(8,128)S(1)} %get-tuple-element.82.refs_1_.lo_ref), channel_id=1, source_target_pairs={{0,7},{1,0},{2,1},{3,2},{4,3},{5,4},{6,5},{7,6},{8,15},{9,8},{10,9... | collective-permute-start | bytes 491528 | tf_op jit(solution)/shard_map/ppermute | solution.py:242
  72.4 1.4 %advance.7.z_ref.refs_0_ = f32[2,5,128,128]{3,2,1,0:T(8,128)S(1)} custom-call(f32[2,5,128,128]{3,2,1,0:T(8,128)S(1)} %get-tuple-element.81.refs_0_, f32[2,5,32,128]{3,2,1,0:T(8,128)S(1)} %get-tuple-element.82.refs_1_.lo_ref, f32[2,5,32,128]{3,2,1,0:T(8,128)S(1)} %get-tuple-element.83.refs_2_.hi_ref, f32[128,128]{1,0:T(8,128)S(1)} %get-tuple-element.65.refs_3_, ...), custom_call_target="tpu_custom_call" | custom-call | flops 1006632960 | bytes 5031936 | tf_op jit(solution)/shard_map/advance/pallas_call | solution.py:147
  73.9 0.9 collective-permute-done.13.below_ref
  74.7 1.4 %collective-permute-done.14.above_ref = f32[2,5,32,128]{3,2,1,0:T(8,128)S(1)} collective-permute-done((f32[2,5,32,128]{3,2,1,0:T(8,128)S(1)}, f32[2,5,32,128]{3,2,1,0:T(8,128)S(1)}, u32[]{:S(2)}, u32[]{:S(2)}) %collective-permute-start.14) | collective-permute-done | bytes 163872 | tf_op jit(solution)/shard_map/ppermute | solution.py:242
  76.2 2.9 %collective-permute-start.18 = (f32[2,5,32,128]{3,2,1,0:T(8,128)S(1)}, f32[2,5,32,128]{3,2,1,0:T(8,128)S(1)}, u32[]{:S(2)}, u32[]{:S(2)}) collective-permute-start(f32[2,5,32,128]{3,2,1,0:T(8,128)S(1)} %get-tuple-element.88.refs_1_.lo_ref), channel_id=1, source_target_pairs={{0,7},{1,0},{2,1},{3,2},{4,3},{5,4},{6,5},{7,6},{8,15},{9,8},{10,9... | collective-permute-start | bytes 491528 | tf_op jit(solution)/shard_map/ppermute | solution.py:242
  79.1 1.4 %advance.8.z_ref.refs_0_ = f32[2,5,128,128]{3,2,1,0:T(8,128)S(1)} custom-call(f32[2,5,128,128]{3,2,1,0:T(8,128)S(1)} %advance.6.z_ref.refs_0_, f32[2,5,32,128]{3,2,1,0:T(8,128)S(1)} %get-tuple-element.86.refs_1_.lo_ref, f32[2,5,32,128]{3,2,1,0:T(8,128)S(1)} %get-tuple-element.90.refs_2_.hi_ref, f32[128,128]{1,0:T(8,128)S(1)} %get-tuple-element.65.refs_3_, ...), custom_call_target="tpu_custom_call" | custom-call | flops 1006632960 | bytes 5031936 | tf_op jit(solution)/shard_map/advance/pallas_call | solution.py:147
  80.7 2.7 %collective-permute-start.20 = (f32[2,5,32,128]{3,2,1,0:T(8,128)S(1)}, f32[2,5,32,128]{3,2,1,0:T(8,128)S(1)}, u32[]{:S(2)}, u32[]{:S(2)}) collective-permute-start(f32[2,5,32,128]{3,2,1,0:T(8,128)S(1)} %get-tuple-element.92.refs_1_), channel_id=1, source_target_pairs={{0,7},{1,0},{2,1},{3,2},{4,3},{5,4},{6,5},{7,6},{8,15},{9,8},{10,9... | collective-permute-start | bytes 491528 | tf_op jit(solution)/shard_map/ppermute | solution.py:242
  83.4 1.4 %advance.9.z_ref.refs_0_ = f32[2,5,128,128]{3,2,1,0:T(8,128)S(1)} custom-call(f32[2,5,128,128]{3,2,1,0:T(8,128)S(1)} %advance.7.z_ref.refs_0_, f32[2,5,32,128]{3,2,1,0:T(8,128)S(1)} %get-tuple-element.88.refs_1_.lo_ref, f32[2,5,32,128]{3,2,1,0:T(8,128)S(1)} %get-tuple-element.89.refs_2_.hi_ref, f32[128,128]{1,0:T(8,128)S(1)} %get-tuple-element.65.refs_3_, ...), custom_call_target="tpu_custom_call" | custom-call | flops 1006632960 | bytes 5031936 | tf_op jit(solution)/shard_map/advance/pallas_call | solution.py:147
  84.8 0.5 collective-permute-done.17.below_ref
  85.5 2.2 %collective-permute-start.22 = (f32[2,5,32,128]{3,2,1,0:T(8,128)S(1)}, f32[2,5,32,128]{3,2,1,0:T(8,128)S(1)}, u32[]{:S(2)}, u32[]{:S(2)}) collective-permute-start(f32[2,5,32,128]{3,2,1,0:T(8,128)S(1)} %get-tuple-element.94.refs_1_), channel_id=1, source_target_pairs={{0,7},{1,0},{2,1},{3,2},{4,3},{5,4},{6,5},{7,6},{8,15},{9,8},{10,9... | collective-permute-start | bytes 491528 | tf_op jit(solution)/shard_map/ppermute | solution.py:242
  87.7 1.6 %last_bulk.2 = (f32[2,5,128,128]{3,2,1,0:T(8,128)S(1)}, f32[4,5,125,1,128]{4,3,2,1,0:T(1,128)}) custom-call(f32[2,5,128,128]{3,2,1,0:T(8,128)S(1)} %advance.8.z_ref.refs_0_, f32[2,5,32,128]{3,2,1,0:T(8,128)S(1)} %get-tuple-element.92.refs_1_, f32[2,5,32,128]{3,2,1,0:T(8,128)S(1)} %get-tuple-element.96.refs_2_, f32[128,128]{1,0:T(8,128)S(1)} %get-tuple-element.65.refs_3_, ...), custom_call_target="tpu_custom_call" | custom-call | flops 1006632960 | bytes 6293504 | tf_op jit(solution)/shard_map/last_bulk/pallas_call | solution.py:147
  89.2 1.3 %collective-permute-done.19.refs_3_ = f32[2,5,32,128]{3,2,1,0:T(8,128)S(1)} collective-permute-done((f32[2,5,32,128]{3,2,1,0:T(8,128)S(1)}, f32[2,5,32,128]{3,2,1,0:T(8,128)S(1)}, u32[]{:S(2)}, u32[]{:S(2)}) %collective-permute-start.19) | collective-permute-done | bytes 163872 | tf_op jit(solution)/shard_map/ppermute | solution.py:242
  90.5 1.2 %last_faces.2.refs_8_ = f32[4,5,125,1,128]{4,3,2,1,0:T(1,128)} custom-call(f32[2,5,128,128]{3,2,1,0:T(8,128)S(1)} %get-tuple-element.98.refs_0_, f32[2,5,32,128]{3,2,1,0:T(8,128)S(1)} %get-tuple-element.92.refs_1_, f32[2,5,32,128]{3,2,1,0:T(8,128)S(1)} %get-tuple-element.96.refs_2_, f32[2,5,32,128]{3,2,1,0:T(8,128)S(1)} %collective-permute-done.19.refs_3_, ...), custom_call_target="tpu_custom_call" | custom-call | bytes 2681856 | tf_op jit(solution)/shard_map/last_faces/pallas_call | solution.py:147
  91.8 1.6 %last_bulk.3 = (f32[2,5,128,128]{3,2,1,0:T(8,128)S(1)}, f32[4,5,125,1,128]{4,3,2,1,0:T(1,128)}) custom-call(f32[2,5,128,128]{3,2,1,0:T(8,128)S(1)} %advance.9.z_ref.refs_0_, f32[2,5,32,128]{3,2,1,0:T(8,128)S(1)} %get-tuple-element.94.refs_1_, f32[2,5,32,128]{3,2,1,0:T(8,128)S(1)} %get-tuple-element.95.refs_2_, ...), custom_call_target="tpu_custom_call", output_to_operand_aliasing={{1}: (7, {})} | custom-call | flops 1006632960 | bytes 7573504 | tf_op jit(solution)/shard_map/last_bulk/pallas_call | solution.py:147
  93.4 1.3 %last_faces.3 = f32[4,5,125,1,128]{4,3,2,1,0:T(1,128)} custom-call(f32[2,5,128,128]{3,2,1,0:T(8,128)S(1)} %get-tuple-element.103.refs_0_, f32[2,5,32,128]{3,2,1,0:T(8,128)S(1)} %get-tuple-element.94.refs_1_, f32[2,5,32,128]{3,2,1,0:T(8,128)S(1)} %get-tuple-element.95.refs_2_, ...), custom_call_target="tpu_custom_call", output_to_operand_aliasing={{}: (8, {})} | custom-call | bytes 3961856 | tf_op jit(solution)/shard_map/last_faces/pallas_call | solution.py:147
  (47 shorter events, 1.9 us)
Async XLA Ops:
  0.6 13.5 %copy-start.3 = (f32[5,128,128]{2,1,0:T(8,128)S(1)}, f32[5,128,128]{2,1,0:T(8,128)}, u32[]{:S(2)}) copy-start(f32[5,128,128]{2,1,0:T(8,128)} %constant.21.clone.flux_ref) | copy-start | bytes 983044
  0.6 13.5 %copy-start = (f32[4,5,1,125,128]{4,2,3,1,0:T(1,128)S(1)}, f32[4,5,1,125,128]{4,2,3,1,0:T(1,128)}, u32[]{:S(2)}) copy-start(f32[4,5,1,125,128]{4,2,3,1,0:T(1,128)} %param.13) | copy-start | bytes 3840004
  3.8 22.6 %collective-permute-start = (f32[4,5,32,128]{3,2,1,0:T(8,128)}, f32[4,5,32,128]{3,2,1,0:T(8,128)S(1)}, u32[]{:S(2)}, u32[]{:S(2)}) collective-permute-start(f32[4,5,32,128]{3,2,1,0:T(8,128)} %get-tuple-element.54), channel_id=1, source_target_pairs={{0,8},{8,16},{16,24},{24,0},{1,9},{9,17},{17,25},{25,1},{2,10},{10... | collective-permute-start | bytes 983048 | tf_op jit(solution)/shard_map/ppermute | solution.py:239
  6.9 24.1 %collective-permute-start.1 = (f32[4,5,32,128]{3,2,1,0:T(8,128)}, f32[4,5,32,128]{3,2,1,0:T(8,128)S(1)}, u32[]{:S(2)}, u32[]{:S(2)}) collective-permute-start(f32[4,5,32,128]{3,2,1,0:T(8,128)} %get-tuple-element.55), channel_id=1, source_target_pairs={{0,16},{8,24},{16,0},{24,8},{1,17},{9,25},{17,1},{25,9},{2,18},{10... | collective-permute-start | bytes 983048 | tf_op jit(solution)/shard_map/ppermute | solution.py:239
  9.5 21.5 %collective-permute-start.2 = (f32[4,5,32,128]{3,2,1,0:T(8,128)}, f32[4,5,32,128]{3,2,1,0:T(8,128)S(1)}, u32[]{:S(2)}, u32[]{:S(2)}) collective-permute-start(f32[4,5,32,128]{3,2,1,0:T(8,128)} %get-tuple-element.56), channel_id=1, source_target_pairs={{0,24},{8,0},{16,8},{24,16},{1,25},{9,1},{17,9},{25,17},{2,26},{10... | collective-permute-start | bytes 983048 | tf_op jit(solution)/shard_map/ppermute | solution.py:239
  13.1 17.9 %copy-start.2 = (f32[4,5,32,128]{3,2,1,0:T(8,128)S(1)}, f32[4,5,32,128]{3,2,1,0:T(8,128)}, u32[]{:S(2)}) copy-start(f32[4,5,32,128]{3,2,1,0:T(8,128)} %get-tuple-element.53.refs_0_) | copy-start | bytes 983044
  14.2 1.0 %copy-start.4 = (f32[5,128,128]{2,1,0:T(8,128)S(1)}, f32[5,128,128]{2,1,0:T(8,128)}, u32[]{:S(2)}) copy-start(f32[5,128,128]{2,1,0:T(8,128)} %constant.22.clone.damp_ref) | copy-start | bytes 983044
  15.1 0.8 copy-start.6
  16.0 0.8 copy-start.7
  16.8 0.8 copy-start.8
  17.6 0.8 copy-start.9
  23.7 18.2 %collective-permute-start.6 = (f32[4,5,32,128]{3,2,1,0:T(8,128)S(1)}, f32[4,5,32,128]{3,2,1,0:T(8,128)S(1)}, u32[]{:S(2)}, u32[]{:S(2)}) collective-permute-start(f32[4,5,32,128]{3,2,1,0:T(8,128)S(1)} %get-tuple-element.64.refs_2_.hi_ref), channel_id=1, source_target_pairs={{0,1},{1,2},{2,3},{3,4},{4,5},{5,6},{6,7},{7,0},{8,9},{9,10},{10,1... | collective-permute-start | bytes 983048 | tf_op jit(solution)/shard_map/ppermute | solution.py:242
  23.7 20.1 %collective-permute-start.7 = (f32[4,5,32,128]{3,2,1,0:T(8,128)S(1)}, f32[4,5,32,128]{3,2,1,0:T(8,128)S(1)}, u32[]{:S(2)}, u32[]{:S(2)}) collective-permute-start(f32[4,5,32,128]{3,2,1,0:T(8,128)S(1)} %get-tuple-element.63.refs_1_.lo_ref), channel_id=1, source_target_pairs={{0,7},{1,0},{2,1},{3,2},{4,3},{5,4},{6,5},{7,6},{8,15},{9,8},{10,9... | collective-permute-start | bytes 983048 | tf_op jit(solution)/shard_map/ppermute | solution.py:242
  31.9 13.4 %collective-permute-start.3 = (f32[2,5,32,128]{3,2,1,0:T(8,128)S(1)}, f32[2,5,32,128]{3,2,1,0:T(8,128)S(1)}, u32[]{:S(2)}, u32[]{:S(2)}) collective-permute-start(f32[2,5,32,128]{3,2,1,0:T(8,128)S(1)} %get-tuple-element.59), channel_id=1, source_target_pairs={{0,8},{8,16},{16,24},{24,0},{1,9},{9,17},{17,25},{25,1},{2,10},{10... | collective-permute-start | bytes 491528 | tf_op jit(solution)/shard_map/ppermute | solution.py:239
  39.4 11.5 %collective-permute-start.4 = (f32[2,5,32,128]{3,2,1,0:T(8,128)S(1)}, f32[2,5,32,128]{3,2,1,0:T(8,128)S(1)}, u32[]{:S(2)}, u32[]{:S(2)}) collective-permute-start(f32[2,5,32,128]{3,2,1,0:T(8,128)S(1)} %get-tuple-element.60), channel_id=1, source_target_pairs={{0,16},{8,24},{16,0},{24,8},{1,17},{9,25},{17,1},{25,9},{2,18},{10... | collective-permute-start | bytes 491528 | tf_op jit(solution)/shard_map/ppermute | solution.py:239
  41.0 10.9 %collective-permute-start.5 = (f32[2,5,32,128]{3,2,1,0:T(8,128)S(1)}, f32[2,5,32,128]{3,2,1,0:T(8,128)S(1)}, u32[]{:S(2)}, u32[]{:S(2)}) collective-permute-start(f32[2,5,32,128]{3,2,1,0:T(8,128)S(1)} %get-tuple-element.61), channel_id=1, source_target_pairs={{0,24},{8,0},{16,8},{24,16},{1,25},{9,1},{17,9},{25,17},{2,26},{10... | collective-permute-start | bytes 491528 | tf_op jit(solution)/shard_map/ppermute | solution.py:239
  41.9 13.8 %collective-permute-start.10 = (f32[2,5,32,128]{3,2,1,0:T(8,128)S(1)}, f32[2,5,32,128]{3,2,1,0:T(8,128)S(1)}, u32[]{:S(2)}, u32[]{:S(2)}) collective-permute-start(f32[2,5,32,128]{3,2,1,0:T(8,128)S(1)} %get-tuple-element.80), channel_id=1, source_target_pairs={{0,24},{8,0},{16,8},{24,16},{1,25},{9,1},{17,9},{25,17},{2,26},{10... | collective-permute-start | bytes 491528 | tf_op jit(solution)/shard_map/ppermute | solution.py:239
  43.8 15.5 %collective-permute-start.8 = (f32[2,5,32,128]{3,2,1,0:T(8,128)S(1)}, f32[2,5,32,128]{3,2,1,0:T(8,128)S(1)}, u32[]{:S(2)}, u32[]{:S(2)}) collective-permute-start(f32[2,5,32,128]{3,2,1,0:T(8,128)S(1)} %get-tuple-element.78), channel_id=1, source_target_pairs={{0,8},{8,16},{16,24},{24,0},{1,9},{9,17},{17,25},{25,1},{2,10},{10... | collective-permute-start | bytes 491528 | tf_op jit(solution)/shard_map/ppermute | solution.py:239
  45.3 23.1 %collective-permute-start.9 = (f32[2,5,32,128]{3,2,1,0:T(8,128)S(1)}, f32[2,5,32,128]{3,2,1,0:T(8,128)S(1)}, u32[]{:S(2)}, u32[]{:S(2)}) collective-permute-start(f32[2,5,32,128]{3,2,1,0:T(8,128)S(1)} %get-tuple-element.79), channel_id=1, source_target_pairs={{0,16},{8,24},{16,0},{24,8},{1,17},{9,25},{17,1},{25,9},{2,18},{10... | collective-permute-start | bytes 491528 | tf_op jit(solution)/shard_map/ppermute | solution.py:239
  49.0 2.9 %copy-start.5 = (bf16[128,128]{1,0:T(8,128)(2,1)S(1)}, bf16[128,128]{1,0:T(8,128)(2,1)}, u32[]{:S(2)}) copy-start(bf16[128,128]{1,0:T(8,128)(2,1)} %constant.25.clone.refs_9_) | copy-start | bytes 98308
  52.5 19.2 %collective-permute-start.12 = (f32[2,5,32,128]{3,2,1,0:T(8,128)S(1)}, f32[2,5,32,128]{3,2,1,0:T(8,128)S(1)}, u32[]{:S(2)}, u32[]{:S(2)}) collective-permute-start(f32[2,5,32,128]{3,2,1,0:T(8,128)S(1)} %get-tuple-element.73.refs_1_.lo_ref), channel_id=1, source_target_pairs={{0,7},{1,0},{2,1},{3,2},{4,3},{5,4},{6,5},{7,6},{8,15},{9,8},{10,9... | collective-permute-start | bytes 491528 | tf_op jit(solution)/shard_map/ppermute | solution.py:242
  53.6 18.1 %collective-permute-start.11 = (f32[2,5,32,128]{3,2,1,0:T(8,128)S(1)}, f32[2,5,32,128]{3,2,1,0:T(8,128)S(1)}, u32[]{:S(2)}, u32[]{:S(2)}) collective-permute-start(f32[2,5,32,128]{3,2,1,0:T(8,128)S(1)} %get-tuple-element.74.refs_2_.hi_ref), channel_id=1, source_target_pairs={{0,1},{1,2},{2,3},{3,4},{4,5},{5,6},{6,7},{7,0},{8,9},{9,10},{10,1... | collective-permute-start | bytes 491528 | tf_op jit(solution)/shard_map/ppermute | solution.py:242
  69.0 5.7 %collective-permute-start.13 = (f32[2,5,32,128]{3,2,1,0:T(8,128)S(1)}, f32[2,5,32,128]{3,2,1,0:T(8,128)S(1)}, u32[]{:S(2)}, u32[]{:S(2)}) collective-permute-start(f32[2,5,32,128]{3,2,1,0:T(8,128)S(1)} %get-tuple-element.83.refs_2_.hi_ref), channel_id=1, source_target_pairs={{0,1},{1,2},{2,3},{3,4},{4,5},{5,6},{6,7},{7,0},{8,9},{9,10},{10,1... | collective-permute-start | bytes 491528 | tf_op jit(solution)/shard_map/ppermute | solution.py:242
  69.1 7.0 %collective-permute-start.14 = (f32[2,5,32,128]{3,2,1,0:T(8,128)S(1)}, f32[2,5,32,128]{3,2,1,0:T(8,128)S(1)}, u32[]{:S(2)}, u32[]{:S(2)}) collective-permute-start(f32[2,5,32,128]{3,2,1,0:T(8,128)S(1)} %get-tuple-element.82.refs_1_.lo_ref), channel_id=1, source_target_pairs={{0,7},{1,0},{2,1},{3,2},{4,3},{5,4},{6,5},{7,6},{8,15},{9,8},{10,9... | collective-permute-start | bytes 491528 | tf_op jit(solution)/shard_map/ppermute | solution.py:242
  71.9 8.6 %collective-permute-start.16 = (f32[2,5,32,128]{3,2,1,0:T(8,128)S(1)}, f32[2,5,32,128]{3,2,1,0:T(8,128)S(1)}, u32[]{:S(2)}, u32[]{:S(2)}) collective-permute-start(f32[2,5,32,128]{3,2,1,0:T(8,128)S(1)} %get-tuple-element.86.refs_1_.lo_ref), channel_id=1, source_target_pairs={{0,7},{1,0},{2,1},{3,2},{4,3},{5,4},{6,5},{7,6},{8,15},{9,8},{10,9... | collective-permute-start | bytes 491528 | tf_op jit(solution)/shard_map/ppermute | solution.py:242
  71.9 8.6 %collective-permute-start.15 = (f32[2,5,32,128]{3,2,1,0:T(8,128)S(1)}, f32[2,5,32,128]{3,2,1,0:T(8,128)S(1)}, u32[]{:S(2)}, u32[]{:S(2)}) collective-permute-start(f32[2,5,32,128]{3,2,1,0:T(8,128)S(1)} %get-tuple-element.90.refs_2_.hi_ref), channel_id=1, source_target_pairs={{0,1},{1,2},{2,3},{3,4},{4,5},{5,6},{6,7},{7,0},{8,9},{9,10},{10,1... | collective-permute-start | bytes 491528 | tf_op jit(solution)/shard_map/ppermute | solution.py:242
  76.2 9.1 %collective-permute-start.18 = (f32[2,5,32,128]{3,2,1,0:T(8,128)S(1)}, f32[2,5,32,128]{3,2,1,0:T(8,128)S(1)}, u32[]{:S(2)}, u32[]{:S(2)}) collective-permute-start(f32[2,5,32,128]{3,2,1,0:T(8,128)S(1)} %get-tuple-element.88.refs_1_.lo_ref), channel_id=1, source_target_pairs={{0,7},{1,0},{2,1},{3,2},{4,3},{5,4},{6,5},{7,6},{8,15},{9,8},{10,9... | collective-permute-start | bytes 491528 | tf_op jit(solution)/shard_map/ppermute | solution.py:242
  79.1 6.2 %collective-permute-start.17 = (f32[2,5,32,128]{3,2,1,0:T(8,128)S(1)}, f32[2,5,32,128]{3,2,1,0:T(8,128)S(1)}, u32[]{:S(2)}, u32[]{:S(2)}) collective-permute-start(f32[2,5,32,128]{3,2,1,0:T(8,128)S(1)} %get-tuple-element.89.refs_2_.hi_ref), channel_id=1, source_target_pairs={{0,1},{1,2},{2,3},{3,4},{4,5},{5,6},{6,7},{7,0},{8,9},{9,10},{10,1... | collective-permute-start | bytes 491528 | tf_op jit(solution)/shard_map/ppermute | solution.py:242
  80.7 9.8 %collective-permute-start.20 = (f32[2,5,32,128]{3,2,1,0:T(8,128)S(1)}, f32[2,5,32,128]{3,2,1,0:T(8,128)S(1)}, u32[]{:S(2)}, u32[]{:S(2)}) collective-permute-start(f32[2,5,32,128]{3,2,1,0:T(8,128)S(1)} %get-tuple-element.92.refs_1_), channel_id=1, source_target_pairs={{0,7},{1,0},{2,1},{3,2},{4,3},{5,4},{6,5},{7,6},{8,15},{9,8},{10,9... | collective-permute-start | bytes 491528 | tf_op jit(solution)/shard_map/ppermute | solution.py:242
  83.4 7.1 %collective-permute-start.19 = (f32[2,5,32,128]{3,2,1,0:T(8,128)S(1)}, f32[2,5,32,128]{3,2,1,0:T(8,128)S(1)}, u32[]{:S(2)}, u32[]{:S(2)}) collective-permute-start(f32[2,5,32,128]{3,2,1,0:T(8,128)S(1)} %get-tuple-element.96.refs_2_), channel_id=1, source_target_pairs={{0,1},{1,2},{2,3},{3,4},{4,5},{5,6},{6,7},{7,0},{8,9},{9,10},{10,1... | collective-permute-start | bytes 491528 | tf_op jit(solution)/shard_map/ppermute | solution.py:242
  84.8 2.9 %copy-start.1 = (bf16[128,128]{1,0:T(8,128)(2,1)S(1)}, bf16[128,128]{1,0:T(8,128)(2,1)}, u32[]{:S(2)}) copy-start(bf16[128,128]{1,0:T(8,128)(2,1)} %constant.26.clone.refs_6_.refs_7_) | copy-start | bytes 98308
  85.5 7.9 %collective-permute-start.22 = (f32[2,5,32,128]{3,2,1,0:T(8,128)S(1)}, f32[2,5,32,128]{3,2,1,0:T(8,128)S(1)}, u32[]{:S(2)}, u32[]{:S(2)}) collective-permute-start(f32[2,5,32,128]{3,2,1,0:T(8,128)S(1)} %get-tuple-element.94.refs_1_), channel_id=1, source_target_pairs={{0,7},{1,0},{2,1},{3,2},{4,3},{5,4},{6,5},{7,6},{8,15},{9,8},{10,9... | collective-permute-start | bytes 491528 | tf_op jit(solution)/shard_map/ppermute | solution.py:242
  87.7 5.7 %collective-permute-start.21 = (f32[2,5,32,128]{3,2,1,0:T(8,128)S(1)}, f32[2,5,32,128]{3,2,1,0:T(8,128)S(1)}, u32[]{:S(2)}, u32[]{:S(2)}) collective-permute-start(f32[2,5,32,128]{3,2,1,0:T(8,128)S(1)} %get-tuple-element.95.refs_2_), channel_id=1, source_target_pairs={{0,1},{1,2},{2,3},{3,4},{4,5},{5,6},{6,7},{7,0},{8,9},{9,10},{10,1... | collective-permute-start | bytes 491528 | tf_op jit(solution)/shard_map/ppermute | solution.py:242

commit v3 on v2

--- a/solution.py
+++ b/solution.py
@@ -137,13 +137,12 @@
 
 
 VMEM_LIMIT = 20 * 2**20
-VMEM_ALONE = 56 * 2**20
-
-
-def call(kernel, outs, ins, in_spaces, out_spaces=None, scratch=(), flops=0, alias=None, name=None, limit=VMEM_LIMIT):
+LONG = 2 * 10**9
+
+
+def call(kernel, outs, ins, in_spaces, out_spaces=None, scratch=(), flops=0, alias=None, name=None):
     out_spaces = out_spaces or ["v"] * len(outs)
     space = {"v": pltpu.VMEM, "s": pltpu.SMEM, "a": pl.ANY, "h": pltpu.HBM}
-    nbytes = sum(int(np.prod(x.shape)) * x.dtype.itemsize for x in list(ins) + list(outs))
     return pl.pallas_call(
         kernel,
         out_shape=outs,
@@ -151,8 +150,8 @@
         out_specs=[pl.BlockSpec(memory_space=space[s]) for s in out_spaces],
         scratch_shapes=list(scratch),
         input_output_aliases=alias or {},
-        compiler_params=pltpu.CompilerParams(vmem_limit_bytes=limit),
-        cost_estimate=pl.CostEstimate(flops=flops, bytes_accessed=nbytes, transcendentals=0),
+        compiler_params=pltpu.CompilerParams(vmem_limit_bytes=VMEM_LIMIT),
+        cost_estimate=pl.CostEstimate(flops=max(flops, 1), bytes_accessed=1, transcendentals=0),
         name=name,
     )(*ins)
 
@@ -209,13 +208,9 @@
         copies = []
         for d in range(n_tm):
             start = jnp.minimum(lax.rem(me + d, n_tm) * block, nodes - block)
-            for n in range(inst):
-                for v in range(nv):
-                    copies.append(
-                        pltpu.make_async_copy(
-                            state_ref.at[n, v, pl.ds(start, block), 0, :], outs[d].at[n, v], sem.at[d, n, v]
-                        )
-                    )
+            copies.append(
+                pltpu.make_async_copy(state_ref.at[:, :, pl.ds(start, block), 0, :], outs[d], sem.at[d])
+            )
         for copy in copies:
             copy.start()
         for copy in copies:
@@ -227,9 +222,8 @@
         [piece] * n_tm,
         [state_rows],
         "h",
-        scratch=[pltpu.SemaphoreType.DMA((n_tm, inst, nv))],
+        scratch=[pltpu.SemaphoreType.DMA((n_tm,))],
         name="pack",
-        limit=VMEM_ALONE,
     )
 
     def after(x, *before):
@@ -245,9 +239,14 @@
     for d in sorted(range(1, n_tm), key=lambda d: abs(2 * d - n_tm)):
         arrived[d] = along_tm(pieces[d], d)
 
+    scale_at = inst * nv + -(-inst * nv // (FACE // 8))
+
+    def table_place(index):
+        return inst * nv + index // (FACE // 8), 8 * (index % (FACE // 8))
+
     def prep_kernel(
         state_ref, metric_ref, coef_ref, order_ref, flux_ref, damp_ref, inlet_ref, inlet_table_ref, mix_ref, p_ref,
-        x_ref, lo_ref, hi_ref, m_ref, mf_ref, lhs_ref, col_ref, fc_ref, pc_ref, padded_ref, buf, sem,
+        x_ref, lo_ref, hi_ref, m_ref, mf_ref, lhs_ref, col_ref, fc_ref, pc_ref, low_table_ref, high_table_ref, padded_ref, buf, sem,
     ):
         buf[pl.ds(ROWS - 8, 8), :] = jnp.zeros((8, lanes), F32)
         padded_ref[:, :, pl.ds(ROWS - 8, 8), :] = jnp.zeros((inst, nv, 8, lanes), F32)
@@ -282,7 +281,17 @@
             for n in range(inst):
                 for v in range(nv):
                     weights = [p_ref[n, v, pl.ds(u, 1), :] for u in range(nv)]
-                    pc_ref[side, n, v] = mixed(weights, tables_of)
+                    update = mixed(weights, tables_of)
+                    pc_ref[side, n, v] = update
+                    at, row = table_place(n * nv + v)
+                    table_ref = (low_table_ref, high_table_ref)[side]
+                    table_ref[at, pl.ds(row, 8), :] = jnp.concatenate(
+                        [update, jnp.zeros((8 - nv, lanes), F32)], axis=0
+                    )
+            for spare in range(inst * nv, (scale_at - inst * nv) * (FACE // 8)):
+                at, row = table_place(spare)
+                table_ref[at, pl.ds(row, 8), :] = jnp.zeros((8, lanes), F32)
+            table_ref[scale_at] = mf_ref[side]
         for v in range(nv):
             rows = pl.ds(v * ROWS, ROWS)
             for w in range(nv):
@@ -328,8 +337,10 @@
                 x_ref[n, v] = part
                 lo_ref[n, v] = part[0:FACE]
                 hi_ref[n, v] = part[HIGH:ROWS]
-
-    x0, lo0, hi0, metric, metric_face, lhs, inlet_cols, face_coef, face_update = call(
+                low_table_ref[n * nv + v] = part[0:FACE]
+                high_table_ref[n * nv + v] = part[HIGH:ROWS]
+
+    x0, lo0, hi0, metric, metric_face, lhs, inlet_cols, face_coef, face_update, low_table, high_table = call(
         prep_kernel,
         [
             shape(inst, nv, ROWS, lanes),
@@ -341,6 +352,8 @@
             shape(ROWS, ROWS),
             shape(2, nv, nv, lanes),
             shape(2, inst, nv, nv, lanes),
+            shape(scale_at + 1, FACE, lanes),
+            shape(scale_at + 1, FACE, lanes),
         ],
         [
             state_rows,
@@ -386,9 +399,8 @@
     def whole(lo_ref, z_ref, hi_ref, n, at, v):
         return jnp.concatenate([lo_ref[n, v], z_ref[at, v, FACE:HIGH, :], hi_ref[n, v]], axis=0)
 
-    bulk_flops = 2 * 3 * depth * nv * ROWS * lanes
-
-    def advance(z, lo, hi, extra, first, size):
+
+    def advance(z, lo, hi, extra, first, size, flops=0):
         def kernel(*refs):
             z_ref, lo_ref, hi_ref, m_ref, p_ref, lhs_ref = refs[:6]
             out_ref = refs[-1]
@@ -412,17 +424,17 @@
             [shape(size, nv, ROWS, lanes)],
             ins,
             "vvvvvv" + ("" if extra is None else "v"),
-            flops=bulk_flops * size,
+            flops=flops,
             name="advance",
         )[0]
 
-    def face_terms(n, lo_ref, hi_ref, below_ref, above_ref, table_of, mf_ref):
+    def face_terms(n, lo_ref, hi_ref, below, above, table_of, mf_ref):
         position = lax.rem(lax.axis_index("elem") + PR // 2, PR)
         low_w, high_w = [], []
         for v in range(nv):
             sign = -1.0 if v == 2 else 1.0
-            low_w.append(jnp.where(position == 0, sign * lo_ref[n, v], below_ref[n, v]))
-            high_w.append(jnp.where(position == PR - 1, sign * hi_ref[n, v], above_ref[n, v]))
+            low_w.append(jnp.where(position == 0, sign * lo_ref[n, v], below[v]))
+            high_w.append(jnp.where(position == PR - 1, sign * hi_ref[n, v], above[v]))
         lows, highs = [], []
         for v in range(nv):
             lows.append(mf_ref[0] * mixed([table_of(0, v, w) for w in range(nv)], low_w))
@@ -439,7 +451,10 @@
                 def table_of(side, v, w, n=n):
                     return pc_ref[side, first + n, v, pl.ds(w, 1), :]
 
-                lows, highs = face_terms(n, lo_ref, hi_ref, below_ref, above_ref, table_of, mf_ref)
+                flat = len(below_ref.shape) == 3
+                below = [below_ref[n * nv + v] if flat else below_ref[n, v] for v in range(nv)]
+                above = [above_ref[n * nv + v] if flat else above_ref[n, v] for v in range(nv)]
+                lows, highs = face_terms(n, lo_ref, hi_ref, below, above, table_of, mf_ref)
                 for v in range(nv):
                     nlo_ref[n, v] = z_ref[n, v, 0:FACE, :] - lows[v]
                     nhi_ref[n, v] = z_ref[n, v, HIGH:ROWS, :] - highs[v]
@@ -452,6 +467,93 @@
             name="faces",
         )
 
+    def paired_first(z, lo, hi, spec, first):
+        def kernel(z_ref, lo_ref, hi_ref, m_ref, p_ref, lhs_ref, spec_ref, out_ref, down_ref, up_ref):
+            metric_value = m_ref[...]
+            for at in range(0, per, 2):
+                ids = list(range(at, min(at + 2, per)))
+                xs = [[whole(lo_ref, z_ref, hi_ref, n, n, v) for v in range(nv)] for n in ids]
+                result = bulk(xs, lhs_ref)
+                for m, n in enumerate(ids):
+                    res = [metric_value * block_of(result, m, v) + spec_ref[n, v] for v in range(nv)]
+                    for v in range(nv):
+                        weights = [p_ref[first + n, v, pl.ds(w, 1), :] for w in range(nv)]
+                        value = xs[m][v] - mixed(weights, res)
+                        out_ref[n, v] = value
+                        down_ref[0, n, v], up_ref[0, n, v] = lo_ref[n, v], hi_ref[n, v]
+                        down_ref[1, n, v], up_ref[1, n, v] = value[0:FACE], value[HIGH:ROWS]
+
+        return call(
+            kernel,
+            [shape(per, nv, ROWS, lanes)] + [shape(2, per, nv, FACE, lanes)] * 2,
+            [z, lo, hi, metric, precond, lhs, spec],
+            "v" * 7,
+            name="paired_first",
+        )
+
+    def paired_second(z, down, up, below, above, below_table, above_table, spec, first):
+        def kernel(*refs):
+            z_ref, down_ref, up_ref, below_ref, above_ref = refs[:5]
+            low_ref, high_ref, below_table_ref, above_table_ref = refs[5:9]
+            m_ref, p_ref, lhs_ref, spec_ref, out_ref, out_lo_ref, out_hi_ref = refs[9:]
+            metric_value = m_ref[...]
+            position = lax.rem(lax.axis_index("elem") + PR // 2, PR)
+
+            def update(table_ref, n, values):
+                result = []
+                for v in range(nv):
+                    at, row = table_place((first + n) * nv + v)
+                    weights = [table_ref[at, pl.ds(row + w, 1), :] for w in range(nv)]
+                    result.append(table_ref[scale_at] * mixed(weights, values))
+                return result
+
+            def across(at, own, other):
+                return [
+                    jnp.where(position == at, -own[v] if v == 2 else own[v], other[v]) for v in range(nv)
+                ]
+
+            def minus(a, b):
+                return [p - q for p, q in zip(a, b)]
+
+            for at in range(0, per, 2):
+                ids = list(range(at, min(at + 2, per)))
+                xs, beyond = [], []
+                for n in ids:
+                    lo, zlo = ([down_ref[k, n, v] for v in range(nv)] for k in range(2))
+                    hi, zhi = ([up_ref[k, n, v] for v in range(nv)] for k in range(2))
+                    low_w, low_z = ([below_ref[k, n, v] for v in range(nv)] for k in range(2))
+                    high_w, high_z = ([above_ref[k, n, v] for v in range(nv)] for k in range(2))
+                    new_lo = minus(zlo, update(low_ref, n, across(0, lo, low_w)))
+                    new_hi = minus(zhi, update(high_ref, n, across(PR - 1, hi, high_w)))
+                    next_low = across(0, new_lo, minus(low_z, update(below_table_ref, n, lo)))
+                    next_high = across(PR - 1, new_hi, minus(high_z, update(above_table_ref, n, hi)))
+                    xs.append(
+                        [
+                            jnp.concatenate([new_lo[v], z_ref[n, v, FACE:HIGH, :], new_hi[v]], axis=0)
+                            for v in range(nv)
+                        ]
+                    )
+                    beyond.append((update(low_ref, n, next_low), update(high_ref, n, next_high)))
+                result = bulk(xs, lhs_ref)
+                for m, n in enumerate(ids):
+                    res = [metric_value * block_of(result, m, v) + spec_ref[n, v] for v in range(nv)]
+                    for v in range(nv):
+                        weights = [p_ref[first + n, v, pl.ds(w, 1), :] for w in range(nv)]
+                        value = xs[m][v] - mixed(weights, res)
+                        lo, hi = value[0:FACE] - beyond[m][0][v], value[HIGH:ROWS] - beyond[m][1][v]
+                        out_ref[n, v] = value
+                        out_lo_ref[n, v] = lo
+                        out_hi_ref[n, v] = hi
+
+        return call(
+            kernel,
+            [shape(per, nv, ROWS, lanes)] + [shape(per, nv, FACE, lanes)] * 2,
+            [z, down, up, below, above, low_table, high_table, below_table, above_table]
+            + [metric, precond, lhs, spec],
+            "v" * 13,
+            name="paired_second",
+        )
+
     def circ_extra(z, lo, hi):
         x = jnp.concatenate([lo, z[:, :, FACE:HIGH], hi], axis=2)
         picks = np.zeros((2, 25, ROWS), dtype=np.float32)
@@ -473,7 +575,7 @@
         low_term = -5.0 * (mix(below) + damping[0] * below)
         return metric * (placed(1, high_term) + placed(0, low_term))
 
-    below0, above0 = swap_faces(lo0, hi0)
+    below0, above0 = swap_faces(low_table, high_table)
     t0 = advance(x0, lo0, hi0, None if own_circ else circ_extra(x0, lo0, hi0), 0, inst)
     tlo, thi = close_faces(t0, lo0, hi0, below0, above0, 0, inst)
 
@@ -528,9 +630,13 @@
         for e in sorted(range(1, n_tm), key=lambda e: abs(2 * e - n_tm)):
             spectral[g][e] = along_tm(coupled[e * groups + g], e)
 
-    def first_pass(parts, first):
+    def first_pass(parts, first, flops=0):
+        distances = list(range(n_tm))
+        if first > 0:
+            distances.sort(key=lambda d: min(d, n_tm - d))
+
         def kernel(*refs):
-            part_refs = refs[:n_tm]
+            part_refs = [refs[distances.index(d)] for d in range(n_tm)]
             t_ref, tlo_ref, thi_ref, p_ref, col_ref, order_ref = refs[n_tm : n_tm + 6]
             x_ref, lo_ref, hi_ref, s_ref, buf = refs[n_tm + 6 :]
             me = lax.axis_index("tm")
@@ -565,9 +671,10 @@
                 shape(per, nv, FACE, lanes),
                 shape(per, nv, ROWS, lanes),
             ],
-            list(parts) + [t0, tlo, thi, precond, inlet_cols, spectral_order.astype(ml_dtypes.bfloat16)],
+            [parts[d] for d in distances] + [t0, tlo, thi, precond, inlet_cols, spectral_order.astype(ml_dtypes.bfloat16)],
             "v" * (n_tm + 6),
             scratch=[pltpu.VMEM((per, nv, ROWS, lanes), F32)],
+            flops=flops,
             name="first_pass",
         )
 
@@ -617,7 +724,6 @@
             "vvvvvvv" + ("" if out is None else "a"),
             out_spaces="va",
             scratch=[pltpu.VMEM((per, nv, ROWS, lanes), F32), pltpu.SemaphoreType.DMA((per, nv))],
-            flops=bulk_flops * per,
             alias=None if out is None else {7: 1},
             name="last_bulk",
         )
@@ -631,7 +737,9 @@
                 return fc_ref[side, v, pl.ds(w, 1), :]
 
             def work(n):
-                lows, highs = face_terms(n, lo_ref, hi_ref, below_ref, above_ref, table_of, mf_ref)
+                below = [below_ref[n, v] for v in range(nv)]
+                above = [above_ref[n, v] for v in range(nv)]
+                lows, highs = face_terms(n, lo_ref, hi_ref, below, above, table_of, mf_ref)
                 full = [
                     jnp.concatenate(
                         [
@@ -664,18 +772,19 @@
     new_state, final_residual = None, None
     chains, last = [None] * groups, None
 
-    def begin(g):
+    def begin(g, swap):
         parts = spectral[g] if last is None else [after(spectral[g][0], last)] + spectral[g][1:]
-        z, lo, hi, spec = first_pass(parts, g * per)
-        chains[g] = (z, lo, hi, swap_faces(lo, hi), spec)
+        z, lo, hi, spec = first_pass(parts, g * per, LONG if g == groups - 1 else 0)
+        chains[g] = (z, lo, hi, swap_faces(lo, hi) if swap else None, spec)
         return lo
 
     def local_part(g, count_done):
         nonlocal new_state
         z, lo, hi, swapped, spec = chains[g]
-        extra = after(spec if own_circ else spec + circ_extra(z, lo, hi), last)
+        extra = spec if own_circ else spec + circ_extra(z, lo, hi)
+        extra = extra if last is None else after(extra, last)
         if count_done < PASSES - 1:
-            z = advance(z, lo, hi, extra, g * per, per)
+            z = advance(z, lo, hi, extra, g * per, per, LONG)
         else:
             z, new_state = last_bulk(z, lo, hi, extra, g * per, new_state)
         chains[g] = (z, lo, hi, swapped, spec)
@@ -692,18 +801,51 @@
         final_residual = last_faces(z, lo, hi, below, above, g * per, final_residual)
         return final_residual
 
-    for g in range(groups - 1):
-        last = begin(g)
-        last = local_part(g, 0)
-    last = begin(groups - 1)
-    for count_done in range(PASSES):
-        for g in range(groups - 1):
-            last = face_part(g, count_done)
-        last = local_part(groups - 1, count_done)
-        last = face_part(groups - 1, count_done)
-        if count_done < PASSES - 1:
-            for g in range(groups - 1):
-                last = local_part(g, count_done + 1)
+    def pair_begin(g):
+        z, lo, hi, _, spec = chains[g]
+        z, down, up = paired_first(z, lo, hi, after(spec, last), g * per)
+        chains[g] = (z, down, up, (along_elem(up, 1), along_elem(down, -1)), spec)
+        return z
+
+    def pair_end(g, *before):
+        z, down, up, (below, above), spec = chains[g]
+        z, lo, hi = paired_second(
+            z, down, up, below, above, below0, above0, after(spec, last), g * per
+        )
+        chains[g] = (z, lo, hi, None, spec)
+        return z
+
+    def pair_swap(g):
+        z, lo, hi, _, spec = chains[g]
+        lo, hi = lax.optimization_barrier((lo, hi, last))[:2]
+        chains[g] = (z, lo, hi, swap_faces(lo, hi), spec)
+
+    end = groups - 1
+    if own_circ and PASSES == 3:
+        for g in range(end):
+            last = begin(g, False)
+            last = pair_begin(g)
+        last = begin(end, True)
+        last = local_part(end, 0)
+        for g in range(end):
+            last = pair_end(g)
+        last = face_part(end, 0)
+        for g in range(end):
+            pair_swap(g)
+        last = local_part(end, 1)
+        for g in range(end):
+            last = local_part(g, 2)
+        last = face_part(end, 1)
+        for g in range(end):
+            last = face_part(g, 2)
+        last = local_part(end, 2)
+        last = face_part(end, 2)
+    else:
+        for g in range(groups):
+            last = begin(g, True)
+            for count_done in range(PASSES):
+                last = local_part(g, count_done)
+                last = face_part(g, count_done)
     return (new_state.reshape(state.shape), final_residual.reshape(state.shape))
 
 

time: 95.3 us -> 91.9 us (0.964)
  Pallas kernels: 25.3 us -> 23.3 us
  starting transfers between devices: 34.8 us -> 33 us
    ppermute x14 -> x12, starting transfers between devices: 14.8 us -> 11.6 us  [along_elem(): lax.ppermute(x, 'elem', [(i, (i + d) % n_elem) for i in range(n_elem)])]
    pallas_call x19 -> x17, Pallas kernels: 25.3 us -> 23.3 us  [call(): pl.pallas_call(kernel, out_shape=outs, in_specs=[pl.BlockSpec(memory_spac...]
    ppermute x9, starting transfers between devices: 20 us -> 21.4 us  [along_tm(): return lax.ppermute(x, 'tm', [(i, (i + d) % n_tm) for i in range(n_tm)])]
    ppermute x14 -> x12, waiting for transfers between devices: 4.03 us -> 3.7 us  [along_elem(): lax.ppermute(x, 'elem', [(i, (i + d) % n_elem) for i in range(n_elem)])]
  transfers between devices with their start and end apart: 23 -> 21, of which waited for: 11 -> 8; matrix products, arithmetic and copies ran while one was open for 3% -> 4% of each run, Pallas kernels for 22% -> 23%
where the time goes in v3:
time: 91.9 us; the launch traced here: 91 us
  starting transfers between devices  33 us (36%)
  waiting for transfers between devices  26.4 us (29%)
  Pallas kernels  23.3 us (25%)
  local copies, waits for them, and re-layouts  5.6 us (6%)
  other arithmetic  1.62 us (2%)
  between operations  1.06 us (1%)
    pallas_call x17, Pallas kernels, call(): pl.pallas_call(kernel, out_shape=outs, in_specs=[pl.BlockSpec(memory_spac...  23.3 us
    ppermute x9, waiting for transfers between devices, along_tm(): return lax.ppermute(x, 'tm', [(i, (i + d) % n_tm) for i in range(n_tm)])  22.7 us
    ppermute x9, starting transfers between devices, along_tm(): return lax.ppermute(x, 'tm', [(i, (i + d) % n_tm) for i in range(n_tm)])  21.4 us
    ppermute x12, starting transfers between devices, along_elem(): lax.ppermute(x, 'elem', [(i, (i + d) % n_elem) for i in range(n_elem)])  11.6 us
    unnamed x22, local copies, waits for them, and re-layouts  5.49 us
    ppermute x12, waiting for transfers between devices, along_elem(): lax.ppermute(x, 'elem', [(i, (i + d) % n_elem) for i in range(n_elem)])  3.7 us
  transfers between devices with their start and end apart: 21, of which 8 were waited for; matrix products, arithmetic and copies ran while one was open for 4% of the time, Pallas kernels for 23%

profile of v3, /device:TPU:0, one launch (start us, length us, event | category | flops | bytes accessed | tf_op | source)
XLA Modules:
  0.0 91.0 jit_solution(13039317030334893558)
XLA Ops:
  0.6 1.3 %copy-done = f32[4,5,1,125,128]{4,2,3,1,0:T(1,128)S(1)} copy-done((f32[4,5,1,125,128]{4,2,3,1,0:T(1,128)S(1)}, f32[4,5,1,125,128]{4,2,3,1,0:T(1,128)}, u32[]{:S(2)}) %copy-start) | copy-done | bytes 1280024
  1.9 1.0 %pack.1 = (f32[4,5,32,128]{3,2,1,0:T(8,128)S(1)}, f32[4,5,32,128]{3,2,1,0:T(8,128)}, f32[4,5,32,128]{3,2,1,0:T(8,128)}, f32[4,5,32,128]{3,2,1,0:T(8,128)S(1)}) custom-call(f32[4,5,125,1,128]{4,3,2,1,0:T(1,128)S(1)} %bitcast.7), custom_call_target="tpu_custom_call" | custom-call | flops 1 | bytes 1 | tf_op jit(solution)/shard_map/pack/pallas_call | solution.py:146
  2.9 3.1 %collective-permute-start = (f32[4,5,32,128]{3,2,1,0:T(8,128)}, f32[4,5,32,128]{3,2,1,0:T(8,128)S(1)}, u32[]{:S(2)}, u32[]{:S(2)}) collective-permute-start(f32[4,5,32,128]{3,2,1,0:T(8,128)} %get-tuple-element.62), channel_id=1, source_target_pairs={{0,8},{8,16},{16,24},{24,0},{1,9},{9,17},{17,25},{25,1},{2,10},{10... | collective-permute-start | bytes 983048 | tf_op jit(solution)/shard_map/ppermute | solution.py:233
  6.0 2.6 %collective-permute-start.1 = (f32[4,5,32,128]{3,2,1,0:T(8,128)}, f32[4,5,32,128]{3,2,1,0:T(8,128)S(1)}, u32[]{:S(2)}, u32[]{:S(2)}) collective-permute-start(f32[4,5,32,128]{3,2,1,0:T(8,128)} %get-tuple-element.63), channel_id=1, source_target_pairs={{0,16},{8,24},{16,0},{24,8},{1,17},{9,25},{17,1},{25,9},{2,18},{10... | collective-permute-start | bytes 983048 | tf_op jit(solution)/shard_map/ppermute | solution.py:233
  8.6 1.3 %collective-permute-start.2 = (f32[4,5,32,128]{3,2,1,0:T(8,128)S(1)}, f32[4,5,32,128]{3,2,1,0:T(8,128)S(1)}, u32[]{:S(2)}, u32[]{:S(2)}) collective-permute-start(f32[4,5,32,128]{3,2,1,0:T(8,128)S(1)} %get-tuple-element.64), channel_id=1, source_target_pairs={{0,24},{8,0},{16,8},{24,16},{1,25},{9,1},{17,9},{25,17},{2,26},{10... | collective-permute-start | bytes 983048 | tf_op jit(solution)/shard_map/ppermute | solution.py:233
  10.0 0.8 abs_reduce_fusion
  10.7 0.7 copy.28
  11.5 0.7 reduce
  12.3 0.8 copy.40
  13.3 1.0 %copy-done.4 = f32[5,128,128]{2,1,0:T(8,128)S(1)} copy-done((f32[5,128,128]{2,1,0:T(8,128)S(1)}, f32[5,128,128]{2,1,0:T(8,128)}, u32[]{:S(2)}) %copy-start.4) | copy-done | bytes 327704
  14.2 0.8 copy-done.6
  15.1 0.8 copy-done.7
  15.9 5.2 %prep.1 = (f32[4,5,128,128]{3,2,1,0:T(8,128)S(1)}, f32[4,5,32,128]{3,2,1,0:T(8,128)S(1)}, f32[4,5,32,128]{3,2,1,0:T(8,128)S(1)}, f32[128,128]{1,0:T(8,128)S(1)},...) custom-call(f32[4,5,125,1,128]{4,3,2,1,0:T(1,128)S(1)} %bitcast.8, ...), custom_call_target="tpu_custom_call" | custom-call | flops 1 | bytes 1 | tf_op jit(solution)/shard_map/prep/pallas_call | solution.py:146
  21.2 2.6 %collective-permute-start.7 = (f32[26,32,128]{2,1,0:T(8,128)S(1)}, f32[26,32,128]{2,1,0:T(8,128)S(1)}, u32[]{:S(2)}, u32[]{:S(2)}) collective-permute-start(f32[26,32,128]{2,1,0:T(8,128)S(1)} %get-tuple-element.76.refs_5_), channel_id=1, source_target_pairs={{0,7},{1,0},{2,1},{3,2},{4,3},{5,4},{6,5},{7,6},{8,15},{9,8},{10,9... | collective-permute-start | bytes 1277960 | tf_op jit(solution)/shard_map/ppermute | solution.py:236
  23.9 6.3 %collective-permute-done.1.refs_2_ = f32[4,5,32,128]{3,2,1,0:T(8,128)S(1)} collective-permute-done((f32[4,5,32,128]{3,2,1,0:T(8,128)}, f32[4,5,32,128]{3,2,1,0:T(8,128)S(1)}, u32[]{:S(2)}, u32[]{:S(2)}) %collective-permute-start.1) | collective-permute-done | bytes 327712 | tf_op jit(solution)/shard_map/ppermute | solution.py:233
  30.1 0.9 coupling.1
  31.0 7.5 %collective-permute-start.3 = (f32[2,5,32,128]{3,2,1,0:T(8,128)S(1)}, f32[2,5,32,128]{3,2,1,0:T(8,128)S(1)}, u32[]{:S(2)}, u32[]{:S(2)}) collective-permute-start(f32[2,5,32,128]{3,2,1,0:T(8,128)S(1)} %get-tuple-element.67), channel_id=1, source_target_pairs={{0,8},{8,16},{16,24},{24,0},{1,9},{9,17},{17,25},{25,1},{2,10},{10... | collective-permute-start | bytes 491528 | tf_op jit(solution)/shard_map/ppermute | solution.py:233
  38.6 1.6 %collective-permute-start.4 = (f32[2,5,32,128]{3,2,1,0:T(8,128)S(1)}, f32[2,5,32,128]{3,2,1,0:T(8,128)S(1)}, u32[]{:S(2)}, u32[]{:S(2)}) collective-permute-start(f32[2,5,32,128]{3,2,1,0:T(8,128)S(1)} %get-tuple-element.68), channel_id=1, source_target_pairs={{0,16},{8,24},{16,0},{24,8},{1,17},{9,25},{17,1},{25,9},{2,18},{10... | collective-permute-start | bytes 491528 | tf_op jit(solution)/shard_map/ppermute | solution.py:233
  40.2 0.9 collective-permute-start.5
  41.0 1.2 %collective-permute-start.8 = (f32[2,5,32,128]{3,2,1,0:T(8,128)S(1)}, f32[2,5,32,128]{3,2,1,0:T(8,128)S(1)}, u32[]{:S(2)}, u32[]{:S(2)}) collective-permute-start(f32[2,5,32,128]{3,2,1,0:T(8,128)S(1)} %get-tuple-element.89), channel_id=1, source_target_pairs={{0,8},{8,16},{16,24},{24,0},{1,9},{9,17},{17,25},{25,1},{2,10},{10... | collective-permute-start | bytes 491528 | tf_op jit(solution)/shard_map/ppermute | solution.py:233
  42.2 2.6 %collective-permute-start.9 = (f32[2,5,32,128]{3,2,1,0:T(8,128)S(1)}, f32[2,5,32,128]{3,2,1,0:T(8,128)S(1)}, u32[]{:S(2)}, u32[]{:S(2)}) collective-permute-start(f32[2,5,32,128]{3,2,1,0:T(8,128)S(1)} %get-tuple-element.90), channel_id=1, source_target_pairs={{0,24},{8,0},{16,8},{24,16},{1,25},{9,1},{17,9},{25,17},{2,26},{10... | collective-permute-start | bytes 491528 | tf_op jit(solution)/shard_map/ppermute | solution.py:233
  44.9 0.6 collective-permute-start.10
  45.4 2.7 %advance.3.z_ref.refs_4_ = f32[4,5,128,128]{3,2,1,0:T(8,128)S(1)} custom-call(f32[4,5,128,128]{3,2,1,0:T(8,128)S(1)} %get-tuple-element.70.refs_0_, f32[4,5,32,128]{3,2,1,0:T(8,128)S(1)} %get-tuple-element.71.refs_1_.lo_ref, f32[4,5,32,128]{3,2,1,0:T(8,128)S(1)} %get-tuple-element.72.refs_2_.hi_ref, f32[128,128]{1,0:T(8,128)S(1)} %get-tuple-element.73.refs_3_.m_ref.refs_9_, ...), custom_call_target="tpu_custom_call" | custom-call | flops 1 | bytes 1 | tf_op jit(solution)/shard_map/advance/pallas_call | solution.py:146
  48.2 0.3 faces.3
  48.5 3.8 %collective-permute-done.4.refs_2_ = f32[2,5,32,128]{3,2,1,0:T(8,128)S(1)} collective-permute-done((f32[2,5,32,128]{3,2,1,0:T(8,128)S(1)}, f32[2,5,32,128]{3,2,1,0:T(8,128)S(1)}, u32[]{:S(2)}, u32[]{:S(2)}) %collective-permute-start.4) | collective-permute-done | bytes 163872 | tf_op jit(solution)/shard_map/ppermute | solution.py:233
  52.3 2.0 %collective-permute-done.5.refs_3_ = f32[2,5,32,128]{3,2,1,0:T(8,128)S(1)} collective-permute-done((f32[2,5,32,128]{3,2,1,0:T(8,128)S(1)}, f32[2,5,32,128]{3,2,1,0:T(8,128)S(1)}, u32[]{:S(2)}, u32[]{:S(2)}) %collective-permute-start.5) | collective-permute-done | bytes 163872 | tf_op jit(solution)/shard_map/ppermute | solution.py:233
  54.3 0.6 first_pass.2
  54.9 1.5 %paired_first.1 = (f32[2,5,128,128]{3,2,1,0:T(8,128)S(1)}, f32[2,2,5,32,128]{4,3,2,1,0:T(8,128)S(1)}, f32[2,2,5,32,128]{4,3,2,1,0:T(8,128)S(1)}) custom-call(f32[2,5,128,128]{3,2,1,0:T(8,128)S(1)} %get-tuple-element.82.z_ref, f32[2,5,32,128]{3,2,1,0:T(8,128)S(1)} %get-tuple-element.83.lo_ref, f32[2,5,32,128]{3,2,1,0:T(8,128)S(1)} %get-tuple-element.84.hi_ref, ...), custom_call_target="tpu_custom_call" | custom-call | flops 1 | bytes 1 | tf_op jit(solution)/shard_map/paired_first/pallas_call | solution.py:146
  56.4 0.5 collective-permute-start.11
  56.9 0.4 collective-permute-done.9.refs_2_
  57.3 10.3 %collective-permute-done.10.refs_3_ = f32[2,5,32,128]{3,2,1,0:T(8,128)S(1)} collective-permute-done((f32[2,5,32,128]{3,2,1,0:T(8,128)S(1)}, f32[2,5,32,128]{3,2,1,0:T(8,128)S(1)}, u32[]{:S(2)}, u32[]{:S(2)}) %collective-permute-start.10) | collective-permute-done | bytes 163872 | tf_op jit(solution)/shard_map/ppermute | solution.py:233
  67.6 0.6 first_pass.3
  68.2 2.1 %collective-permute-start.14 = (f32[2,5,32,128]{3,2,1,0:T(8,128)S(1)}, f32[2,5,32,128]{3,2,1,0:T(8,128)S(1)}, u32[]{:S(2)}, u32[]{:S(2)}) collective-permute-start(f32[2,5,32,128]{3,2,1,0:T(8,128)S(1)} %get-tuple-element.93.refs_1_.lo_ref), channel_id=1, source_target_pairs={{0,7},{1,0},{2,1},{3,2},{4,3},{5,4},{6,5},{7,6},{8,15},{9,8},{10,9... | collective-permute-start | bytes 491528 | tf_op jit(solution)/shard_map/ppermute | solution.py:236
  70.3 1.4 %advance.4.z_ref.refs_0_ = f32[2,5,128,128]{3,2,1,0:T(8,128)S(1)} custom-call(f32[2,5,128,128]{3,2,1,0:T(8,128)S(1)} %get-tuple-element.92.refs_0_, f32[2,5,32,128]{3,2,1,0:T(8,128)S(1)} %get-tuple-element.93.refs_1_.lo_ref, f32[2,5,32,128]{3,2,1,0:T(8,128)S(1)} %get-tuple-element.94.refs_2_.hi_ref, f32[128,128]{1,0:T(8,128)S(1)} %get-tuple-element.73.refs_3_.m_ref.refs_9_, ...), custom_call_target="tpu_custom_call" | custom-call | flops 2000000000 | bytes 1 | tf_op jit(solution)/shard_map/advance/pallas_call | solution.py:146
  71.7 1.7 %paired_second.1 = (f32[2,5,128,128]{3,2,1,0:T(8,128)S(1)}, f32[2,5,32,128]{3,2,1,0:T(8,128)S(1)}, f32[2,5,32,128]{3,2,1,0:T(8,128)S(1)}) custom-call(f32[2,5,128,128]{3,2,1,0:T(8,128)S(1)} %get-tuple-element.87.refs_0_, f32[2,2,5,32,128]{4,3,2,1,0:T(8,128)S(1)} %get-tuple-element.97.refs_1_, f32[2,2,5,32,128]{4,3,2,1,0:T(8,128)S(1)} %get-tuple-element.98.refs_2_, ...), custom_call_target="tpu_custom_call" | custom-call | flops 1 | bytes 1 | tf_op jit(solution)/shard_map/paired_second/pallas_call | solution.py:146
  73.5 2.5 %collective-permute-done.13.below_ref = f32[2,5,32,128]{3,2,1,0:T(8,128)S(1)} collective-permute-done((f32[2,5,32,128]{3,2,1,0:T(8,128)S(1)}, f32[2,5,32,128]{3,2,1,0:T(8,128)S(1)}, u32[]{:S(2)}, u32[]{:S(2)}) %collective-permute-start.13) | collective-permute-done | bytes 163872 | tf_op jit(solution)/shard_map/ppermute | solution.py:236
  75.9 0.1 faces.4
  76.1 0.8 collective-permute-start.16
  76.9 1.4 %advance.5.z_ref.refs_0_ = f32[2,5,128,128]{3,2,1,0:T(8,128)S(1)} custom-call(f32[2,5,128,128]{3,2,1,0:T(8,128)S(1)} %advance.4.z_ref.refs_0_, f32[2,5,32,128]{3,2,1,0:T(8,128)S(1)} %get-tuple-element.102.refs_1_.lo_ref, f32[2,5,32,128]{3,2,1,0:T(8,128)S(1)} %get-tuple-element.103.refs_2_.hi_ref, f32[128,128]{1,0:T(8,128)S(1)} %get-tuple-element.73.refs_3_.m_ref.refs_9_, ...), custom_call_target="tpu_custom_call" | custom-call | flops 2000000000 | bytes 1 | tf_op jit(solution)/shard_map/advance/pallas_call | solution.py:146
  78.3 2.7 %collective-permute-start.18 = (f32[2,5,32,128]{3,2,1,0:T(8,128)S(1)}, f32[2,5,32,128]{3,2,1,0:T(8,128)S(1)}, u32[]{:S(2)}, u32[]{:S(2)}) collective-permute-start(f32[2,5,32,128]{3,2,1,0:T(8,128)S(1)} %get-tuple-element.107.refs_1_), channel_id=1, source_target_pairs={{0,7},{1,0},{2,1},{3,2},{4,3},{5,4},{6,5},{7,6},{8,15},{9,8},{10,9... | collective-permute-start | bytes 491528 | tf_op jit(solution)/shard_map/ppermute | solution.py:236
  81.0 1.6 %last_bulk.2 = (f32[2,5,128,128]{3,2,1,0:T(8,128)S(1)}, f32[4,5,125,1,128]{4,3,2,1,0:T(1,128)}) custom-call(f32[2,5,128,128]{3,2,1,0:T(8,128)S(1)} %get-tuple-element.100.refs_0_, f32[2,5,32,128]{3,2,1,0:T(8,128)S(1)} %get-tuple-element.107.refs_1_, f32[2,5,32,128]{3,2,1,0:T(8,128)S(1)} %get-tuple-element.108.refs_2_, ...), custom_call_target="tpu_custom_call" | custom-call | flops 1 | bytes 1 | tf_op jit(solution)/shard_map/last_bulk/pallas_call | solution.py:146
  82.6 0.2 faces.5
  82.8 2.7 %collective-permute-start.20 = (f32[2,5,32,128]{3,2,1,0:T(8,128)S(1)}, f32[2,5,32,128]{3,2,1,0:T(8,128)S(1)}, u32[]{:S(2)}, u32[]{:S(2)}) collective-permute-start(f32[2,5,32,128]{3,2,1,0:T(8,128)S(1)} %get-tuple-element.112.refs_1_), channel_id=1, source_target_pairs={{0,7},{1,0},{2,1},{3,2},{4,3},{5,4},{6,5},{7,6},{8,15},{9,8},{10,9... | collective-permute-start | bytes 491528 | tf_op jit(solution)/shard_map/ppermute | solution.py:236
  85.5 1.1 %collective-permute-done.17.refs_3_ = f32[2,5,32,128]{3,2,1,0:T(8,128)S(1)} collective-permute-done((f32[2,5,32,128]{3,2,1,0:T(8,128)S(1)}, f32[2,5,32,128]{3,2,1,0:T(8,128)S(1)}, u32[]{:S(2)}, u32[]{:S(2)}) %collective-permute-start.17) | collective-permute-done | bytes 163872 | tf_op jit(solution)/shard_map/ppermute | solution.py:236
  86.7 1.2 %last_faces.2.refs_8_ = f32[4,5,125,1,128]{4,3,2,1,0:T(1,128)} custom-call(f32[2,5,128,128]{3,2,1,0:T(8,128)S(1)} %get-tuple-element.114.refs_0_, f32[2,5,32,128]{3,2,1,0:T(8,128)S(1)} %get-tuple-element.107.refs_1_, f32[2,5,32,128]{3,2,1,0:T(8,128)S(1)} %get-tuple-element.108.refs_2_, f32[2,5,32,128]{3,2,1,0:T(8,128)S(1)} %collective-permute-done.17.refs_3_, ...), custom_call_target="tpu_custom_call" | custom-call | flops 1 | bytes 1 | tf_op jit(solution)/shard_map/last_faces/pallas_call | solution.py:146
  87.9 1.6 %last_bulk.3 = (f32[2,5,128,128]{3,2,1,0:T(8,128)S(1)}, f32[4,5,125,1,128]{4,3,2,1,0:T(1,128)}) custom-call(f32[2,5,128,128]{3,2,1,0:T(8,128)S(1)} %advance.5.z_ref.refs_0_, f32[2,5,32,128]{3,2,1,0:T(8,128)S(1)} %get-tuple-element.112.refs_1_, f32[2,5,32,128]{3,2,1,0:T(8,128)S(1)} %get-tuple-element.113.refs_2_, ...), custom_call_target="tpu_custom_call", output_to_operand_aliasing={{1}: (7, {})} | custom-call | flops 1 | bytes 1 | tf_op jit(solution)/shard_map/last_bulk/pallas_call | solution.py:146
  89.5 0.1 collective-permute-done.19.refs_3_
  89.6 1.2 %last_faces.3 = f32[4,5,125,1,128]{4,3,2,1,0:T(1,128)} custom-call(f32[2,5,128,128]{3,2,1,0:T(8,128)S(1)} %get-tuple-element.119.refs_0_, f32[2,5,32,128]{3,2,1,0:T(8,128)S(1)} %get-tuple-element.112.refs_1_, f32[2,5,32,128]{3,2,1,0:T(8,128)S(1)} %get-tuple-element.113.refs_2_, ...), custom_call_target="tpu_custom_call", output_to_operand_aliasing={{}: (8, {})} | custom-call | flops 1 | bytes 1 | tf_op jit(solution)/shard_map/last_faces/pallas_call | solution.py:146
  (41 shorter events, 0.5 us)
Async XLA Ops:
  0.6 1.3 %copy-start = (f32[4,5,1,125,128]{4,2,3,1,0:T(1,128)S(1)}, f32[4,5,1,125,128]{4,2,3,1,0:T(1,128)}, u32[]{:S(2)}) copy-start(f32[4,5,1,125,128]{4,2,3,1,0:T(1,128)} %param.13) | copy-start | bytes 3840004
  1.9 11.3 %copy-start.1 = (f32[4,5,1,125,128]{4,2,3,1,0:T(1,128)S(1)}, f32[4,5,1,125,128]{4,2,3,1,0:T(1,128)}, u32[]{:S(2)}) copy-start(f32[4,5,1,125,128]{4,2,3,1,0:T(1,128)} %param.13) | copy-start | bytes 3840004
  1.9 11.3 %copy-start.3 = (f32[5,128,128]{2,1,0:T(8,128)S(1)}, f32[5,128,128]{2,1,0:T(8,128)}, u32[]{:S(2)}) copy-start(f32[5,128,128]{2,1,0:T(8,128)} %constant.22.clone.damp_ref) | copy-start | bytes 983044
  1.9 11.3 %copy-start.5 = (s32[128,128]{1,0:T(8,128)S(1)}, s32[128,128]{1,0:T(8,128)}, u32[]{:S(2)}) copy-start(s32[128,128]{1,0:T(8,128)} %constant.24.clone.mix_ref) | copy-start | bytes 196612
  1.9 11.3 %copy-start.9 = (bf16[128,128]{1,0:T(8,128)(2,1)S(1)}, bf16[128,128]{1,0:T(8,128)(2,1)}, u32[]{:S(2)}) copy-start(bf16[128,128]{1,0:T(8,128)(2,1)} %constant.20.clone.order_ref) | copy-start | bytes 98308
  2.9 20.9 %collective-permute-start = (f32[4,5,32,128]{3,2,1,0:T(8,128)}, f32[4,5,32,128]{3,2,1,0:T(8,128)S(1)}, u32[]{:S(2)}, u32[]{:S(2)}) collective-permute-start(f32[4,5,32,128]{3,2,1,0:T(8,128)} %get-tuple-element.62), channel_id=1, source_target_pairs={{0,8},{8,16},{16,24},{24,0},{1,9},{9,17},{17,25},{25,1},{2,10},{10... | collective-permute-start | bytes 983048 | tf_op jit(solution)/shard_map/ppermute | solution.py:233
  6.0 24.1 %collective-permute-start.1 = (f32[4,5,32,128]{3,2,1,0:T(8,128)}, f32[4,5,32,128]{3,2,1,0:T(8,128)S(1)}, u32[]{:S(2)}, u32[]{:S(2)}) collective-permute-start(f32[4,5,32,128]{3,2,1,0:T(8,128)} %get-tuple-element.63), channel_id=1, source_target_pairs={{0,16},{8,24},{16,0},{24,8},{1,17},{9,25},{17,1},{25,9},{2,18},{10... | collective-permute-start | bytes 983048 | tf_op jit(solution)/shard_map/ppermute | solution.py:233
  8.6 21.5 %collective-permute-start.2 = (f32[4,5,32,128]{3,2,1,0:T(8,128)S(1)}, f32[4,5,32,128]{3,2,1,0:T(8,128)S(1)}, u32[]{:S(2)}, u32[]{:S(2)}) collective-permute-start(f32[4,5,32,128]{3,2,1,0:T(8,128)S(1)} %get-tuple-element.64), channel_id=1, source_target_pairs={{0,24},{8,0},{16,8},{24,16},{1,25},{9,1},{17,9},{25,17},{2,26},{10... | collective-permute-start | bytes 983048 | tf_op jit(solution)/shard_map/ppermute | solution.py:233
  13.3 1.0 %copy-start.4 = (f32[5,128,128]{2,1,0:T(8,128)S(1)}, f32[5,128,128]{2,1,0:T(8,128)}, u32[]{:S(2)}) copy-start(f32[5,128,128]{2,1,0:T(8,128)} %constant.21.clone.flux_ref) | copy-start | bytes 983044
  14.2 0.8 copy-start.6
  15.1 0.8 copy-start.7
  21.2 19.9 %collective-permute-start.6 = (f32[26,32,128]{2,1,0:T(8,128)S(1)}, f32[26,32,128]{2,1,0:T(8,128)S(1)}, u32[]{:S(2)}, u32[]{:S(2)}) collective-permute-start(f32[26,32,128]{2,1,0:T(8,128)S(1)} %get-tuple-element.75.refs_6_), channel_id=1, source_target_pairs={{0,1},{1,2},{2,3},{3,4},{4,5},{5,6},{6,7},{7,0},{8,9},{9,10},{10,1... | collective-permute-start | bytes 1277960 | tf_op jit(solution)/shard_map/ppermute | solution.py:236
  21.2 21.0 %collective-permute-start.7 = (f32[26,32,128]{2,1,0:T(8,128)S(1)}, f32[26,32,128]{2,1,0:T(8,128)S(1)}, u32[]{:S(2)}, u32[]{:S(2)}) collective-permute-start(f32[26,32,128]{2,1,0:T(8,128)S(1)} %get-tuple-element.76.refs_5_), channel_id=1, source_target_pairs={{0,7},{1,0},{2,1},{3,2},{4,3},{5,4},{6,5},{7,6},{8,15},{9,8},{10,9... | collective-permute-start | bytes 1277960 | tf_op jit(solution)/shard_map/ppermute | solution.py:236
  31.0 13.8 %collective-permute-start.3 = (f32[2,5,32,128]{3,2,1,0:T(8,128)S(1)}, f32[2,5,32,128]{3,2,1,0:T(8,128)S(1)}, u32[]{:S(2)}, u32[]{:S(2)}) collective-permute-start(f32[2,5,32,128]{3,2,1,0:T(8,128)S(1)} %get-tuple-element.67), channel_id=1, source_target_pairs={{0,8},{8,16},{16,24},{24,0},{1,9},{9,17},{17,25},{25,1},{2,10},{10... | collective-permute-start | bytes 491528 | tf_op jit(solution)/shard_map/ppermute | solution.py:233
  38.6 13.7 %collective-permute-start.4 = (f32[2,5,32,128]{3,2,1,0:T(8,128)S(1)}, f32[2,5,32,128]{3,2,1,0:T(8,128)S(1)}, u32[]{:S(2)}, u32[]{:S(2)}) collective-permute-start(f32[2,5,32,128]{3,2,1,0:T(8,128)S(1)} %get-tuple-element.68), channel_id=1, source_target_pairs={{0,16},{8,24},{16,0},{24,8},{1,17},{9,25},{17,1},{25,9},{2,18},{10... | collective-permute-start | bytes 491528 | tf_op jit(solution)/shard_map/ppermute | solution.py:233
  40.2 14.1 %collective-permute-start.5 = (f32[2,5,32,128]{3,2,1,0:T(8,128)S(1)}, f32[2,5,32,128]{3,2,1,0:T(8,128)S(1)}, u32[]{:S(2)}, u32[]{:S(2)}) collective-permute-start(f32[2,5,32,128]{3,2,1,0:T(8,128)S(1)} %get-tuple-element.69), channel_id=1, source_target_pairs={{0,24},{8,0},{16,8},{24,16},{1,25},{9,1},{17,9},{25,17},{2,26},{10... | collective-permute-start | bytes 491528 | tf_op jit(solution)/shard_map/ppermute | solution.py:233
  41.0 15.9 %collective-permute-start.8 = (f32[2,5,32,128]{3,2,1,0:T(8,128)S(1)}, f32[2,5,32,128]{3,2,1,0:T(8,128)S(1)}, u32[]{:S(2)}, u32[]{:S(2)}) collective-permute-start(f32[2,5,32,128]{3,2,1,0:T(8,128)S(1)} %get-tuple-element.89), channel_id=1, source_target_pairs={{0,8},{8,16},{16,24},{24,0},{1,9},{9,17},{17,25},{25,1},{2,10},{10... | collective-permute-start | bytes 491528 | tf_op jit(solution)/shard_map/ppermute | solution.py:233
  42.2 15.1 %collective-permute-start.9 = (f32[2,5,32,128]{3,2,1,0:T(8,128)S(1)}, f32[2,5,32,128]{3,2,1,0:T(8,128)S(1)}, u32[]{:S(2)}, u32[]{:S(2)}) collective-permute-start(f32[2,5,32,128]{3,2,1,0:T(8,128)S(1)} %get-tuple-element.90), channel_id=1, source_target_pairs={{0,24},{8,0},{16,8},{24,16},{1,25},{9,1},{17,9},{25,17},{2,26},{10... | collective-permute-start | bytes 491528 | tf_op jit(solution)/shard_map/ppermute | solution.py:233
  44.9 22.7 %collective-permute-start.10 = (f32[2,5,32,128]{3,2,1,0:T(8,128)S(1)}, f32[2,5,32,128]{3,2,1,0:T(8,128)S(1)}, u32[]{:S(2)}, u32[]{:S(2)}) collective-permute-start(f32[2,5,32,128]{3,2,1,0:T(8,128)S(1)} %get-tuple-element.91), channel_id=1, source_target_pairs={{0,16},{8,24},{16,0},{24,8},{1,17},{9,25},{17,1},{25,9},{2,18},{10... | collective-permute-start | bytes 491528 | tf_op jit(solution)/shard_map/ppermute | solution.py:233
  48.2 6.1 %copy-start.8 = (bf16[128,128]{1,0:T(8,128)(2,1)S(1)}, bf16[128,128]{1,0:T(8,128)(2,1)}, u32[]{:S(2)}) copy-start(bf16[128,128]{1,0:T(8,128)(2,1)} %constant.25.clone.refs_9_) | copy-start | bytes 98308
  56.4 15.4 %collective-permute-start.12 = (f32[2,2,5,32,128]{4,3,2,1,0:T(8,128)S(1)}, f32[2,2,5,32,128]{4,3,2,1,0:T(8,128)S(1)}, u32[]{:S(2)}, u32[]{:S(2)}) collective-permute-start(f32[2,2,5,32,128]{4,3,2,1,0:T(8,128)S(1)} %get-tuple-element.97.refs_1_), channel_id=1, source_target_pairs={{0,7},{1,0},{2,1},{3,2},{4,3},{5,4},{6,5},{7,6},{8,15},{9,8},{10,9... | collective-permute-start | bytes 983048 | tf_op jit(solution)/shard_map/ppermute | solution.py:236
  56.4 15.3 %collective-permute-start.11 = (f32[2,2,5,32,128]{4,3,2,1,0:T(8,128)S(1)}, f32[2,2,5,32,128]{4,3,2,1,0:T(8,128)S(1)}, u32[]{:S(2)}, u32[]{:S(2)}) collective-permute-start(f32[2,2,5,32,128]{4,3,2,1,0:T(8,128)S(1)} %get-tuple-element.98.refs_2_), channel_id=1, source_target_pairs={{0,1},{1,2},{2,3},{3,4},{4,5},{5,6},{6,7},{7,0},{8,9},{9,10},{10,1... | collective-permute-start | bytes 983048 | tf_op jit(solution)/shard_map/ppermute | solution.py:236
  68.2 7.8 %collective-permute-start.14 = (f32[2,5,32,128]{3,2,1,0:T(8,128)S(1)}, f32[2,5,32,128]{3,2,1,0:T(8,128)S(1)}, u32[]{:S(2)}, u32[]{:S(2)}) collective-permute-start(f32[2,5,32,128]{3,2,1,0:T(8,128)S(1)} %get-tuple-element.93.refs_1_.lo_ref), channel_id=1, source_target_pairs={{0,7},{1,0},{2,1},{3,2},{4,3},{5,4},{6,5},{7,6},{8,15},{9,8},{10,9... | collective-permute-start | bytes 491528 | tf_op jit(solution)/shard_map/ppermute | solution.py:236
  70.3 5.6 %collective-permute-start.13 = (f32[2,5,32,128]{3,2,1,0:T(8,128)S(1)}, f32[2,5,32,128]{3,2,1,0:T(8,128)S(1)}, u32[]{:S(2)}, u32[]{:S(2)}) collective-permute-start(f32[2,5,32,128]{3,2,1,0:T(8,128)S(1)} %get-tuple-element.94.refs_2_.hi_ref), channel_id=1, source_target_pairs={{0,1},{1,2},{2,3},{3,4},{4,5},{5,6},{6,7},{7,0},{8,9},{9,10},{10,1... | collective-permute-start | bytes 491528 | tf_op jit(solution)/shard_map/ppermute | solution.py:236
  76.1 6.5 %collective-permute-start.16 = (f32[2,5,32,128]{3,2,1,0:T(8,128)S(1)}, f32[2,5,32,128]{3,2,1,0:T(8,128)S(1)}, u32[]{:S(2)}, u32[]{:S(2)}) collective-permute-start(f32[2,5,32,128]{3,2,1,0:T(8,128)S(1)} %get-tuple-element.102.refs_1_.lo_ref), channel_id=1, source_target_pairs={{0,7},{1,0},{2,1},{3,2},{4,3},{5,4},{6,5},{7,6},{8,15},{9,8},{10,9... | collective-permute-start | bytes 491528 | tf_op jit(solution)/shard_map/ppermute | solution.py:236
  76.9 4.1 %copy-start.2 = (bf16[128,128]{1,0:T(8,128)(2,1)S(1)}, bf16[128,128]{1,0:T(8,128)(2,1)}, u32[]{:S(2)}) copy-start(bf16[128,128]{1,0:T(8,128)(2,1)} %constant.26.clone.refs_6_.refs_7_) | copy-start | bytes 98308
  76.9 5.7 %collective-permute-start.15 = (f32[2,5,32,128]{3,2,1,0:T(8,128)S(1)}, f32[2,5,32,128]{3,2,1,0:T(8,128)S(1)}, u32[]{:S(2)}, u32[]{:S(2)}) collective-permute-start(f32[2,5,32,128]{3,2,1,0:T(8,128)S(1)} %get-tuple-element.103.refs_2_.hi_ref), channel_id=1, source_target_pairs={{0,1},{1,2},{2,3},{3,4},{4,5},{5,6},{6,7},{7,0},{8,9},{9,10},{10,1... | collective-permute-start | bytes 491528 | tf_op jit(solution)/shard_map/ppermute | solution.py:236
  78.3 7.2 %collective-permute-start.18 = (f32[2,5,32,128]{3,2,1,0:T(8,128)S(1)}, f32[2,5,32,128]{3,2,1,0:T(8,128)S(1)}, u32[]{:S(2)}, u32[]{:S(2)}) collective-permute-start(f32[2,5,32,128]{3,2,1,0:T(8,128)S(1)} %get-tuple-element.107.refs_1_), channel_id=1, source_target_pairs={{0,7},{1,0},{2,1},{3,2},{4,3},{5,4},{6,5},{7,6},{8,15},{9,8},{10,9... | collective-permute-start | bytes 491528 | tf_op jit(solution)/shard_map/ppermute | solution.py:236
  81.0 5.6 %collective-permute-start.17 = (f32[2,5,32,128]{3,2,1,0:T(8,128)S(1)}, f32[2,5,32,128]{3,2,1,0:T(8,128)S(1)}, u32[]{:S(2)}, u32[]{:S(2)}) collective-permute-start(f32[2,5,32,128]{3,2,1,0:T(8,128)S(1)} %get-tuple-element.108.refs_2_), channel_id=1, source_target_pairs={{0,1},{1,2},{2,3},{3,4},{4,5},{5,6},{6,7},{7,0},{8,9},{9,10},{10,1... | collective-permute-start | bytes 491528 | tf_op jit(solution)/shard_map/ppermute | solution.py:236
  82.8 6.8 %collective-permute-start.19 = (f32[2,5,32,128]{3,2,1,0:T(8,128)S(1)}, f32[2,5,32,128]{3,2,1,0:T(8,128)S(1)}, u32[]{:S(2)}, u32[]{:S(2)}) collective-permute-start(f32[2,5,32,128]{3,2,1,0:T(8,128)S(1)} %get-tuple-element.113.refs_2_), channel_id=1, source_target_pairs={{0,1},{1,2},{2,3},{3,4},{4,5},{5,6},{6,7},{7,0},{8,9},{9,10},{10,1... | collective-permute-start | bytes 491528 | tf_op jit(solution)/shard_map/ppermute | solution.py:236
  82.8 6.8 %collective-permute-start.20 = (f32[2,5,32,128]{3,2,1,0:T(8,128)S(1)}, f32[2,5,32,128]{3,2,1,0:T(8,128)S(1)}, u32[]{:S(2)}, u32[]{:S(2)}) collective-permute-start(f32[2,5,32,128]{3,2,1,0:T(8,128)S(1)} %get-tuple-element.112.refs_1_), channel_id=1, source_target_pairs={{0,7},{1,0},{2,1},{3,2},{4,3},{5,4},{6,5},{7,6},{8,15},{9,8},{10,9... | collective-permute-start | bytes 491528 | tf_op jit(solution)/shard_map/ppermute | solution.py:236

commit v4 on v3

--- a/solution.py
+++ b/solution.py
@@ -127,6 +127,18 @@
         total = moved if total is None else total + moved
         values = values - part.astype(F32)
     return total
+
+
+SIDE = 25
+
+
+def put_rows(ref, at, v, value):
+    ref[(*at, pl.ds(SIDE * v, SIDE), slice(None))] = value[0:SIDE]
+
+
+def get_rows(ref, at, v):
+    rows = ref[(*at, pl.ds(SIDE * v, SIDE), slice(None))]
+    return jnp.concatenate([rows, jnp.zeros((FACE - SIDE, rows.shape[1]), F32)], axis=0)
 
 
 def mixed(weights, parts):
@@ -444,31 +456,34 @@
     def swap_faces(lo, hi):
         return along_elem(hi, 1), along_elem(lo, -1)
 
-    def close_faces(z, lo, hi, below, above, first, size):
-        def kernel(z_ref, lo_ref, hi_ref, below_ref, above_ref, mf_ref, pc_ref, nlo_ref, nhi_ref):
+    def close_faces(z, lo, hi, below, above, first, size, send=True):
+        def kernel(z_ref, lo_ref, hi_ref, below_ref, above_ref, mf_ref, pc_ref, nlo_ref, nhi_ref, *sends):
             for n in range(size):
 
                 def table_of(side, v, w, n=n):
                     return pc_ref[side, first + n, v, pl.ds(w, 1), :]
 
-                flat = len(below_ref.shape) == 3
-                below = [below_ref[n * nv + v] if flat else below_ref[n, v] for v in range(nv)]
-                above = [above_ref[n * nv + v] if flat else above_ref[n, v] for v in range(nv)]
+                flat = not sends
+                below = [below_ref[n * nv + v] if flat else get_rows(below_ref, (n,), v) for v in range(nv)]
+                above = [above_ref[n * nv + v] if flat else get_rows(above_ref, (n,), v) for v in range(nv)]
                 lows, highs = face_terms(n, lo_ref, hi_ref, below, above, table_of, mf_ref)
                 for v in range(nv):
-                    nlo_ref[n, v] = z_ref[n, v, 0:FACE, :] - lows[v]
-                    nhi_ref[n, v] = z_ref[n, v, HIGH:ROWS, :] - highs[v]
+                    new_lo, new_hi = z_ref[n, v, 0:FACE, :] - lows[v], z_ref[n, v, HIGH:ROWS, :] - highs[v]
+                    nlo_ref[n, v], nhi_ref[n, v] = new_lo, new_hi
+                    if sends:
+                        put_rows(sends[0], (n,), v, new_lo)
+                        put_rows(sends[1], (n,), v, new_hi)
 
         return call(
             kernel,
-            [shape(size, nv, FACE, lanes)] * 2,
+            [shape(size, nv, FACE, lanes)] * 2 + ([shape(size, ROWS, lanes)] * 2 if send else []),
             [z, lo, hi, below, above, metric_face, face_update],
             "v" * 7,
             name="faces",
         )
 
     def paired_first(z, lo, hi, spec, first):
-        def kernel(z_ref, lo_ref, hi_ref, m_ref, p_ref, lhs_ref, spec_ref, out_ref, down_ref, up_ref):
+        def kernel(z_ref, lo_ref, hi_ref, m_ref, p_ref, lhs_ref, spec_ref, out_ref, down_ref, up_ref, send_down_ref, send_up_ref):
             metric_value = m_ref[...]
             for at in range(0, per, 2):
                 ids = list(range(at, min(at + 2, per)))
@@ -482,10 +497,16 @@
                         out_ref[n, v] = value
                         down_ref[0, n, v], up_ref[0, n, v] = lo_ref[n, v], hi_ref[n, v]
                         down_ref[1, n, v], up_ref[1, n, v] = value[0:FACE], value[HIGH:ROWS]
+                        put_rows(send_down_ref, (0, n), v, lo_ref[n, v])
+                        put_rows(send_up_ref, (0, n), v, hi_ref[n, v])
+                        put_rows(send_down_ref, (1, n), v, value[0:FACE])
+                        put_rows(send_up_ref, (1, n), v, value[HIGH:ROWS])
 
         return call(
             kernel,
-            [shape(per, nv, ROWS, lanes)] + [shape(2, per, nv, FACE, lanes)] * 2,
+            [shape(per, nv, ROWS, lanes)]
+            + [shape(2, per, nv, FACE, lanes)] * 2
+            + [shape(2, per, ROWS, lanes)] * 2,
             [z, lo, hi, metric, precond, lhs, spec],
             "v" * 7,
             name="paired_first",
@@ -495,7 +516,7 @@
         def kernel(*refs):
             z_ref, down_ref, up_ref, below_ref, above_ref = refs[:5]
             low_ref, high_ref, below_table_ref, above_table_ref = refs[5:9]
-            m_ref, p_ref, lhs_ref, spec_ref, out_ref, out_lo_ref, out_hi_ref = refs[9:]
+            m_ref, p_ref, lhs_ref, spec_ref, out_ref, out_lo_ref, out_hi_ref, send_lo_ref, send_hi_ref = refs[9:]
             metric_value = m_ref[...]
             position = lax.rem(lax.axis_index("elem") + PR // 2, PR)
 
@@ -521,8 +542,8 @@
                 for n in ids:
                     lo, zlo = ([down_ref[k, n, v] for v in range(nv)] for k in range(2))
                     hi, zhi = ([up_ref[k, n, v] for v in range(nv)] for k in range(2))
-                    low_w, low_z = ([below_ref[k, n, v] for v in range(nv)] for k in range(2))
-                    high_w, high_z = ([above_ref[k, n, v] for v in range(nv)] for k in range(2))
+                    low_w, low_z = ([get_rows(below_ref, (k, n), v) for v in range(nv)] for k in range(2))
+                    high_w, high_z = ([get_rows(above_ref, (k, n), v) for v in range(nv)] for k in range(2))
                     new_lo = minus(zlo, update(low_ref, n, across(0, lo, low_w)))
                     new_hi = minus(zhi, update(high_ref, n, across(PR - 1, hi, high_w)))
                     next_low = across(0, new_lo, minus(low_z, update(below_table_ref, n, lo)))
@@ -544,10 +565,14 @@
                         out_ref[n, v] = value
                         out_lo_ref[n, v] = lo
                         out_hi_ref[n, v] = hi
+                        put_rows(send_lo_ref, (n,), v, lo)
+                        put_rows(send_hi_ref, (n,), v, hi)
 
         return call(
             kernel,
-            [shape(per, nv, ROWS, lanes)] + [shape(per, nv, FACE, lanes)] * 2,
+            [shape(per, nv, ROWS, lanes)]
+            + [shape(per, nv, FACE, lanes)] * 2
+            + [shape(per, ROWS, lanes)] * 2,
             [z, down, up, below, above, low_table, high_table, below_table, above_table]
             + [metric, precond, lhs, spec],
             "v" * 13,
@@ -577,7 +602,7 @@
 
     below0, above0 = swap_faces(low_table, high_table)
     t0 = advance(x0, lo0, hi0, None if own_circ else circ_extra(x0, lo0, hi0), 0, inst)
-    tlo, thi = close_faces(t0, lo0, hi0, below0, above0, 0, inst)
+    tlo, thi = close_faces(t0, lo0, hi0, below0, above0, 0, inst, send=False)
 
     half_pair = n_tm % 2 == 0
 
@@ -638,7 +663,7 @@
         def kernel(*refs):
             part_refs = [refs[distances.index(d)] for d in range(n_tm)]
             t_ref, tlo_ref, thi_ref, p_ref, col_ref, order_ref = refs[n_tm : n_tm + 6]
-            x_ref, lo_ref, hi_ref, s_ref, buf = refs[n_tm + 6 :]
+            x_ref, lo_ref, hi_ref, s_ref, send_lo_ref, send_hi_ref, buf = refs[n_tm + 6 :]
             me = lax.axis_index("tm")
             for d in range(n_tm):
                 start = pl.multiple_of(lax.rem(me - d + n_tm, n_tm) * block, block)
@@ -662,6 +687,8 @@
                     x_ref[n, v] = x
                     lo_ref[n, v] = x[0:FACE]
                     hi_ref[n, v] = x[HIGH:ROWS]
+                    put_rows(send_lo_ref, (n,), v, x[0:FACE])
+                    put_rows(send_hi_ref, (n,), v, x[HIGH:ROWS])
 
         return call(
             kernel,
@@ -670,6 +697,8 @@
                 shape(per, nv, FACE, lanes),
                 shape(per, nv, FACE, lanes),
                 shape(per, nv, ROWS, lanes),
+                shape(per, ROWS, lanes),
+                shape(per, ROWS, lanes),
             ],
             [parts[d] for d in distances] + [t0, tlo, thi, precond, inlet_cols, spectral_order.astype(ml_dtypes.bfloat16)],
             "v" * (n_tm + 6),
@@ -737,8 +766,8 @@
                 return fc_ref[side, v, pl.ds(w, 1), :]
 
             def work(n):
-                below = [below_ref[n, v] for v in range(nv)]
-                above = [above_ref[n, v] for v in range(nv)]
+                below = [get_rows(below_ref, (n,), v) for v in range(nv)]
+                above = [get_rows(above_ref, (n,), v) for v in range(nv)]
                 lows, highs = face_terms(n, lo_ref, hi_ref, below, above, table_of, mf_ref)
                 full = [
                     jnp.concatenate(
@@ -774,8 +803,8 @@
 
     def begin(g, swap):
         parts = spectral[g] if last is None else [after(spectral[g][0], last)] + spectral[g][1:]
-        z, lo, hi, spec = first_pass(parts, g * per, LONG if g == groups - 1 else 0)
-        chains[g] = (z, lo, hi, swap_faces(lo, hi) if swap else None, spec)
+        z, lo, hi, spec, send_lo, send_hi = first_pass(parts, g * per, LONG if g == groups - 1 else 0)
+        chains[g] = (z, lo, hi, swap_faces(send_lo, send_hi) if swap else None, spec)
         return lo
 
     def local_part(g, count_done):
@@ -795,30 +824,30 @@
         z, lo, hi, (below, above), spec = chains[g]
         z = after(z, last)
         if count_done < PASSES - 1:
-            lo, hi = close_faces(z, lo, hi, below, above, g * per, per)
-            chains[g] = (z, lo, hi, swap_faces(lo, hi), spec)
+            lo, hi, *sends = close_faces(z, lo, hi, below, above, g * per, per)
+            chains[g] = (z, lo, hi, swap_faces(*sends), spec)
             return lo
         final_residual = last_faces(z, lo, hi, below, above, g * per, final_residual)
         return final_residual
 
     def pair_begin(g):
         z, lo, hi, _, spec = chains[g]
-        z, down, up = paired_first(z, lo, hi, after(spec, last), g * per)
-        chains[g] = (z, down, up, (along_elem(up, 1), along_elem(down, -1)), spec)
+        z, down, up, send_down, send_up = paired_first(z, lo, hi, after(spec, last), g * per)
+        chains[g] = (z, down, up, swap_faces(send_down, send_up), spec)
         return z
 
     def pair_end(g, *before):
         z, down, up, (below, above), spec = chains[g]
-        z, lo, hi = paired_second(
+        z, lo, hi, *sends = paired_second(
             z, down, up, below, above, below0, above0, after(spec, last), g * per
         )
-        chains[g] = (z, lo, hi, None, spec)
+        chains[g] = (z, lo, hi, sends, spec)
         return z
 
     def pair_swap(g):
-        z, lo, hi, _, spec = chains[g]
-        lo, hi = lax.optimization_barrier((lo, hi, last))[:2]
-        chains[g] = (z, lo, hi, swap_faces(lo, hi), spec)
+        z, lo, hi, sends, spec = chains[g]
+        sends = lax.optimization_barrier((*sends, last))[:2]
+        chains[g] = (z, lo, hi, swap_faces(*sends), spec)
 
     end = groups - 1
     if own_circ and PASSES == 3:
@@ -830,16 +859,14 @@
         for g in range(end):
             last = pair_end(g)
         last = face_part(end, 0)
+        last = local_part(end, 1)
         for g in range(end):
             pair_swap(g)
-        last = local_part(end, 1)
-        for g in range(end):
+        last = face_part(end, 1)
+        for g in range(groups):
             last = local_part(g, 2)
-        last = face_part(end, 1)
-        for g in range(end):
+        for g in range(groups):
             last = face_part(g, 2)
-        last = local_part(end, 2)
-        last = face_part(end, 2)
     else:
         for g in range(groups):
             last = begin(g, True)

time: 91.9 us -> 90.3 us (0.983)
  waiting for transfers between devices: 26.4 us -> 19.9 us
  starting transfers between devices: 33 us -> 37.5 us
    ppermute x12, starting transfers between devices: 11.6 us -> 16.2 us  [along_elem(): lax.ppermute(x, 'elem', [(i, (i + d) % n_elem) for i in range(n_elem)])]
    ppermute x12, waiting for transfers between devices: 3.7 us -> 0.03 us  [along_elem(): lax.ppermute(x, 'elem', [(i, (i + d) % n_elem) for i in range(n_elem)])]
    ppermute x9, waiting for transfers between devices: 22.7 us -> 19.9 us  [along_tm(): return lax.ppermute(x, 'tm', [(i, (i + d) % n_tm) for i in range(n_tm)])]
  transfers between devices with their start and end apart: 21 -> 21, of which waited for: 8 -> 4; matrix products, arithmetic and copies ran while one was open for 4% -> 4% of each run, Pallas kernels for 23% -> 24%
where the time goes in v4:
time: 90.3 us; the launch traced here: 89.8 us
  starting transfers between devices  37.5 us (42%)
  Pallas kernels  24 us (27%)
  waiting for transfers between devices  19.9 us (22%)
  local copies, waits for them, and re-layouts  5.6 us (6%)
  other arithmetic  1.62 us (2%)
  between operations  1.09 us (1%)
    pallas_call x17, Pallas kernels, call(): pl.pallas_call(kernel, out_shape=outs, in_specs=[pl.BlockSpec(memory_spac...  24 us
    ppermute x9, starting transfers between devices, along_tm(): return lax.ppermute(x, 'tm', [(i, (i + d) % n_tm) for i in range(n_tm)])  21.4 us
    ppermute x9, waiting for transfers between devices, along_tm(): return lax.ppermute(x, 'tm', [(i, (i + d) % n_tm) for i in range(n_tm)])  19.9 us
    ppermute x12, starting transfers between devices, along_elem(): lax.ppermute(x, 'elem', [(i, (i + d) % n_elem) for i in range(n_elem)])  16.2 us
    unnamed x22, local copies, waits for them, and re-layouts  5.49 us
  transfers between devices with their start and end apart: 21, of which 4 were waited for; matrix products, arithmetic and copies ran while one was open for 4% of the time, Pallas kernels for 24%

profile of v4, /device:TPU:0, one launch (start us, length us, event | category | flops | bytes accessed | tf_op | source)
XLA Modules:
  0.0 89.8 jit_solution(16682224351236336489)
XLA Ops:
  0.6 1.3 %copy-done = f32[4,5,1,125,128]{4,2,3,1,0:T(1,128)S(1)} copy-done((f32[4,5,1,125,128]{4,2,3,1,0:T(1,128)S(1)}, f32[4,5,1,125,128]{4,2,3,1,0:T(1,128)}, u32[]{:S(2)}) %copy-start) | copy-done | bytes 1280024
  1.9 1.0 %pack.1 = (f32[4,5,32,128]{3,2,1,0:T(8,128)S(1)}, f32[4,5,32,128]{3,2,1,0:T(8,128)}, f32[4,5,32,128]{3,2,1,0:T(8,128)}, f32[4,5,32,128]{3,2,1,0:T(8,128)S(1)}) custom-call(f32[4,5,125,1,128]{4,3,2,1,0:T(1,128)S(1)} %bitcast.7), custom_call_target="tpu_custom_call" | custom-call | flops 1 | bytes 1 | tf_op jit(solution)/shard_map/pack/pallas_call | solution.py:158
  2.9 3.1 %collective-permute-start = (f32[4,5,32,128]{3,2,1,0:T(8,128)}, f32[4,5,32,128]{3,2,1,0:T(8,128)S(1)}, u32[]{:S(2)}, u32[]{:S(2)}) collective-permute-start(f32[4,5,32,128]{3,2,1,0:T(8,128)} %get-tuple-element.73), channel_id=1, source_target_pairs={{0,8},{8,16},{16,24},{24,0},{1,9},{9,17},{17,25},{25,1},{2,10},{10... | collective-permute-start | bytes 983048 | tf_op jit(solution)/shard_map/ppermute | solution.py:245
  6.0 2.6 %collective-permute-start.1 = (f32[4,5,32,128]{3,2,1,0:T(8,128)}, f32[4,5,32,128]{3,2,1,0:T(8,128)S(1)}, u32[]{:S(2)}, u32[]{:S(2)}) collective-permute-start(f32[4,5,32,128]{3,2,1,0:T(8,128)} %get-tuple-element.74), channel_id=1, source_target_pairs={{0,16},{8,24},{16,0},{24,8},{1,17},{9,25},{17,1},{25,9},{2,18},{10... | collective-permute-start | bytes 983048 | tf_op jit(solution)/shard_map/ppermute | solution.py:245
  8.6 1.3 %collective-permute-start.2 = (f32[4,5,32,128]{3,2,1,0:T(8,128)S(1)}, f32[4,5,32,128]{3,2,1,0:T(8,128)S(1)}, u32[]{:S(2)}, u32[]{:S(2)}) collective-permute-start(f32[4,5,32,128]{3,2,1,0:T(8,128)S(1)} %get-tuple-element.75), channel_id=1, source_target_pairs={{0,24},{8,0},{16,8},{24,16},{1,25},{9,1},{17,9},{25,17},{2,26},{10... | collective-permute-start | bytes 983048 | tf_op jit(solution)/shard_map/ppermute | solution.py:245
  10.0 0.8 abs_reduce_fusion
  10.7 0.7 copy.28
  11.4 0.1 reshape.27
  11.5 0.7 reduce
  12.3 0.8 copy.40
  13.2 0.1 pad_maximum_fusion.coef_ref
  13.3 1.0 %copy-done.4 = f32[5,128,128]{2,1,0:T(8,128)S(1)} copy-done((f32[5,128,128]{2,1,0:T(8,128)S(1)}, f32[5,128,128]{2,1,0:T(8,128)}, u32[]{:S(2)}) %copy-start.4) | copy-done | bytes 327704
  14.2 0.8 copy-done.6
  15.1 0.8 copy-done.7
  15.9 5.2 %prep.1 = (f32[4,5,128,128]{3,2,1,0:T(8,128)S(1)}, f32[4,5,32,128]{3,2,1,0:T(8,128)S(1)}, f32[4,5,32,128]{3,2,1,0:T(8,128)S(1)}, f32[128,128]{1,0:T(8,128)S(1)},...) custom-call(f32[4,5,125,1,128]{4,3,2,1,0:T(1,128)S(1)} %bitcast.8, ...), custom_call_target="tpu_custom_call" | custom-call | flops 1 | bytes 1 | tf_op jit(solution)/shard_map/prep/pallas_call | solution.py:158
  21.2 2.6 %collective-permute-start.7 = (f32[26,32,128]{2,1,0:T(8,128)S(1)}, f32[26,32,128]{2,1,0:T(8,128)S(1)}, u32[]{:S(2)}, u32[]{:S(2)}) collective-permute-start(f32[26,32,128]{2,1,0:T(8,128)S(1)} %get-tuple-element.87.refs_5_), channel_id=1, source_target_pairs={{0,7},{1,0},{2,1},{3,2},{4,3},{5,4},{6,5},{7,6},{8,15},{9,8},{10,9... | collective-permute-start | bytes 1277960 | tf_op jit(solution)/shard_map/ppermute | solution.py:248
  23.9 6.3 %collective-permute-done.1.refs_2_ = f32[4,5,32,128]{3,2,1,0:T(8,128)S(1)} collective-permute-done((f32[4,5,32,128]{3,2,1,0:T(8,128)}, f32[4,5,32,128]{3,2,1,0:T(8,128)S(1)}, u32[]{:S(2)}, u32[]{:S(2)}) %collective-permute-start.1) | collective-permute-done | bytes 327712 | tf_op jit(solution)/shard_map/ppermute | solution.py:245
  30.1 0.9 coupling.1
  31.0 7.5 %collective-permute-start.3 = (f32[2,5,32,128]{3,2,1,0:T(8,128)S(1)}, f32[2,5,32,128]{3,2,1,0:T(8,128)S(1)}, u32[]{:S(2)}, u32[]{:S(2)}) collective-permute-start(f32[2,5,32,128]{3,2,1,0:T(8,128)S(1)} %get-tuple-element.78), channel_id=1, source_target_pairs={{0,8},{8,16},{16,24},{24,0},{1,9},{9,17},{17,25},{25,1},{2,10},{10... | collective-permute-start | bytes 491528 | tf_op jit(solution)/shard_map/ppermute | solution.py:245
  38.6 1.6 %collective-permute-start.4 = (f32[2,5,32,128]{3,2,1,0:T(8,128)S(1)}, f32[2,5,32,128]{3,2,1,0:T(8,128)S(1)}, u32[]{:S(2)}, u32[]{:S(2)}) collective-permute-start(f32[2,5,32,128]{3,2,1,0:T(8,128)S(1)} %get-tuple-element.79), channel_id=1, source_target_pairs={{0,16},{8,24},{16,0},{24,8},{1,17},{9,25},{17,1},{25,9},{2,18},{10... | collective-permute-start | bytes 491528 | tf_op jit(solution)/shard_map/ppermute | solution.py:245
  40.2 0.9 collective-permute-start.5
  41.0 1.2 %collective-permute-start.8 = (f32[2,5,32,128]{3,2,1,0:T(8,128)S(1)}, f32[2,5,32,128]{3,2,1,0:T(8,128)S(1)}, u32[]{:S(2)}, u32[]{:S(2)}) collective-permute-start(f32[2,5,32,128]{3,2,1,0:T(8,128)S(1)} %get-tuple-element.100), channel_id=1, source_target_pairs={{0,8},{8,16},{16,24},{24,0},{1,9},{9,17},{17,25},{25,1},{2,10},{10... | collective-permute-start | bytes 491528 | tf_op jit(solution)/shard_map/ppermute | solution.py:245
  42.2 2.6 %collective-permute-start.9 = (f32[2,5,32,128]{3,2,1,0:T(8,128)S(1)}, f32[2,5,32,128]{3,2,1,0:T(8,128)S(1)}, u32[]{:S(2)}, u32[]{:S(2)}) collective-permute-start(f32[2,5,32,128]{3,2,1,0:T(8,128)S(1)} %get-tuple-element.101), channel_id=1, source_target_pairs={{0,24},{8,0},{16,8},{24,16},{1,25},{9,1},{17,9},{25,17},{2,26},{10... | collective-permute-start | bytes 491528 | tf_op jit(solution)/shard_map/ppermute | solution.py:245
  44.9 0.6 collective-permute-start.10
  45.4 2.7 %advance.3.z_ref.refs_4_ = f32[4,5,128,128]{3,2,1,0:T(8,128)S(1)} custom-call(f32[4,5,128,128]{3,2,1,0:T(8,128)S(1)} %get-tuple-element.81.refs_0_, f32[4,5,32,128]{3,2,1,0:T(8,128)S(1)} %get-tuple-element.82.refs_1_.lo_ref, f32[4,5,32,128]{3,2,1,0:T(8,128)S(1)} %get-tuple-element.83.refs_2_.hi_ref, f32[128,128]{1,0:T(8,128)S(1)} %get-tuple-element.84.refs_3_.m_ref.refs_9_, ...), custom_call_target="tpu_custom_call" | custom-call | flops 1 | bytes 1 | tf_op jit(solution)/shard_map/advance/pallas_call | solution.py:158
  48.1 0.3 faces.3
  48.4 3.9 %collective-permute-done.4.refs_2_ = f32[2,5,32,128]{3,2,1,0:T(8,128)S(1)} collective-permute-done((f32[2,5,32,128]{3,2,1,0:T(8,128)S(1)}, f32[2,5,32,128]{3,2,1,0:T(8,128)S(1)}, u32[]{:S(2)}, u32[]{:S(2)}) %collective-permute-start.4) | collective-permute-done | bytes 163872 | tf_op jit(solution)/shard_map/ppermute | solution.py:245
  52.3 2.0 %collective-permute-done.5.refs_3_ = f32[2,5,32,128]{3,2,1,0:T(8,128)S(1)} collective-permute-done((f32[2,5,32,128]{3,2,1,0:T(8,128)S(1)}, f32[2,5,32,128]{3,2,1,0:T(8,128)S(1)}, u32[]{:S(2)}, u32[]{:S(2)}) %collective-permute-start.5) | collective-permute-done | bytes 163872 | tf_op jit(solution)/shard_map/ppermute | solution.py:245
  54.3 1.3 %first_pass.2 = (f32[2,5,128,128]{3,2,1,0:T(8,128)S(1)}, f32[2,5,32,128]{3,2,1,0:T(8,128)S(1)}, f32[2,5,32,128]{3,2,1,0:T(8,128)S(1)}, f32[2,5,128,128]{3,2,1,0:...) custom-call(f32[2,5,32,128]{3,2,1,0:T(8,128)S(1)} %get-tuple-element.77.refs_0_, ...), custom_call_target="tpu_custom_call" | custom-call | flops 1 | bytes 1 | tf_op jit(solution)/shard_map/first_pass/pallas_call | solution.py:158
  55.5 1.5 %paired_first.1 = (f32[2,5,128,128]{3,2,1,0:T(8,128)S(1)}, f32[2,2,5,32,128]{4,3,2,1,0:T(8,128)S(1)}, f32[2,2,5,32,128]{4,3,2,1,0:T(8,128)S(1)}, f32[2,2,128,128]{3,2,1,0:T(8,128)S(1)}, f32[2,2,128,128]{3,2,1,0:T(8,128)S(1)}) custom-call(f32[2,5,128,128]{3,2,1,0:T(8,128)S(1)} %get-tuple-element.93.z_ref, f32[2,5,32,128]{3,2,1,0:T(8,128)S(1)} %get-tuple-element.94.lo_ref, ...), custom_call_target="tpu_custom_call" | custom-call | flops 1 | bytes 1 | tf_op jit(solution)/shard_map/paired_first/pallas_call | solution.py:158
  57.1 2.6 %collective-permute-start.12 = (f32[2,2,128,128]{3,2,1,0:T(8,128)S(1)}, f32[2,2,128,128]{3,2,1,0:T(8,128)S(1)}, u32[]{:S(2)}, u32[]{:S(2)}) collective-permute-start(f32[2,2,128,128]{3,2,1,0:T(8,128)S(1)} %get-tuple-element.111), channel_id=1, source_target_pairs={{0,7},{1,0},{2,1},{3,2},{4,3},{5,4},{6,5},{7,6},{8,15},{9,8},{10,9... | collective-permute-start | bytes 786440 | tf_op jit(solution)/shard_map/ppermute | solution.py:248
  59.8 7.8 %collective-permute-done.10.refs_3_ = f32[2,5,32,128]{3,2,1,0:T(8,128)S(1)} collective-permute-done((f32[2,5,32,128]{3,2,1,0:T(8,128)S(1)}, f32[2,5,32,128]{3,2,1,0:T(8,128)S(1)}, u32[]{:S(2)}, u32[]{:S(2)}) %collective-permute-start.10) | collective-permute-done | bytes 163872 | tf_op jit(solution)/shard_map/ppermute | solution.py:245
  67.6 0.6 first_pass.3
  68.2 0.1 collective-permute-start.13
  68.3 2.6 %collective-permute-start.14 = (f32[2,128,128]{2,1,0:T(8,128)S(1)}, f32[2,128,128]{2,1,0:T(8,128)S(1)}, u32[]{:S(2)}, u32[]{:S(2)}) collective-permute-start(f32[2,128,128]{2,1,0:T(8,128)S(1)} %get-tuple-element.116), channel_id=1, source_target_pairs={{0,7},{1,0},{2,1},{3,2},{4,3},{5,4},{6,5},{7,6},{8,15},{9,8},{10,9... | collective-permute-start | bytes 393224 | tf_op jit(solution)/shard_map/ppermute | solution.py:248
  70.9 1.4 %advance.4.z_ref.refs_0_ = f32[2,5,128,128]{3,2,1,0:T(8,128)S(1)} custom-call(f32[2,5,128,128]{3,2,1,0:T(8,128)S(1)} %get-tuple-element.103.refs_0_, f32[2,5,32,128]{3,2,1,0:T(8,128)S(1)} %get-tuple-element.104.refs_1_.lo_ref, f32[2,5,32,128]{3,2,1,0:T(8,128)S(1)} %get-tuple-element.105.refs_2_.hi_ref, ...), custom_call_target="tpu_custom_call" | custom-call | flops 2000000000 | bytes 1 | tf_op jit(solution)/shard_map/advance/pallas_call | solution.py:158
  72.3 1.7 %paired_second.1 = (f32[2,5,128,128]{3,2,1,0:T(8,128)S(1)}, f32[2,5,32,128]{3,2,1,0:T(8,128)S(1)}, f32[2,5,32,128]{3,2,1,0:T(8,128)S(1)}, f32[2,128,128]{2,1,0:T(8,128)S(1)}, f32[2,128,128]{2,1,0:T(8,128)S(1)}) custom-call(f32[2,5,128,128]{3,2,1,0:T(8,128)S(1)} %get-tuple-element.98.refs_0_, f32[2,2,5,32,128]{4,3,2,1,0:T(8,128)S(1)} %get-tuple-element.108.refs_1_, ...), custom_call_target="tpu_custom_call" | custom-call | flops 1 | bytes 1 | tf_op jit(solution)/shard_map/paired_second/pallas_call | solution.py:158
  74.1 0.2 faces.4
  74.3 0.8 collective-permute-start.15
  75.0 1.9 %collective-permute-start.16 = (f32[2,128,128]{2,1,0:T(8,128)S(1)}, f32[2,128,128]{2,1,0:T(8,128)S(1)}, u32[]{:S(2)}, u32[]{:S(2)}) collective-permute-start(f32[2,128,128]{2,1,0:T(8,128)S(1)} %get-tuple-element.122), channel_id=1, source_target_pairs={{0,7},{1,0},{2,1},{3,2},{4,3},{5,4},{6,5},{7,6},{8,15},{9,8},{10,9... | collective-permute-start | bytes 393224 | tf_op jit(solution)/shard_map/ppermute | solution.py:248
  77.0 1.4 %advance.5.z_ref.refs_0_ = f32[2,5,128,128]{3,2,1,0:T(8,128)S(1)} custom-call(f32[2,5,128,128]{3,2,1,0:T(8,128)S(1)} %advance.4.z_ref.refs_0_, f32[2,5,32,128]{3,2,1,0:T(8,128)S(1)} %get-tuple-element.117.refs_1_.lo_ref, f32[2,5,32,128]{3,2,1,0:T(8,128)S(1)} %get-tuple-element.118.refs_2_.hi_ref, f32[128,128]{1,0:T(8,128)S(1)} %get-tuple-element.84.refs_3_.m_ref.refs_9_, ...), custom_call_target="tpu_custom_call" | custom-call | flops 2000000000 | bytes 1 | tf_op jit(solution)/shard_map/advance/pallas_call | solution.py:158
  78.5 2.6 %collective-permute-start.18 = (f32[2,128,128]{2,1,0:T(8,128)S(1)}, f32[2,128,128]{2,1,0:T(8,128)S(1)}, u32[]{:S(2)}, u32[]{:S(2)}) collective-permute-start(f32[2,128,128]{2,1,0:T(8,128)S(1)} %get-tuple-element.137), channel_id=1, source_target_pairs={{0,7},{1,0},{2,1},{3,2},{4,3},{5,4},{6,5},{7,6},{8,15},{9,8},{10,9... | collective-permute-start | bytes 393224 | tf_op jit(solution)/shard_map/ppermute | solution.py:248
  81.1 0.2 faces.5
  81.3 2.6 %collective-permute-start.20 = (f32[2,128,128]{2,1,0:T(8,128)S(1)}, f32[2,128,128]{2,1,0:T(8,128)S(1)}, u32[]{:S(2)}, u32[]{:S(2)}) collective-permute-start(f32[2,128,128]{2,1,0:T(8,128)S(1)} %get-tuple-element.141), channel_id=1, source_target_pairs={{0,7},{1,0},{2,1},{3,2},{4,3},{5,4},{6,5},{7,6},{8,15},{9,8},{10,9... | collective-permute-start | bytes 393224 | tf_op jit(solution)/shard_map/ppermute | solution.py:248
  84.0 1.6 %last_bulk.2 = (f32[2,5,128,128]{3,2,1,0:T(8,128)S(1)}, f32[4,5,125,1,128]{4,3,2,1,0:T(1,128)}) custom-call(f32[2,5,128,128]{3,2,1,0:T(8,128)S(1)} %get-tuple-element.113.refs_0_, f32[2,5,32,128]{3,2,1,0:T(8,128)S(1)} %get-tuple-element.125.refs_1_, f32[2,5,32,128]{3,2,1,0:T(8,128)S(1)} %get-tuple-element.126.refs_2_, ...), custom_call_target="tpu_custom_call" | custom-call | flops 1 | bytes 1 | tf_op jit(solution)/shard_map/last_bulk/pallas_call | solution.py:158
  85.5 1.6 %last_bulk.3 = (f32[2,5,128,128]{3,2,1,0:T(8,128)S(1)}, f32[4,5,125,1,128]{4,3,2,1,0:T(1,128)}) custom-call(f32[2,5,128,128]{3,2,1,0:T(8,128)S(1)} %advance.5.z_ref.refs_0_, f32[2,5,32,128]{3,2,1,0:T(8,128)S(1)} %get-tuple-element.123.refs_1_, f32[2,5,32,128]{3,2,1,0:T(8,128)S(1)} %get-tuple-element.124.refs_2_, ...), custom_call_target="tpu_custom_call", output_to_operand_aliasing={{1}: (7, {})} | custom-call | flops 1 | bytes 1 | tf_op jit(solution)/shard_map/last_bulk/pallas_call | solution.py:158
  87.1 1.2 %last_faces.2.refs_8_ = f32[4,5,125,1,128]{4,3,2,1,0:T(1,128)} custom-call(f32[2,5,128,128]{3,2,1,0:T(8,128)S(1)} %get-tuple-element.133.refs_0_, f32[2,5,32,128]{3,2,1,0:T(8,128)S(1)} %get-tuple-element.125.refs_1_, f32[2,5,32,128]{3,2,1,0:T(8,128)S(1)} %get-tuple-element.126.refs_2_, f32[2,128,128]{2,1,0:T(8,128)S(1)} %collective-permute-done.17.refs_3_, ...), custom_call_target="tpu_custom_call" | custom-call | flops 1 | bytes 1 | tf_op jit(solution)/shard_map/last_faces/pallas_call | solution.py:158
  88.4 1.2 %last_faces.3 = f32[4,5,125,1,128]{4,3,2,1,0:T(1,128)} custom-call(f32[2,5,128,128]{3,2,1,0:T(8,128)S(1)} %get-tuple-element.139.refs_0_, f32[2,5,32,128]{3,2,1,0:T(8,128)S(1)} %get-tuple-element.123.refs_1_, f32[2,5,32,128]{3,2,1,0:T(8,128)S(1)} %get-tuple-element.124.refs_2_, ...), custom_call_target="tpu_custom_call", output_to_operand_aliasing={{}: (8, {})} | custom-call | flops 1 | bytes 1 | tf_op jit(solution)/shard_map/last_faces/pallas_call | solution.py:158
  (41 shorter events, 0.4 us)
Async XLA Ops:
  0.6 1.3 %copy-start = (f32[4,5,1,125,128]{4,2,3,1,0:T(1,128)S(1)}, f32[4,5,1,125,128]{4,2,3,1,0:T(1,128)}, u32[]{:S(2)}) copy-start(f32[4,5,1,125,128]{4,2,3,1,0:T(1,128)} %param.13) | copy-start | bytes 3840004
  1.9 11.3 %copy-start.1 = (f32[4,5,1,125,128]{4,2,3,1,0:T(1,128)S(1)}, f32[4,5,1,125,128]{4,2,3,1,0:T(1,128)}, u32[]{:S(2)}) copy-start(f32[4,5,1,125,128]{4,2,3,1,0:T(1,128)} %param.13) | copy-start | bytes 3840004
  1.9 11.3 %copy-start.3 = (f32[5,128,128]{2,1,0:T(8,128)S(1)}, f32[5,128,128]{2,1,0:T(8,128)}, u32[]{:S(2)}) copy-start(f32[5,128,128]{2,1,0:T(8,128)} %constant.22.clone.damp_ref) | copy-start | bytes 983044
  1.9 11.3 %copy-start.5 = (s32[128,128]{1,0:T(8,128)S(1)}, s32[128,128]{1,0:T(8,128)}, u32[]{:S(2)}) copy-start(s32[128,128]{1,0:T(8,128)} %constant.24.clone.mix_ref) | copy-start | bytes 196612
  1.9 11.3 %copy-start.9 = (bf16[128,128]{1,0:T(8,128)(2,1)S(1)}, bf16[128,128]{1,0:T(8,128)(2,1)}, u32[]{:S(2)}) copy-start(bf16[128,128]{1,0:T(8,128)(2,1)} %constant.20.clone.order_ref) | copy-start | bytes 98308
  2.9 20.9 %collective-permute-start = (f32[4,5,32,128]{3,2,1,0:T(8,128)}, f32[4,5,32,128]{3,2,1,0:T(8,128)S(1)}, u32[]{:S(2)}, u32[]{:S(2)}) collective-permute-start(f32[4,5,32,128]{3,2,1,0:T(8,128)} %get-tuple-element.73), channel_id=1, source_target_pairs={{0,8},{8,16},{16,24},{24,0},{1,9},{9,17},{17,25},{25,1},{2,10},{10... | collective-permute-start | bytes 983048 | tf_op jit(solution)/shard_map/ppermute | solution.py:245
  6.0 24.1 %collective-permute-start.1 = (f32[4,5,32,128]{3,2,1,0:T(8,128)}, f32[4,5,32,128]{3,2,1,0:T(8,128)S(1)}, u32[]{:S(2)}, u32[]{:S(2)}) collective-permute-start(f32[4,5,32,128]{3,2,1,0:T(8,128)} %get-tuple-element.74), channel_id=1, source_target_pairs={{0,16},{8,24},{16,0},{24,8},{1,17},{9,25},{17,1},{25,9},{2,18},{10... | collective-permute-start | bytes 983048 | tf_op jit(solution)/shard_map/ppermute | solution.py:245
  8.6 21.5 %collective-permute-start.2 = (f32[4,5,32,128]{3,2,1,0:T(8,128)S(1)}, f32[4,5,32,128]{3,2,1,0:T(8,128)S(1)}, u32[]{:S(2)}, u32[]{:S(2)}) collective-permute-start(f32[4,5,32,128]{3,2,1,0:T(8,128)S(1)} %get-tuple-element.75), channel_id=1, source_target_pairs={{0,24},{8,0},{16,8},{24,16},{1,25},{9,1},{17,9},{25,17},{2,26},{10... | collective-permute-start | bytes 983048 | tf_op jit(solution)/shard_map/ppermute | solution.py:245
  13.3 1.0 %copy-start.4 = (f32[5,128,128]{2,1,0:T(8,128)S(1)}, f32[5,128,128]{2,1,0:T(8,128)}, u32[]{:S(2)}) copy-start(f32[5,128,128]{2,1,0:T(8,128)} %constant.21.clone.flux_ref) | copy-start | bytes 983044
  14.2 0.8 copy-start.6
  15.1 0.8 copy-start.7
  21.2 19.9 %collective-permute-start.6 = (f32[26,32,128]{2,1,0:T(8,128)S(1)}, f32[26,32,128]{2,1,0:T(8,128)S(1)}, u32[]{:S(2)}, u32[]{:S(2)}) collective-permute-start(f32[26,32,128]{2,1,0:T(8,128)S(1)} %get-tuple-element.86.refs_6_), channel_id=1, source_target_pairs={{0,1},{1,2},{2,3},{3,4},{4,5},{5,6},{6,7},{7,0},{8,9},{9,10},{10,1... | collective-permute-start | bytes 1277960 | tf_op jit(solution)/shard_map/ppermute | solution.py:248
  21.2 21.0 %collective-permute-start.7 = (f32[26,32,128]{2,1,0:T(8,128)S(1)}, f32[26,32,128]{2,1,0:T(8,128)S(1)}, u32[]{:S(2)}, u32[]{:S(2)}) collective-permute-start(f32[26,32,128]{2,1,0:T(8,128)S(1)} %get-tuple-element.87.refs_5_), channel_id=1, source_target_pairs={{0,7},{1,0},{2,1},{3,2},{4,3},{5,4},{6,5},{7,6},{8,15},{9,8},{10,9... | collective-permute-start | bytes 1277960 | tf_op jit(solution)/shard_map/ppermute | solution.py:248
  31.0 13.8 %collective-permute-start.3 = (f32[2,5,32,128]{3,2,1,0:T(8,128)S(1)}, f32[2,5,32,128]{3,2,1,0:T(8,128)S(1)}, u32[]{:S(2)}, u32[]{:S(2)}) collective-permute-start(f32[2,5,32,128]{3,2,1,0:T(8,128)S(1)} %get-tuple-element.78), channel_id=1, source_target_pairs={{0,8},{8,16},{16,24},{24,0},{1,9},{9,17},{17,25},{25,1},{2,10},{10... | collective-permute-start | bytes 491528 | tf_op jit(solution)/shard_map/ppermute | solution.py:245
  38.6 13.7 %collective-permute-start.4 = (f32[2,5,32,128]{3,2,1,0:T(8,128)S(1)}, f32[2,5,32,128]{3,2,1,0:T(8,128)S(1)}, u32[]{:S(2)}, u32[]{:S(2)}) collective-permute-start(f32[2,5,32,128]{3,2,1,0:T(8,128)S(1)} %get-tuple-element.79), channel_id=1, source_target_pairs={{0,16},{8,24},{16,0},{24,8},{1,17},{9,25},{17,1},{25,9},{2,18},{10... | collective-permute-start | bytes 491528 | tf_op jit(solution)/shard_map/ppermute | solution.py:245
  40.2 14.1 %collective-permute-start.5 = (f32[2,5,32,128]{3,2,1,0:T(8,128)S(1)}, f32[2,5,32,128]{3,2,1,0:T(8,128)S(1)}, u32[]{:S(2)}, u32[]{:S(2)}) collective-permute-start(f32[2,5,32,128]{3,2,1,0:T(8,128)S(1)} %get-tuple-element.80), channel_id=1, source_target_pairs={{0,24},{8,0},{16,8},{24,16},{1,25},{9,1},{17,9},{25,17},{2,26},{10... | collective-permute-start | bytes 491528 | tf_op jit(solution)/shard_map/ppermute | solution.py:245
  41.0 18.7 %collective-permute-start.8 = (f32[2,5,32,128]{3,2,1,0:T(8,128)S(1)}, f32[2,5,32,128]{3,2,1,0:T(8,128)S(1)}, u32[]{:S(2)}, u32[]{:S(2)}) collective-permute-start(f32[2,5,32,128]{3,2,1,0:T(8,128)S(1)} %get-tuple-element.100), channel_id=1, source_target_pairs={{0,8},{8,16},{16,24},{24,0},{1,9},{9,17},{17,25},{25,1},{2,10},{10... | collective-permute-start | bytes 491528 | tf_op jit(solution)/shard_map/ppermute | solution.py:245
  42.2 17.5 %collective-permute-start.9 = (f32[2,5,32,128]{3,2,1,0:T(8,128)S(1)}, f32[2,5,32,128]{3,2,1,0:T(8,128)S(1)}, u32[]{:S(2)}, u32[]{:S(2)}) collective-permute-start(f32[2,5,32,128]{3,2,1,0:T(8,128)S(1)} %get-tuple-element.101), channel_id=1, source_target_pairs={{0,24},{8,0},{16,8},{24,16},{1,25},{9,1},{17,9},{25,17},{2,26},{10... | collective-permute-start | bytes 491528 | tf_op jit(solution)/shard_map/ppermute | solution.py:245
  44.9 22.7 %collective-permute-start.10 = (f32[2,5,32,128]{3,2,1,0:T(8,128)S(1)}, f32[2,5,32,128]{3,2,1,0:T(8,128)S(1)}, u32[]{:S(2)}, u32[]{:S(2)}) collective-permute-start(f32[2,5,32,128]{3,2,1,0:T(8,128)S(1)} %get-tuple-element.102), channel_id=1, source_target_pairs={{0,16},{8,24},{16,0},{24,8},{1,17},{9,25},{17,1},{25,9},{2,18},{10... | collective-permute-start | bytes 491528 | tf_op jit(solution)/shard_map/ppermute | solution.py:245
  48.1 6.1 %copy-start.8 = (bf16[128,128]{1,0:T(8,128)(2,1)S(1)}, bf16[128,128]{1,0:T(8,128)(2,1)}, u32[]{:S(2)}) copy-start(bf16[128,128]{1,0:T(8,128)(2,1)} %constant.25.clone.refs_9_) | copy-start | bytes 98308
  57.1 15.3 %collective-permute-start.11 = (f32[2,2,128,128]{3,2,1,0:T(8,128)S(1)}, f32[2,2,128,128]{3,2,1,0:T(8,128)S(1)}, u32[]{:S(2)}, u32[]{:S(2)}) collective-permute-start(f32[2,2,128,128]{3,2,1,0:T(8,128)S(1)} %get-tuple-element.110), channel_id=1, source_target_pairs={{0,1},{1,2},{2,3},{3,4},{4,5},{5,6},{6,7},{7,0},{8,9},{9,10},{10,1... | collective-permute-start | bytes 786440 | tf_op jit(solution)/shard_map/ppermute | solution.py:248
  57.1 15.2 %collective-permute-start.12 = (f32[2,2,128,128]{3,2,1,0:T(8,128)S(1)}, f32[2,2,128,128]{3,2,1,0:T(8,128)S(1)}, u32[]{:S(2)}, u32[]{:S(2)}) collective-permute-start(f32[2,2,128,128]{3,2,1,0:T(8,128)S(1)} %get-tuple-element.111), channel_id=1, source_target_pairs={{0,7},{1,0},{2,1},{3,2},{4,3},{5,4},{6,5},{7,6},{8,15},{9,8},{10,9... | collective-permute-start | bytes 786440 | tf_op jit(solution)/shard_map/ppermute | solution.py:248
  68.2 5.9 %collective-permute-start.13 = (f32[2,128,128]{2,1,0:T(8,128)S(1)}, f32[2,128,128]{2,1,0:T(8,128)S(1)}, u32[]{:S(2)}, u32[]{:S(2)}) collective-permute-start(f32[2,128,128]{2,1,0:T(8,128)S(1)} %get-tuple-element.115), channel_id=1, source_target_pairs={{0,1},{1,2},{2,3},{3,4},{4,5},{5,6},{6,7},{7,0},{8,9},{9,10},{10,1... | collective-permute-start | bytes 393224 | tf_op jit(solution)/shard_map/ppermute | solution.py:248
  68.3 5.8 %collective-permute-start.14 = (f32[2,128,128]{2,1,0:T(8,128)S(1)}, f32[2,128,128]{2,1,0:T(8,128)S(1)}, u32[]{:S(2)}, u32[]{:S(2)}) collective-permute-start(f32[2,128,128]{2,1,0:T(8,128)S(1)} %get-tuple-element.116), channel_id=1, source_target_pairs={{0,7},{1,0},{2,1},{3,2},{4,3},{5,4},{6,5},{7,6},{8,15},{9,8},{10,9... | collective-permute-start | bytes 393224 | tf_op jit(solution)/shard_map/ppermute | solution.py:248
  74.3 6.8 %collective-permute-start.15 = (f32[2,128,128]{2,1,0:T(8,128)S(1)}, f32[2,128,128]{2,1,0:T(8,128)S(1)}, u32[]{:S(2)}, u32[]{:S(2)}) collective-permute-start(f32[2,128,128]{2,1,0:T(8,128)S(1)} %get-tuple-element.121), channel_id=1, source_target_pairs={{0,1},{1,2},{2,3},{3,4},{4,5},{5,6},{6,7},{7,0},{8,9},{9,10},{10,1... | collective-permute-start | bytes 393224 | tf_op jit(solution)/shard_map/ppermute | solution.py:248
  75.0 6.1 %collective-permute-start.16 = (f32[2,128,128]{2,1,0:T(8,128)S(1)}, f32[2,128,128]{2,1,0:T(8,128)S(1)}, u32[]{:S(2)}, u32[]{:S(2)}) collective-permute-start(f32[2,128,128]{2,1,0:T(8,128)S(1)} %get-tuple-element.122), channel_id=1, source_target_pairs={{0,7},{1,0},{2,1},{3,2},{4,3},{5,4},{6,5},{7,6},{8,15},{9,8},{10,9... | collective-permute-start | bytes 393224 | tf_op jit(solution)/shard_map/ppermute | solution.py:248
  78.4 5.6 %copy-start.2 = (bf16[128,128]{1,0:T(8,128)(2,1)S(1)}, bf16[128,128]{1,0:T(8,128)(2,1)}, u32[]{:S(2)}) copy-start(bf16[128,128]{1,0:T(8,128)(2,1)} %constant.26.clone.refs_6_.refs_7_) | copy-start | bytes 98308
  78.4 8.7 %collective-permute-start.17 = (f32[2,128,128]{2,1,0:T(8,128)S(1)}, f32[2,128,128]{2,1,0:T(8,128)S(1)}, u32[]{:S(2)}, u32[]{:S(2)}) collective-permute-start(f32[2,128,128]{2,1,0:T(8,128)S(1)} %get-tuple-element.136), channel_id=1, source_target_pairs={{0,1},{1,2},{2,3},{3,4},{4,5},{5,6},{6,7},{7,0},{8,9},{9,10},{10,1... | collective-permute-start | bytes 393224 | tf_op jit(solution)/shard_map/ppermute | solution.py:248
  78.5 8.7 %collective-permute-start.18 = (f32[2,128,128]{2,1,0:T(8,128)S(1)}, f32[2,128,128]{2,1,0:T(8,128)S(1)}, u32[]{:S(2)}, u32[]{:S(2)}) collective-permute-start(f32[2,128,128]{2,1,0:T(8,128)S(1)} %get-tuple-element.137), channel_id=1, source_target_pairs={{0,7},{1,0},{2,1},{3,2},{4,3},{5,4},{6,5},{7,6},{8,15},{9,8},{10,9... | collective-permute-start | bytes 393224 | tf_op jit(solution)/shard_map/ppermute | solution.py:248
  81.3 7.1 %collective-permute-start.19 = (f32[2,128,128]{2,1,0:T(8,128)S(1)}, f32[2,128,128]{2,1,0:T(8,128)S(1)}, u32[]{:S(2)}, u32[]{:S(2)}) collective-permute-start(f32[2,128,128]{2,1,0:T(8,128)S(1)} %get-tuple-element.140), channel_id=1, source_target_pairs={{0,1},{1,2},{2,3},{3,4},{4,5},{5,6},{6,7},{7,0},{8,9},{9,10},{10,1... | collective-permute-start | bytes 393224 | tf_op jit(solution)/shard_map/ppermute | solution.py:248
  81.3 7.1 %collective-permute-start.20 = (f32[2,128,128]{2,1,0:T(8,128)S(1)}, f32[2,128,128]{2,1,0:T(8,128)S(1)}, u32[]{:S(2)}, u32[]{:S(2)}) collective-permute-start(f32[2,128,128]{2,1,0:T(8,128)S(1)} %get-tuple-element.141), channel_id=1, source_target_pairs={{0,7},{1,0},{2,1},{3,2},{4,3},{5,4},{6,5},{7,6},{8,15},{9,8},{10,9... | collective-permute-start | bytes 393224 | tf_op jit(solution)/shard_map/ppermute | solution.py:248

commit v5 on v4

--- a/solution.py
+++ b/solution.py
@@ -854,19 +854,18 @@
         for g in range(end):
             last = begin(g, False)
             last = pair_begin(g)
-        last = begin(end, True)
-        last = local_part(end, 0)
+        last = begin(end, False)
+        last = pair_begin(end)
         for g in range(end):
             last = pair_end(g)
-        last = face_part(end, 0)
-        last = local_part(end, 1)
+            pair_swap(g)
+            last = local_part(g, 2)
+        last = pair_end(end)
+        pair_swap(end)
         for g in range(end):
-            pair_swap(g)
-        last = face_part(end, 1)
-        for g in range(groups):
-            last = local_part(g, 2)
-        for g in range(groups):
             last = face_part(g, 2)
+        last = local_part(end, 2)
+        last = face_part(end, 2)
     else:
         for g in range(groups):
             last = begin(g, True)

time: 90.3 us -> 89.4 us (0.990)
  starting transfers between devices: 37.5 us -> 35.1 us
    ppermute x12 -> x10, starting transfers between devices: 16.2 us -> 13.7 us  [along_elem(): lax.ppermute(x, 'elem', [(i, (i + d) % n_elem) for i in range(n_elem)])]
    pallas_call x17 -> x15, Pallas kernels: 24 us -> 24.7 us  [call(): pl.pallas_call(kernel, out_shape=outs, in_specs=[pl.BlockSpec(memory_spac...]
  transfers between devices with their start and end apart: 21 -> 19, of which waited for: 4 -> 6; matrix products, arithmetic and copies ran while one was open for 4% -> 4% of each run, Pallas kernels for 24% -> 25%
where the time goes in v5:
time: 89.4 us; the launch traced here: 88.6 us
  starting transfers between devices  35.1 us (39%)
  Pallas kernels  24.7 us (28%)
  waiting for transfers between devices  20.6 us (23%)
  local copies, waits for them, and re-layouts  5.6 us (6%)
  other arithmetic  1.62 us (2%)
  between operations  1.01 us (1%)
    pallas_call x15, Pallas kernels, call(): pl.pallas_call(kernel, out_shape=outs, in_specs=[pl.BlockSpec(memory_spac...  24.7 us
    ppermute x9, starting transfers between devices, along_tm(): return lax.ppermute(x, 'tm', [(i, (i + d) % n_tm) for i in range(n_tm)])  21.4 us
    ppermute x9, waiting for transfers between devices, along_tm(): return lax.ppermute(x, 'tm', [(i, (i + d) % n_tm) for i in range(n_tm)])  19.9 us
    ppermute x10, starting transfers between devices, along_elem(): lax.ppermute(x, 'elem', [(i, (i + d) % n_elem) for i in range(n_elem)])  13.7 us
    unnamed x22, local copies, waits for them, and re-layouts  5.49 us
  transfers between devices with their start and end apart: 19, of which 6 were waited for; matrix products, arithmetic and copies ran while one was open for 4% of the time, Pallas kernels for 25%

profile of v5, /device:TPU:0, one launch (start us, length us, event | category | flops | bytes accessed | tf_op | source)
XLA Modules:
  0.0 88.6 jit_solution(18343972384405019842)
XLA Ops:
  0.6 1.3 %copy-done = f32[4,5,1,125,128]{4,2,3,1,0:T(1,128)S(1)} copy-done((f32[4,5,1,125,128]{4,2,3,1,0:T(1,128)S(1)}, f32[4,5,1,125,128]{4,2,3,1,0:T(1,128)}, u32[]{:S(2)}) %copy-start) | copy-done | bytes 1280024
  1.9 1.0 %pack.1 = (f32[4,5,32,128]{3,2,1,0:T(8,128)S(1)}, f32[4,5,32,128]{3,2,1,0:T(8,128)}, f32[4,5,32,128]{3,2,1,0:T(8,128)}, f32[4,5,32,128]{3,2,1,0:T(8,128)S(1)}) custom-call(f32[4,5,125,1,128]{4,3,2,1,0:T(1,128)S(1)} %bitcast.7), custom_call_target="tpu_custom_call" | custom-call | flops 1 | bytes 1 | tf_op jit(solution)/shard_map/pack/pallas_call | solution.py:158
  2.9 3.1 %collective-permute-start = (f32[4,5,32,128]{3,2,1,0:T(8,128)}, f32[4,5,32,128]{3,2,1,0:T(8,128)S(1)}, u32[]{:S(2)}, u32[]{:S(2)}) collective-permute-start(f32[4,5,32,128]{3,2,1,0:T(8,128)} %get-tuple-element.72), channel_id=1, source_target_pairs={{0,8},{8,16},{16,24},{24,0},{1,9},{9,17},{17,25},{25,1},{2,10},{10... | collective-permute-start | bytes 983048 | tf_op jit(solution)/shard_map/ppermute | solution.py:245
  6.0 2.6 %collective-permute-start.1 = (f32[4,5,32,128]{3,2,1,0:T(8,128)}, f32[4,5,32,128]{3,2,1,0:T(8,128)S(1)}, u32[]{:S(2)}, u32[]{:S(2)}) collective-permute-start(f32[4,5,32,128]{3,2,1,0:T(8,128)} %get-tuple-element.73), channel_id=1, source_target_pairs={{0,16},{8,24},{16,0},{24,8},{1,17},{9,25},{17,1},{25,9},{2,18},{10... | collective-permute-start | bytes 983048 | tf_op jit(solution)/shard_map/ppermute | solution.py:245
  8.6 1.3 %collective-permute-start.2 = (f32[4,5,32,128]{3,2,1,0:T(8,128)S(1)}, f32[4,5,32,128]{3,2,1,0:T(8,128)S(1)}, u32[]{:S(2)}, u32[]{:S(2)}) collective-permute-start(f32[4,5,32,128]{3,2,1,0:T(8,128)S(1)} %get-tuple-element.74), channel_id=1, source_target_pairs={{0,24},{8,0},{16,8},{24,16},{1,25},{9,1},{17,9},{25,17},{2,26},{10... | collective-permute-start | bytes 983048 | tf_op jit(solution)/shard_map/ppermute | solution.py:245
  10.0 0.8 abs_reduce_fusion
  10.7 0.7 copy.28
  11.4 0.1 reshape.27
  11.5 0.7 reduce
  12.3 0.8 copy.40
  13.2 0.1 pad_maximum_fusion.coef_ref
  13.3 1.0 %copy-done.4 = f32[5,128,128]{2,1,0:T(8,128)S(1)} copy-done((f32[5,128,128]{2,1,0:T(8,128)S(1)}, f32[5,128,128]{2,1,0:T(8,128)}, u32[]{:S(2)}) %copy-start.4) | copy-done | bytes 327704
  14.2 0.8 copy-done.6
  15.1 0.8 copy-done.7
  15.9 5.2 %prep.1 = (f32[4,5,128,128]{3,2,1,0:T(8,128)S(1)}, f32[4,5,32,128]{3,2,1,0:T(8,128)S(1)}, f32[4,5,32,128]{3,2,1,0:T(8,128)S(1)}, f32[128,128]{1,0:T(8,128)S(1)},...) custom-call(f32[4,5,125,1,128]{4,3,2,1,0:T(1,128)S(1)} %bitcast.8, ...), custom_call_target="tpu_custom_call" | custom-call | flops 1 | bytes 1 | tf_op jit(solution)/shard_map/prep/pallas_call | solution.py:158
  21.2 0.1 collective-permute-start.6
  21.2 2.6 %collective-permute-start.7 = (f32[26,32,128]{2,1,0:T(8,128)S(1)}, f32[26,32,128]{2,1,0:T(8,128)S(1)}, u32[]{:S(2)}, u32[]{:S(2)}) collective-permute-start(f32[26,32,128]{2,1,0:T(8,128)S(1)} %get-tuple-element.86.refs_5_), channel_id=1, source_target_pairs={{0,7},{1,0},{2,1},{3,2},{4,3},{5,4},{6,5},{7,6},{8,15},{9,8},{10,9... | collective-permute-start | bytes 1277960 | tf_op jit(solution)/shard_map/ppermute | solution.py:248
  23.9 6.3 %collective-permute-done.1.refs_2_ = f32[4,5,32,128]{3,2,1,0:T(8,128)S(1)} collective-permute-done((f32[4,5,32,128]{3,2,1,0:T(8,128)}, f32[4,5,32,128]{3,2,1,0:T(8,128)S(1)}, u32[]{:S(2)}, u32[]{:S(2)}) %collective-permute-start.1) | collective-permute-done | bytes 327712 | tf_op jit(solution)/shard_map/ppermute | solution.py:245
  30.1 0.9 coupling.1
  31.0 7.5 %collective-permute-start.3 = (f32[2,5,32,128]{3,2,1,0:T(8,128)S(1)}, f32[2,5,32,128]{3,2,1,0:T(8,128)S(1)}, u32[]{:S(2)}, u32[]{:S(2)}) collective-permute-start(f32[2,5,32,128]{3,2,1,0:T(8,128)S(1)} %get-tuple-element.77), channel_id=1, source_target_pairs={{0,8},{8,16},{16,24},{24,0},{1,9},{9,17},{17,25},{25,1},{2,10},{10... | collective-permute-start | bytes 491528 | tf_op jit(solution)/shard_map/ppermute | solution.py:245
  38.6 1.6 %collective-permute-start.4 = (f32[2,5,32,128]{3,2,1,0:T(8,128)S(1)}, f32[2,5,32,128]{3,2,1,0:T(8,128)S(1)}, u32[]{:S(2)}, u32[]{:S(2)}) collective-permute-start(f32[2,5,32,128]{3,2,1,0:T(8,128)S(1)} %get-tuple-element.78), channel_id=1, source_target_pairs={{0,16},{8,24},{16,0},{24,8},{1,17},{9,25},{17,1},{25,9},{2,18},{10... | collective-permute-start | bytes 491528 | tf_op jit(solution)/shard_map/ppermute | solution.py:245
  40.2 0.9 collective-permute-start.5
  41.0 1.2 %collective-permute-start.8 = (f32[2,5,32,128]{3,2,1,0:T(8,128)S(1)}, f32[2,5,32,128]{3,2,1,0:T(8,128)S(1)}, u32[]{:S(2)}, u32[]{:S(2)}) collective-permute-start(f32[2,5,32,128]{3,2,1,0:T(8,128)S(1)} %get-tuple-element.99), channel_id=1, source_target_pairs={{0,8},{8,16},{16,24},{24,0},{1,9},{9,17},{17,25},{25,1},{2,10},{10... | collective-permute-start | bytes 491528 | tf_op jit(solution)/shard_map/ppermute | solution.py:245
  42.2 2.6 %collective-permute-start.9 = (f32[2,5,32,128]{3,2,1,0:T(8,128)S(1)}, f32[2,5,32,128]{3,2,1,0:T(8,128)S(1)}, u32[]{:S(2)}, u32[]{:S(2)}) collective-permute-start(f32[2,5,32,128]{3,2,1,0:T(8,128)S(1)} %get-tuple-element.100), channel_id=1, source_target_pairs={{0,24},{8,0},{16,8},{24,16},{1,25},{9,1},{17,9},{25,17},{2,26},{10... | collective-permute-start | bytes 491528 | tf_op jit(solution)/shard_map/ppermute | solution.py:245
  44.9 0.6 collective-permute-start.10
  45.4 2.7 %advance.1.z_ref.refs_4_ = f32[4,5,128,128]{3,2,1,0:T(8,128)S(1)} custom-call(f32[4,5,128,128]{3,2,1,0:T(8,128)S(1)} %get-tuple-element.80.refs_0_, f32[4,5,32,128]{3,2,1,0:T(8,128)S(1)} %get-tuple-element.81.refs_1_.lo_ref, f32[4,5,32,128]{3,2,1,0:T(8,128)S(1)} %get-tuple-element.82.refs_2_.hi_ref, f32[128,128]{1,0:T(8,128)S(1)} %get-tuple-element.83.refs_3_.m_ref.refs_9_, ...), custom_call_target="tpu_custom_call" | custom-call | flops 1 | bytes 1 | tf_op jit(solution)/shard_map/advance/pallas_call | solution.py:158
  48.1 0.3 faces.1
  48.4 3.9 %collective-permute-done.4.refs_2_ = f32[2,5,32,128]{3,2,1,0:T(8,128)S(1)} collective-permute-done((f32[2,5,32,128]{3,2,1,0:T(8,128)S(1)}, f32[2,5,32,128]{3,2,1,0:T(8,128)S(1)}, u32[]{:S(2)}, u32[]{:S(2)}) %collective-permute-start.4) | collective-permute-done | bytes 163872 | tf_op jit(solution)/shard_map/ppermute | solution.py:245
  52.3 2.0 %collective-permute-done.5.refs_3_ = f32[2,5,32,128]{3,2,1,0:T(8,128)S(1)} collective-permute-done((f32[2,5,32,128]{3,2,1,0:T(8,128)S(1)}, f32[2,5,32,128]{3,2,1,0:T(8,128)S(1)}, u32[]{:S(2)}, u32[]{:S(2)}) %collective-permute-start.5) | collective-permute-done | bytes 163872 | tf_op jit(solution)/shard_map/ppermute | solution.py:245
  54.3 1.3 %first_pass.2 = (f32[2,5,128,128]{3,2,1,0:T(8,128)S(1)}, f32[2,5,32,128]{3,2,1,0:T(8,128)S(1)}, f32[2,5,32,128]{3,2,1,0:T(8,128)S(1)}, f32[2,5,128,128]{3,2,1,0:...) custom-call(f32[2,5,32,128]{3,2,1,0:T(8,128)S(1)} %get-tuple-element.76.refs_0_, ...), custom_call_target="tpu_custom_call" | custom-call | flops 1 | bytes 1 | tf_op jit(solution)/shard_map/first_pass/pallas_call | solution.py:158
  55.5 1.5 %paired_first.2 = (f32[2,5,128,128]{3,2,1,0:T(8,128)S(1)}, f32[2,2,5,32,128]{4,3,2,1,0:T(8,128)S(1)}, f32[2,2,5,32,128]{4,3,2,1,0:T(8,128)S(1)}, f32[2,2,128,128]{3,2,1,0:T(8,128)S(1)}, f32[2,2,128,128]{3,2,1,0:T(8,128)S(1)}) custom-call(f32[2,5,128,128]{3,2,1,0:T(8,128)S(1)} %get-tuple-element.92.z_ref, f32[2,5,32,128]{3,2,1,0:T(8,128)S(1)} %get-tuple-element.93.lo_ref, ...), custom_call_target="tpu_custom_call" | custom-call | flops 1 | bytes 1 | tf_op jit(solution)/shard_map/paired_first/pallas_call | solution.py:158
  57.1 2.6 %collective-permute-start.14 = (f32[2,2,128,128]{3,2,1,0:T(8,128)S(1)}, f32[2,2,128,128]{3,2,1,0:T(8,128)S(1)}, u32[]{:S(2)}, u32[]{:S(2)}) collective-permute-start(f32[2,2,128,128]{3,2,1,0:T(8,128)S(1)} %get-tuple-element.115), channel_id=1, source_target_pairs={{0,7},{1,0},{2,1},{3,2},{4,3},{5,4},{6,5},{7,6},{8,15},{9,8},{10,9... | collective-permute-start | bytes 786440 | tf_op jit(solution)/shard_map/ppermute | solution.py:248
  59.8 7.8 %collective-permute-done.10.refs_3_ = f32[2,5,32,128]{3,2,1,0:T(8,128)S(1)} collective-permute-done((f32[2,5,32,128]{3,2,1,0:T(8,128)S(1)}, f32[2,5,32,128]{3,2,1,0:T(8,128)S(1)}, u32[]{:S(2)}, u32[]{:S(2)}) %collective-permute-start.10) | collective-permute-done | bytes 163872 | tf_op jit(solution)/shard_map/ppermute | solution.py:245
  67.6 1.3 %first_pass.3 = (f32[2,5,128,128]{3,2,1,0:T(8,128)S(1)}, f32[2,5,32,128]{3,2,1,0:T(8,128)S(1)}, f32[2,5,32,128]{3,2,1,0:T(8,128)S(1)}, f32[2,5,128,128]{3,2,1,0:...) custom-call(f32[2,5,32,128]{3,2,1,0:T(8,128)S(1)} %get-tuple-element.98.refs_0_, ...), custom_call_target="tpu_custom_call" | custom-call | flops 2000000000 | bytes 1 | tf_op jit(solution)/shard_map/first_pass/pallas_call | solution.py:158
  68.8 1.5 %paired_first.3 = (f32[2,5,128,128]{3,2,1,0:T(8,128)S(1)}, f32[2,2,5,32,128]{4,3,2,1,0:T(8,128)S(1)}, f32[2,2,5,32,128]{4,3,2,1,0:T(8,128)S(1)}, f32[2,2,128,128]{3,2,1,0:T(8,128)S(1)}, f32[2,2,128,128]{3,2,1,0:T(8,128)S(1)}) custom-call(f32[2,5,128,128]{3,2,1,0:T(8,128)S(1)} %get-tuple-element.102.z_ref, f32[2,5,32,128]{3,2,1,0:T(8,128)S(1)} %get-tuple-element.103.lo_ref, ...), custom_call_target="tpu_custom_call" | custom-call | flops 1 | bytes 1 | tf_op jit(solution)/shard_map/paired_first/pallas_call | solution.py:158
  70.4 0.1 collective-permute-start.11
  70.4 2.6 %collective-permute-start.12 = (f32[2,2,128,128]{3,2,1,0:T(8,128)S(1)}, f32[2,2,128,128]{3,2,1,0:T(8,128)S(1)}, u32[]{:S(2)}, u32[]{:S(2)}) collective-permute-start(f32[2,2,128,128]{3,2,1,0:T(8,128)S(1)} %get-tuple-element.111), channel_id=1, source_target_pairs={{0,7},{1,0},{2,1},{3,2},{4,3},{5,4},{6,5},{7,6},{8,15},{9,8},{10,9... | collective-permute-start | bytes 786440 | tf_op jit(solution)/shard_map/ppermute | solution.py:248
  73.1 1.7 %paired_second.2 = (f32[2,5,128,128]{3,2,1,0:T(8,128)S(1)}, f32[2,5,32,128]{3,2,1,0:T(8,128)S(1)}, f32[2,5,32,128]{3,2,1,0:T(8,128)S(1)}, f32[2,128,128]{2,1,0:T(8,128)S(1)}, f32[2,128,128]{2,1,0:T(8,128)S(1)}) custom-call(f32[2,5,128,128]{3,2,1,0:T(8,128)S(1)} %get-tuple-element.97.refs_0_, f32[2,2,5,32,128]{4,3,2,1,0:T(8,128)S(1)} %get-tuple-element.112.refs_1_, ...), custom_call_target="tpu_custom_call" | custom-call | flops 1 | bytes 1 | tf_op jit(solution)/shard_map/paired_second/pallas_call | solution.py:158
  74.9 2.6 %collective-permute-start.16 = (f32[2,128,128]{2,1,0:T(8,128)S(1)}, f32[2,128,128]{2,1,0:T(8,128)S(1)}, u32[]{:S(2)}, u32[]{:S(2)}) collective-permute-start(f32[2,128,128]{2,1,0:T(8,128)S(1)} %get-tuple-element.130), channel_id=1, source_target_pairs={{0,7},{1,0},{2,1},{3,2},{4,3},{5,4},{6,5},{7,6},{8,15},{9,8},{10,9... | collective-permute-start | bytes 393224 | tf_op jit(solution)/shard_map/ppermute | solution.py:248
  77.5 1.6 %last_bulk.2 = (f32[2,5,128,128]{3,2,1,0:T(8,128)S(1)}, f32[4,5,125,1,128]{4,3,2,1,0:T(1,128)}) custom-call(f32[2,5,128,128]{3,2,1,0:T(8,128)S(1)} %get-tuple-element.117.refs_0_, f32[2,5,32,128]{3,2,1,0:T(8,128)S(1)} %get-tuple-element.118.refs_1_, f32[2,5,32,128]{3,2,1,0:T(8,128)S(1)} %get-tuple-element.119.refs_2_, ...), custom_call_target="tpu_custom_call" | custom-call | flops 1 | bytes 1 | tf_op jit(solution)/shard_map/last_bulk/pallas_call | solution.py:158
  79.1 0.3 collective-permute-done.12.refs_4_
  79.4 1.7 %paired_second.3 = (f32[2,5,128,128]{3,2,1,0:T(8,128)S(1)}, f32[2,5,32,128]{3,2,1,0:T(8,128)S(1)}, f32[2,5,32,128]{3,2,1,0:T(8,128)S(1)}, f32[2,128,128]{2,1,0:T(8,128)S(1)}, f32[2,128,128]{2,1,0:T(8,128)S(1)}) custom-call(f32[2,5,128,128]{3,2,1,0:T(8,128)S(1)} %get-tuple-element.107.refs_0_, f32[2,2,5,32,128]{4,3,2,1,0:T(8,128)S(1)} %get-tuple-element.108.refs_1_, ...), custom_call_target="tpu_custom_call" | custom-call | flops 1 | bytes 1 | tf_op jit(solution)/shard_map/paired_second/pallas_call | solution.py:158
  81.2 1.5 %collective-permute-start.17 = (f32[2,128,128]{2,1,0:T(8,128)S(1)}, f32[2,128,128]{2,1,0:T(8,128)S(1)}, u32[]{:S(2)}, u32[]{:S(2)}) collective-permute-start(f32[2,128,128]{2,1,0:T(8,128)S(1)} %get-tuple-element.138), channel_id=1, source_target_pairs={{0,1},{1,2},{2,3},{3,4},{4,5},{5,6},{6,7},{7,0},{8,9},{9,10},{10,1... | collective-permute-start | bytes 393224 | tf_op jit(solution)/shard_map/ppermute | solution.py:248
  82.7 1.4 %collective-permute-start.18 = (f32[2,128,128]{2,1,0:T(8,128)S(1)}, f32[2,128,128]{2,1,0:T(8,128)S(1)}, u32[]{:S(2)}, u32[]{:S(2)}) collective-permute-start(f32[2,128,128]{2,1,0:T(8,128)S(1)} %get-tuple-element.139), channel_id=1, source_target_pairs={{0,7},{1,0},{2,1},{3,2},{4,3},{5,4},{6,5},{7,6},{8,15},{9,8},{10,9... | collective-permute-start | bytes 393224 | tf_op jit(solution)/shard_map/ppermute | solution.py:248
  84.1 1.2 %last_faces.2.refs_8_ = f32[4,5,125,1,128]{4,3,2,1,0:T(1,128)} custom-call(f32[2,5,128,128]{3,2,1,0:T(8,128)S(1)} %get-tuple-element.126.refs_0_, f32[2,5,32,128]{3,2,1,0:T(8,128)S(1)} %get-tuple-element.118.refs_1_, f32[2,5,32,128]{3,2,1,0:T(8,128)S(1)} %get-tuple-element.119.refs_2_, f32[2,128,128]{2,1,0:T(8,128)S(1)} %collective-permute-done.15.refs_3_, ...), custom_call_target="tpu_custom_call" | custom-call | flops 1 | bytes 1 | tf_op jit(solution)/shard_map/last_faces/pallas_call | solution.py:158
  85.3 1.6 %last_bulk.3 = (f32[2,5,128,128]{3,2,1,0:T(8,128)S(1)}, f32[4,5,125,1,128]{4,3,2,1,0:T(1,128)}) custom-call(f32[2,5,128,128]{3,2,1,0:T(8,128)S(1)} %get-tuple-element.123.refs_0_, f32[2,5,32,128]{3,2,1,0:T(8,128)S(1)} %get-tuple-element.124.refs_1_, f32[2,5,32,128]{3,2,1,0:T(8,128)S(1)} %get-tuple-element.125.refs_2_, ...), custom_call_target="tpu_custom_call", output_to_operand_aliasing={{1}: (7, {})} | custom-call | flops 1 | bytes 1 | tf_op jit(solution)/shard_map/last_bulk/pallas_call | solution.py:158
  86.9 0.3 collective-permute-done.17.refs_3_
  87.2 1.3 %last_faces.3 = f32[4,5,125,1,128]{4,3,2,1,0:T(1,128)} custom-call(f32[2,5,128,128]{3,2,1,0:T(8,128)S(1)} %get-tuple-element.135.refs_0_, f32[2,5,32,128]{3,2,1,0:T(8,128)S(1)} %get-tuple-element.124.refs_1_, f32[2,5,32,128]{3,2,1,0:T(8,128)S(1)} %get-tuple-element.125.refs_2_, ...), custom_call_target="tpu_custom_call", output_to_operand_aliasing={{}: (8, {})} | custom-call | flops 1 | bytes 1 | tf_op jit(solution)/shard_map/last_faces/pallas_call | solution.py:158
  (35 shorter events, 0.2 us)
Async XLA Ops:
  0.6 1.3 %copy-start = (f32[4,5,1,125,128]{4,2,3,1,0:T(1,128)S(1)}, f32[4,5,1,125,128]{4,2,3,1,0:T(1,128)}, u32[]{:S(2)}) copy-start(f32[4,5,1,125,128]{4,2,3,1,0:T(1,128)} %param.13) | copy-start | bytes 3840004
  1.9 11.3 %copy-start.1 = (f32[4,5,1,125,128]{4,2,3,1,0:T(1,128)S(1)}, f32[4,5,1,125,128]{4,2,3,1,0:T(1,128)}, u32[]{:S(2)}) copy-start(f32[4,5,1,125,128]{4,2,3,1,0:T(1,128)} %param.13) | copy-start | bytes 3840004
  1.9 11.3 %copy-start.3 = (f32[5,128,128]{2,1,0:T(8,128)S(1)}, f32[5,128,128]{2,1,0:T(8,128)}, u32[]{:S(2)}) copy-start(f32[5,128,128]{2,1,0:T(8,128)} %constant.22.clone.damp_ref) | copy-start | bytes 983044
  1.9 11.3 %copy-start.5 = (s32[128,128]{1,0:T(8,128)S(1)}, s32[128,128]{1,0:T(8,128)}, u32[]{:S(2)}) copy-start(s32[128,128]{1,0:T(8,128)} %constant.24.clone.mix_ref) | copy-start | bytes 196612
  1.9 11.3 %copy-start.9 = (bf16[128,128]{1,0:T(8,128)(2,1)S(1)}, bf16[128,128]{1,0:T(8,128)(2,1)}, u32[]{:S(2)}) copy-start(bf16[128,128]{1,0:T(8,128)(2,1)} %constant.20.clone.order_ref) | copy-start | bytes 98308
  2.9 20.9 %collective-permute-start = (f32[4,5,32,128]{3,2,1,0:T(8,128)}, f32[4,5,32,128]{3,2,1,0:T(8,128)S(1)}, u32[]{:S(2)}, u32[]{:S(2)}) collective-permute-start(f32[4,5,32,128]{3,2,1,0:T(8,128)} %get-tuple-element.72), channel_id=1, source_target_pairs={{0,8},{8,16},{16,24},{24,0},{1,9},{9,17},{17,25},{25,1},{2,10},{10... | collective-permute-start | bytes 983048 | tf_op jit(solution)/shard_map/ppermute | solution.py:245
  6.0 24.1 %collective-permute-start.1 = (f32[4,5,32,128]{3,2,1,0:T(8,128)}, f32[4,5,32,128]{3,2,1,0:T(8,128)S(1)}, u32[]{:S(2)}, u32[]{:S(2)}) collective-permute-start(f32[4,5,32,128]{3,2,1,0:T(8,128)} %get-tuple-element.73), channel_id=1, source_target_pairs={{0,16},{8,24},{16,0},{24,8},{1,17},{9,25},{17,1},{25,9},{2,18},{10... | collective-permute-start | bytes 983048 | tf_op jit(solution)/shard_map/ppermute | solution.py:245
  8.6 21.5 %collective-permute-start.2 = (f32[4,5,32,128]{3,2,1,0:T(8,128)S(1)}, f32[4,5,32,128]{3,2,1,0:T(8,128)S(1)}, u32[]{:S(2)}, u32[]{:S(2)}) collective-permute-start(f32[4,5,32,128]{3,2,1,0:T(8,128)S(1)} %get-tuple-element.74), channel_id=1, source_target_pairs={{0,24},{8,0},{16,8},{24,16},{1,25},{9,1},{17,9},{25,17},{2,26},{10... | collective-permute-start | bytes 983048 | tf_op jit(solution)/shard_map/ppermute | solution.py:245
  13.3 1.0 %copy-start.4 = (f32[5,128,128]{2,1,0:T(8,128)S(1)}, f32[5,128,128]{2,1,0:T(8,128)}, u32[]{:S(2)}) copy-start(f32[5,128,128]{2,1,0:T(8,128)} %constant.21.clone.flux_ref) | copy-start | bytes 983044
  14.2 0.8 copy-start.6
  15.1 0.8 copy-start.7
  21.2 19.9 %collective-permute-start.6 = (f32[26,32,128]{2,1,0:T(8,128)S(1)}, f32[26,32,128]{2,1,0:T(8,128)S(1)}, u32[]{:S(2)}, u32[]{:S(2)}) collective-permute-start(f32[26,32,128]{2,1,0:T(8,128)S(1)} %get-tuple-element.85.refs_6_), channel_id=1, source_target_pairs={{0,1},{1,2},{2,3},{3,4},{4,5},{5,6},{6,7},{7,0},{8,9},{9,10},{10,1... | collective-permute-start | bytes 1277960 | tf_op jit(solution)/shard_map/ppermute | solution.py:248
  21.2 21.0 %collective-permute-start.7 = (f32[26,32,128]{2,1,0:T(8,128)S(1)}, f32[26,32,128]{2,1,0:T(8,128)S(1)}, u32[]{:S(2)}, u32[]{:S(2)}) collective-permute-start(f32[26,32,128]{2,1,0:T(8,128)S(1)} %get-tuple-element.86.refs_5_), channel_id=1, source_target_pairs={{0,7},{1,0},{2,1},{3,2},{4,3},{5,4},{6,5},{7,6},{8,15},{9,8},{10,9... | collective-permute-start | bytes 1277960 | tf_op jit(solution)/shard_map/ppermute | solution.py:248
  31.0 13.8 %collective-permute-start.3 = (f32[2,5,32,128]{3,2,1,0:T(8,128)S(1)}, f32[2,5,32,128]{3,2,1,0:T(8,128)S(1)}, u32[]{:S(2)}, u32[]{:S(2)}) collective-permute-start(f32[2,5,32,128]{3,2,1,0:T(8,128)S(1)} %get-tuple-element.77), channel_id=1, source_target_pairs={{0,8},{8,16},{16,24},{24,0},{1,9},{9,17},{17,25},{25,1},{2,10},{10... | collective-permute-start | bytes 491528 | tf_op jit(solution)/shard_map/ppermute | solution.py:245
  38.6 13.7 %collective-permute-start.4 = (f32[2,5,32,128]{3,2,1,0:T(8,128)S(1)}, f32[2,5,32,128]{3,2,1,0:T(8,128)S(1)}, u32[]{:S(2)}, u32[]{:S(2)}) collective-permute-start(f32[2,5,32,128]{3,2,1,0:T(8,128)S(1)} %get-tuple-element.78), channel_id=1, source_target_pairs={{0,16},{8,24},{16,0},{24,8},{1,17},{9,25},{17,1},{25,9},{2,18},{10... | collective-permute-start | bytes 491528 | tf_op jit(solution)/shard_map/ppermute | solution.py:245
  40.2 14.1 %collective-permute-start.5 = (f32[2,5,32,128]{3,2,1,0:T(8,128)S(1)}, f32[2,5,32,128]{3,2,1,0:T(8,128)S(1)}, u32[]{:S(2)}, u32[]{:S(2)}) collective-permute-start(f32[2,5,32,128]{3,2,1,0:T(8,128)S(1)} %get-tuple-element.79), channel_id=1, source_target_pairs={{0,24},{8,0},{16,8},{24,16},{1,25},{9,1},{17,9},{25,17},{2,26},{10... | collective-permute-start | bytes 491528 | tf_op jit(solution)/shard_map/ppermute | solution.py:245
  41.0 18.7 %collective-permute-start.8 = (f32[2,5,32,128]{3,2,1,0:T(8,128)S(1)}, f32[2,5,32,128]{3,2,1,0:T(8,128)S(1)}, u32[]{:S(2)}, u32[]{:S(2)}) collective-permute-start(f32[2,5,32,128]{3,2,1,0:T(8,128)S(1)} %get-tuple-element.99), channel_id=1, source_target_pairs={{0,8},{8,16},{16,24},{24,0},{1,9},{9,17},{17,25},{25,1},{2,10},{10... | collective-permute-start | bytes 491528 | tf_op jit(solution)/shard_map/ppermute | solution.py:245
  42.2 17.5 %collective-permute-start.9 = (f32[2,5,32,128]{3,2,1,0:T(8,128)S(1)}, f32[2,5,32,128]{3,2,1,0:T(8,128)S(1)}, u32[]{:S(2)}, u32[]{:S(2)}) collective-permute-start(f32[2,5,32,128]{3,2,1,0:T(8,128)S(1)} %get-tuple-element.100), channel_id=1, source_target_pairs={{0,24},{8,0},{16,8},{24,16},{1,25},{9,1},{17,9},{25,17},{2,26},{10... | collective-permute-start | bytes 491528 | tf_op jit(solution)/shard_map/ppermute | solution.py:245
  44.9 22.7 %collective-permute-start.10 = (f32[2,5,32,128]{3,2,1,0:T(8,128)S(1)}, f32[2,5,32,128]{3,2,1,0:T(8,128)S(1)}, u32[]{:S(2)}, u32[]{:S(2)}) collective-permute-start(f32[2,5,32,128]{3,2,1,0:T(8,128)S(1)} %get-tuple-element.101), channel_id=1, source_target_pairs={{0,16},{8,24},{16,0},{24,8},{1,17},{9,25},{17,1},{25,9},{2,18},{10... | collective-permute-start | bytes 491528 | tf_op jit(solution)/shard_map/ppermute | solution.py:245
  48.1 6.2 %copy-start.8 = (bf16[128,128]{1,0:T(8,128)(2,1)S(1)}, bf16[128,128]{1,0:T(8,128)(2,1)}, u32[]{:S(2)}) copy-start(bf16[128,128]{1,0:T(8,128)(2,1)} %constant.25.clone.refs_9_) | copy-start | bytes 98308
  57.0 16.0 %collective-permute-start.13 = (f32[2,2,128,128]{3,2,1,0:T(8,128)S(1)}, f32[2,2,128,128]{3,2,1,0:T(8,128)S(1)}, u32[]{:S(2)}, u32[]{:S(2)}) collective-permute-start(f32[2,2,128,128]{3,2,1,0:T(8,128)S(1)} %get-tuple-element.114), channel_id=1, source_target_pairs={{0,1},{1,2},{2,3},{3,4},{4,5},{5,6},{6,7},{7,0},{8,9},{9,10},{10,1... | collective-permute-start | bytes 786440 | tf_op jit(solution)/shard_map/ppermute | solution.py:248
  57.1 15.9 %collective-permute-start.14 = (f32[2,2,128,128]{3,2,1,0:T(8,128)S(1)}, f32[2,2,128,128]{3,2,1,0:T(8,128)S(1)}, u32[]{:S(2)}, u32[]{:S(2)}) collective-permute-start(f32[2,2,128,128]{3,2,1,0:T(8,128)S(1)} %get-tuple-element.115), channel_id=1, source_target_pairs={{0,7},{1,0},{2,1},{3,2},{4,3},{5,4},{6,5},{7,6},{8,15},{9,8},{10,9... | collective-permute-start | bytes 786440 | tf_op jit(solution)/shard_map/ppermute | solution.py:248
  70.4 8.7 %collective-permute-start.11 = (f32[2,2,128,128]{3,2,1,0:T(8,128)S(1)}, f32[2,2,128,128]{3,2,1,0:T(8,128)S(1)}, u32[]{:S(2)}, u32[]{:S(2)}) collective-permute-start(f32[2,2,128,128]{3,2,1,0:T(8,128)S(1)} %get-tuple-element.110), channel_id=1, source_target_pairs={{0,1},{1,2},{2,3},{3,4},{4,5},{5,6},{6,7},{7,0},{8,9},{9,10},{10,1... | collective-permute-start | bytes 786440 | tf_op jit(solution)/shard_map/ppermute | solution.py:248
  70.4 9.0 %collective-permute-start.12 = (f32[2,2,128,128]{3,2,1,0:T(8,128)S(1)}, f32[2,2,128,128]{3,2,1,0:T(8,128)S(1)}, u32[]{:S(2)}, u32[]{:S(2)}) collective-permute-start(f32[2,2,128,128]{3,2,1,0:T(8,128)S(1)} %get-tuple-element.111), channel_id=1, source_target_pairs={{0,7},{1,0},{2,1},{3,2},{4,3},{5,4},{6,5},{7,6},{8,15},{9,8},{10,9... | collective-permute-start | bytes 786440 | tf_op jit(solution)/shard_map/ppermute | solution.py:248
  73.1 4.4 %copy-start.2 = (bf16[128,128]{1,0:T(8,128)(2,1)S(1)}, bf16[128,128]{1,0:T(8,128)(2,1)}, u32[]{:S(2)}) copy-start(bf16[128,128]{1,0:T(8,128)(2,1)} %constant.26.clone.refs_6_.refs_7_) | copy-start | bytes 98308
  74.8 9.3 %collective-permute-start.15 = (f32[2,128,128]{2,1,0:T(8,128)S(1)}, f32[2,128,128]{2,1,0:T(8,128)S(1)}, u32[]{:S(2)}, u32[]{:S(2)}) collective-permute-start(f32[2,128,128]{2,1,0:T(8,128)S(1)} %get-tuple-element.129), channel_id=1, source_target_pairs={{0,1},{1,2},{2,3},{3,4},{4,5},{5,6},{6,7},{7,0},{8,9},{9,10},{10,1... | collective-permute-start | bytes 393224 | tf_op jit(solution)/shard_map/ppermute | solution.py:248
  74.9 9.2 %collective-permute-start.16 = (f32[2,128,128]{2,1,0:T(8,128)S(1)}, f32[2,128,128]{2,1,0:T(8,128)S(1)}, u32[]{:S(2)}, u32[]{:S(2)}) collective-permute-start(f32[2,128,128]{2,1,0:T(8,128)S(1)} %get-tuple-element.130), channel_id=1, source_target_pairs={{0,7},{1,0},{2,1},{3,2},{4,3},{5,4},{6,5},{7,6},{8,15},{9,8},{10,9... | collective-permute-start | bytes 393224 | tf_op jit(solution)/shard_map/ppermute | solution.py:248
  81.2 6.0 %collective-permute-start.17 = (f32[2,128,128]{2,1,0:T(8,128)S(1)}, f32[2,128,128]{2,1,0:T(8,128)S(1)}, u32[]{:S(2)}, u32[]{:S(2)}) collective-permute-start(f32[2,128,128]{2,1,0:T(8,128)S(1)} %get-tuple-element.138), channel_id=1, source_target_pairs={{0,1},{1,2},{2,3},{3,4},{4,5},{5,6},{6,7},{7,0},{8,9},{9,10},{10,1... | collective-permute-start | bytes 393224 | tf_op jit(solution)/shard_map/ppermute | solution.py:248
  82.7 4.5 %collective-permute-start.18 = (f32[2,128,128]{2,1,0:T(8,128)S(1)}, f32[2,128,128]{2,1,0:T(8,128)S(1)}, u32[]{:S(2)}, u32[]{:S(2)}) collective-permute-start(f32[2,128,128]{2,1,0:T(8,128)S(1)} %get-tuple-element.139), channel_id=1, source_target_pairs={{0,7},{1,0},{2,1},{3,2},{4,3},{5,4},{6,5},{7,6},{8,15},{9,8},{10,9... | collective-permute-start | bytes 393224 | tf_op jit(solution)/shard_map/ppermute | solution.py:248

commit v6 on v5

--- a/solution.py
+++ b/solution.py
@@ -655,7 +655,7 @@
         for e in sorted(range(1, n_tm), key=lambda e: abs(2 * e - n_tm)):
             spectral[g][e] = along_tm(coupled[e * groups + g], e)
 
-    def first_pass(parts, first, flops=0):
+    def first_pass(parts, first, flops=0, send=True):
         distances = list(range(n_tm))
         if first > 0:
             distances.sort(key=lambda d: min(d, n_tm - d))
@@ -663,7 +663,7 @@
         def kernel(*refs):
             part_refs = [refs[distances.index(d)] for d in range(n_tm)]
             t_ref, tlo_ref, thi_ref, p_ref, col_ref, order_ref = refs[n_tm : n_tm + 6]
-            x_ref, lo_ref, hi_ref, s_ref, send_lo_ref, send_hi_ref, buf = refs[n_tm + 6 :]
+            x_ref, lo_ref, hi_ref, s_ref, *sends, buf = refs[n_tm + 6 :]
             me = lax.axis_index("tm")
             for d in range(n_tm):
                 start = pl.multiple_of(lax.rem(me - d + n_tm, n_tm) * block, block)
@@ -687,8 +687,9 @@
                     x_ref[n, v] = x
                     lo_ref[n, v] = x[0:FACE]
                     hi_ref[n, v] = x[HIGH:ROWS]
-                    put_rows(send_lo_ref, (n,), v, x[0:FACE])
-                    put_rows(send_hi_ref, (n,), v, x[HIGH:ROWS])
+                    if sends:
+                        put_rows(sends[0], (n,), v, x[0:FACE])
+                        put_rows(sends[1], (n,), v, x[HIGH:ROWS])
 
         return call(
             kernel,
@@ -697,9 +698,8 @@
                 shape(per, nv, FACE, lanes),
                 shape(per, nv, FACE, lanes),
                 shape(per, nv, ROWS, lanes),
-                shape(per, ROWS, lanes),
-                shape(per, ROWS, lanes),
-            ],
+            ]
+            + ([shape(per, ROWS, lanes)] * 2 if send else []),
             [parts[d] for d in distances] + [t0, tlo, thi, precond, inlet_cols, spectral_order.astype(ml_dtypes.bfloat16)],
             "v" * (n_tm + 6),
             scratch=[pltpu.VMEM((per, nv, ROWS, lanes), F32)],
@@ -803,8 +803,8 @@
 
     def begin(g, swap):
         parts = spectral[g] if last is None else [after(spectral[g][0], last)] + spectral[g][1:]
-        z, lo, hi, spec, send_lo, send_hi = first_pass(parts, g * per, LONG if g == groups - 1 else 0)
-        chains[g] = (z, lo, hi, swap_faces(send_lo, send_hi) if swap else None, spec)
+        z, lo, hi, spec, *sends = first_pass(parts, g * per, LONG if g == groups - 1 else 0, swap)
+        chains[g] = (z, lo, hi, swap_faces(*sends) if swap else None, spec)
         return lo
 
     def local_part(g, count_done):

time: 89.4 us -> 88.7 us (level)
  Pallas kernels: 24.7 us -> 23.4 us
    pallas_call x15, Pallas kernels: 24.7 us -> 23.4 us  [call(): pl.pallas_call(kernel, out_shape=outs, in_specs=[pl.BlockSpec(memory_spac...]
  transfers between devices with their start and end apart: 19 -> 19, of which waited for: 6 -> 6; matrix products, arithmetic and copies ran while one was open for 4% -> 4% of each run, Pallas kernels for 25% -> 24%
where the time goes in v6:
time: 88.7 us; the launch traced here: 87.9 us
  starting transfers between devices  35.1 us (40%)
  Pallas kernels  23.4 us (26%)
  waiting for transfers between devices  21.3 us (24%)
  local copies, waits for them, and re-layouts  5.6 us (6%)
  other arithmetic  1.62 us (2%)
  between operations  1.02 us (1%)
    pallas_call x15, Pallas kernels, call(): pl.pallas_call(kernel, out_shape=outs, in_specs=[pl.BlockSpec(memory_spac...  23.4 us
    ppermute x9, starting transfers between devices, along_tm(): return lax.ppermute(x, 'tm', [(i, (i + d) % n_tm) for i in range(n_tm)])  21.4 us
    ppermute x9, waiting for transfers between devices, along_tm(): return lax.ppermute(x, 'tm', [(i, (i + d) % n_tm) for i in range(n_tm)])  20.6 us
    ppermute x10, starting transfers between devices, along_elem(): lax.ppermute(x, 'elem', [(i, (i + d) % n_elem) for i in range(n_elem)])  13.7 us
    unnamed x22, local copies, waits for them, and re-layouts  5.49 us
  transfers between devices with their start and end apart: 19, of which 6 were waited for; matrix products, arithmetic and copies ran while one was open for 4% of the time, Pallas kernels for 24%

profile of v6, /device:TPU:0, one launch (start us, length us, event | category | flops | bytes accessed | tf_op | source)
XLA Modules:
  0.0 87.9 jit_solution(2956478565294970042)
XLA Ops:
  0.6 1.3 %copy-done = f32[4,5,1,125,128]{4,2,3,1,0:T(1,128)S(1)} copy-done((f32[4,5,1,125,128]{4,2,3,1,0:T(1,128)S(1)}, f32[4,5,1,125,128]{4,2,3,1,0:T(1,128)}, u32[]{:S(2)}) %copy-start) | copy-done | bytes 1280024
  1.9 1.0 %pack.1 = (f32[4,5,32,128]{3,2,1,0:T(8,128)S(1)}, f32[4,5,32,128]{3,2,1,0:T(8,128)}, f32[4,5,32,128]{3,2,1,0:T(8,128)}, f32[4,5,32,128]{3,2,1,0:T(8,128)S(1)}) custom-call(f32[4,5,125,1,128]{4,3,2,1,0:T(1,128)S(1)} %bitcast.7), custom_call_target="tpu_custom_call" | custom-call | flops 1 | bytes 1 | tf_op jit(solution)/shard_map/pack/pallas_call | solution.py:158
  2.9 3.1 %collective-permute-start = (f32[4,5,32,128]{3,2,1,0:T(8,128)}, f32[4,5,32,128]{3,2,1,0:T(8,128)S(1)}, u32[]{:S(2)}, u32[]{:S(2)}) collective-permute-start(f32[4,5,32,128]{3,2,1,0:T(8,128)} %get-tuple-element.72), channel_id=1, source_target_pairs={{0,8},{8,16},{16,24},{24,0},{1,9},{9,17},{17,25},{25,1},{2,10},{10... | collective-permute-start | bytes 983048 | tf_op jit(solution)/shard_map/ppermute | solution.py:245
  6.0 2.6 %collective-permute-start.1 = (f32[4,5,32,128]{3,2,1,0:T(8,128)}, f32[4,5,32,128]{3,2,1,0:T(8,128)S(1)}, u32[]{:S(2)}, u32[]{:S(2)}) collective-permute-start(f32[4,5,32,128]{3,2,1,0:T(8,128)} %get-tuple-element.73), channel_id=1, source_target_pairs={{0,16},{8,24},{16,0},{24,8},{1,17},{9,25},{17,1},{25,9},{2,18},{10... | collective-permute-start | bytes 983048 | tf_op jit(solution)/shard_map/ppermute | solution.py:245
  8.6 1.3 %collective-permute-start.2 = (f32[4,5,32,128]{3,2,1,0:T(8,128)S(1)}, f32[4,5,32,128]{3,2,1,0:T(8,128)S(1)}, u32[]{:S(2)}, u32[]{:S(2)}) collective-permute-start(f32[4,5,32,128]{3,2,1,0:T(8,128)S(1)} %get-tuple-element.74), channel_id=1, source_target_pairs={{0,24},{8,0},{16,8},{24,16},{1,25},{9,1},{17,9},{25,17},{2,26},{10... | collective-permute-start | bytes 983048 | tf_op jit(solution)/shard_map/ppermute | solution.py:245
  10.0 0.8 abs_reduce_fusion
  10.7 0.7 copy.28
  11.4 0.1 reshape.27
  11.5 0.7 reduce
  12.3 0.8 copy.40
  13.2 0.1 pad_maximum_fusion.coef_ref
  13.3 1.0 %copy-done.4 = f32[5,128,128]{2,1,0:T(8,128)S(1)} copy-done((f32[5,128,128]{2,1,0:T(8,128)S(1)}, f32[5,128,128]{2,1,0:T(8,128)}, u32[]{:S(2)}) %copy-start.4) | copy-done | bytes 327704
  14.2 0.8 copy-done.6
  15.1 0.8 copy-done.7
  15.9 5.2 %prep.1 = (f32[4,5,128,128]{3,2,1,0:T(8,128)S(1)}, f32[4,5,32,128]{3,2,1,0:T(8,128)S(1)}, f32[4,5,32,128]{3,2,1,0:T(8,128)S(1)}, f32[128,128]{1,0:T(8,128)S(1)},...) custom-call(f32[4,5,125,1,128]{4,3,2,1,0:T(1,128)S(1)} %bitcast.8, ...), custom_call_target="tpu_custom_call" | custom-call | flops 1 | bytes 1 | tf_op jit(solution)/shard_map/prep/pallas_call | solution.py:158
  21.2 0.1 collective-permute-start.6
  21.2 2.6 %collective-permute-start.7 = (f32[26,32,128]{2,1,0:T(8,128)S(1)}, f32[26,32,128]{2,1,0:T(8,128)S(1)}, u32[]{:S(2)}, u32[]{:S(2)}) collective-permute-start(f32[26,32,128]{2,1,0:T(8,128)S(1)} %get-tuple-element.86.refs_5_), channel_id=1, source_target_pairs={{0,7},{1,0},{2,1},{3,2},{4,3},{5,4},{6,5},{7,6},{8,15},{9,8},{10,9... | collective-permute-start | bytes 1277960 | tf_op jit(solution)/shard_map/ppermute | solution.py:248
  23.9 6.3 %collective-permute-done.1.refs_2_ = f32[4,5,32,128]{3,2,1,0:T(8,128)S(1)} collective-permute-done((f32[4,5,32,128]{3,2,1,0:T(8,128)}, f32[4,5,32,128]{3,2,1,0:T(8,128)S(1)}, u32[]{:S(2)}, u32[]{:S(2)}) %collective-permute-start.1) | collective-permute-done | bytes 327712 | tf_op jit(solution)/shard_map/ppermute | solution.py:245
  30.1 0.9 %coupling.1 = (f32[2,5,32,128]{3,2,1,0:T(8,128)S(1)}, f32[2,5,32,128]{3,2,1,0:T(8,128)S(1)}, f32[2,5,32,128]{3,2,1,0:T(8,128)S(1)}, f32[2,5,32,128]{3,2,1,0:T(8,...) custom-call(f32[4,5,32,128]{3,2,1,0:T(8,128)S(1)} %get-tuple-element, ...), custom_call_target="tpu_custom_call" | custom-call | flops 1 | bytes 1 | tf_op jit(solution)/shard_map/coupling/pallas_call | solution.py:158
  31.0 7.5 %collective-permute-start.3 = (f32[2,5,32,128]{3,2,1,0:T(8,128)S(1)}, f32[2,5,32,128]{3,2,1,0:T(8,128)S(1)}, u32[]{:S(2)}, u32[]{:S(2)}) collective-permute-start(f32[2,5,32,128]{3,2,1,0:T(8,128)S(1)} %get-tuple-element.77), channel_id=1, source_target_pairs={{0,8},{8,16},{16,24},{24,0},{1,9},{9,17},{17,25},{25,1},{2,10},{10... | collective-permute-start | bytes 491528 | tf_op jit(solution)/shard_map/ppermute | solution.py:245
  38.6 1.6 %collective-permute-start.4 = (f32[2,5,32,128]{3,2,1,0:T(8,128)S(1)}, f32[2,5,32,128]{3,2,1,0:T(8,128)S(1)}, u32[]{:S(2)}, u32[]{:S(2)}) collective-permute-start(f32[2,5,32,128]{3,2,1,0:T(8,128)S(1)} %get-tuple-element.78), channel_id=1, source_target_pairs={{0,16},{8,24},{16,0},{24,8},{1,17},{9,25},{17,1},{25,9},{2,18},{10... | collective-permute-start | bytes 491528 | tf_op jit(solution)/shard_map/ppermute | solution.py:245
  40.2 0.9 collective-permute-start.5
  41.0 1.2 %collective-permute-start.8 = (f32[2,5,32,128]{3,2,1,0:T(8,128)S(1)}, f32[2,5,32,128]{3,2,1,0:T(8,128)S(1)}, u32[]{:S(2)}, u32[]{:S(2)}) collective-permute-start(f32[2,5,32,128]{3,2,1,0:T(8,128)S(1)} %get-tuple-element.99), channel_id=1, source_target_pairs={{0,8},{8,16},{16,24},{24,0},{1,9},{9,17},{17,25},{25,1},{2,10},{10... | collective-permute-start | bytes 491528 | tf_op jit(solution)/shard_map/ppermute | solution.py:245
  42.2 2.6 %collective-permute-start.9 = (f32[2,5,32,128]{3,2,1,0:T(8,128)S(1)}, f32[2,5,32,128]{3,2,1,0:T(8,128)S(1)}, u32[]{:S(2)}, u32[]{:S(2)}) collective-permute-start(f32[2,5,32,128]{3,2,1,0:T(8,128)S(1)} %get-tuple-element.100), channel_id=1, source_target_pairs={{0,24},{8,0},{16,8},{24,16},{1,25},{9,1},{17,9},{25,17},{2,26},{10... | collective-permute-start | bytes 491528 | tf_op jit(solution)/shard_map/ppermute | solution.py:245
  44.9 0.6 collective-permute-start.10
  45.4 2.7 %advance.1.z_ref.refs_4_ = f32[4,5,128,128]{3,2,1,0:T(8,128)S(1)} custom-call(f32[4,5,128,128]{3,2,1,0:T(8,128)S(1)} %get-tuple-element.80.refs_0_, f32[4,5,32,128]{3,2,1,0:T(8,128)S(1)} %get-tuple-element.81.refs_1_.lo_ref, f32[4,5,32,128]{3,2,1,0:T(8,128)S(1)} %get-tuple-element.82.refs_2_.hi_ref, f32[128,128]{1,0:T(8,128)S(1)} %get-tuple-element.83.refs_3_.m_ref.refs_9_, ...), custom_call_target="tpu_custom_call" | custom-call | flops 1 | bytes 1 | tf_op jit(solution)/shard_map/advance/pallas_call | solution.py:158
  48.1 0.3 faces.1
  48.4 3.9 %collective-permute-done.4.refs_2_ = f32[2,5,32,128]{3,2,1,0:T(8,128)S(1)} collective-permute-done((f32[2,5,32,128]{3,2,1,0:T(8,128)S(1)}, f32[2,5,32,128]{3,2,1,0:T(8,128)S(1)}, u32[]{:S(2)}, u32[]{:S(2)}) %collective-permute-start.4) | collective-permute-done | bytes 163872 | tf_op jit(solution)/shard_map/ppermute | solution.py:245
  52.3 2.0 %collective-permute-done.5.refs_3_ = f32[2,5,32,128]{3,2,1,0:T(8,128)S(1)} collective-permute-done((f32[2,5,32,128]{3,2,1,0:T(8,128)S(1)}, f32[2,5,32,128]{3,2,1,0:T(8,128)S(1)}, u32[]{:S(2)}, u32[]{:S(2)}) %collective-permute-start.5) | collective-permute-done | bytes 163872 | tf_op jit(solution)/shard_map/ppermute | solution.py:245
  54.3 0.6 first_pass.2
  54.9 1.5 %paired_first.2 = (f32[2,5,128,128]{3,2,1,0:T(8,128)S(1)}, f32[2,2,5,32,128]{4,3,2,1,0:T(8,128)S(1)}, f32[2,2,5,32,128]{4,3,2,1,0:T(8,128)S(1)}, f32[2,2,128,128]{3,2,1,0:T(8,128)S(1)}, f32[2,2,128,128]{3,2,1,0:T(8,128)S(1)}) custom-call(f32[2,5,128,128]{3,2,1,0:T(8,128)S(1)} %get-tuple-element.92.z_ref, f32[2,5,32,128]{3,2,1,0:T(8,128)S(1)} %get-tuple-element.93.lo_ref, ...), custom_call_target="tpu_custom_call" | custom-call | flops 1 | bytes 1 | tf_op jit(solution)/shard_map/paired_first/pallas_call | solution.py:158
  56.4 2.6 %collective-permute-start.14 = (f32[2,2,128,128]{3,2,1,0:T(8,128)S(1)}, f32[2,2,128,128]{3,2,1,0:T(8,128)S(1)}, u32[]{:S(2)}, u32[]{:S(2)}) collective-permute-start(f32[2,2,128,128]{3,2,1,0:T(8,128)S(1)} %get-tuple-element.115), channel_id=1, source_target_pairs={{0,7},{1,0},{2,1},{3,2},{4,3},{5,4},{6,5},{7,6},{8,15},{9,8},{10,9... | collective-permute-start | bytes 786440 | tf_op jit(solution)/shard_map/ppermute | solution.py:248
  59.1 8.5 %collective-permute-done.10.refs_3_ = f32[2,5,32,128]{3,2,1,0:T(8,128)S(1)} collective-permute-done((f32[2,5,32,128]{3,2,1,0:T(8,128)S(1)}, f32[2,5,32,128]{3,2,1,0:T(8,128)S(1)}, u32[]{:S(2)}, u32[]{:S(2)}) %collective-permute-start.10) | collective-permute-done | bytes 163872 | tf_op jit(solution)/shard_map/ppermute | solution.py:245
  67.6 0.6 first_pass.3
  68.2 1.5 %paired_first.3 = (f32[2,5,128,128]{3,2,1,0:T(8,128)S(1)}, f32[2,2,5,32,128]{4,3,2,1,0:T(8,128)S(1)}, f32[2,2,5,32,128]{4,3,2,1,0:T(8,128)S(1)}, f32[2,2,128,128]{3,2,1,0:T(8,128)S(1)}, f32[2,2,128,128]{3,2,1,0:T(8,128)S(1)}) custom-call(f32[2,5,128,128]{3,2,1,0:T(8,128)S(1)} %get-tuple-element.102.z_ref, f32[2,5,32,128]{3,2,1,0:T(8,128)S(1)} %get-tuple-element.103.lo_ref, ...), custom_call_target="tpu_custom_call" | custom-call | flops 1 | bytes 1 | tf_op jit(solution)/shard_map/paired_first/pallas_call | solution.py:158
  69.7 0.1 collective-permute-start.11
  69.7 2.6 %collective-permute-start.12 = (f32[2,2,128,128]{3,2,1,0:T(8,128)S(1)}, f32[2,2,128,128]{3,2,1,0:T(8,128)S(1)}, u32[]{:S(2)}, u32[]{:S(2)}) collective-permute-start(f32[2,2,128,128]{3,2,1,0:T(8,128)S(1)} %get-tuple-element.111), channel_id=1, source_target_pairs={{0,7},{1,0},{2,1},{3,2},{4,3},{5,4},{6,5},{7,6},{8,15},{9,8},{10,9... | collective-permute-start | bytes 786440 | tf_op jit(solution)/shard_map/ppermute | solution.py:248
  72.4 1.7 %paired_second.2 = (f32[2,5,128,128]{3,2,1,0:T(8,128)S(1)}, f32[2,5,32,128]{3,2,1,0:T(8,128)S(1)}, f32[2,5,32,128]{3,2,1,0:T(8,128)S(1)}, f32[2,128,128]{2,1,0:T(8,128)S(1)}, f32[2,128,128]{2,1,0:T(8,128)S(1)}) custom-call(f32[2,5,128,128]{3,2,1,0:T(8,128)S(1)} %get-tuple-element.97.refs_0_, f32[2,2,5,32,128]{4,3,2,1,0:T(8,128)S(1)} %get-tuple-element.112.refs_1_, ...), custom_call_target="tpu_custom_call" | custom-call | flops 1 | bytes 1 | tf_op jit(solution)/shard_map/paired_second/pallas_call | solution.py:158
  74.2 2.6 %collective-permute-start.16 = (f32[2,128,128]{2,1,0:T(8,128)S(1)}, f32[2,128,128]{2,1,0:T(8,128)S(1)}, u32[]{:S(2)}, u32[]{:S(2)}) collective-permute-start(f32[2,128,128]{2,1,0:T(8,128)S(1)} %get-tuple-element.130), channel_id=1, source_target_pairs={{0,7},{1,0},{2,1},{3,2},{4,3},{5,4},{6,5},{7,6},{8,15},{9,8},{10,9... | collective-permute-start | bytes 393224 | tf_op jit(solution)/shard_map/ppermute | solution.py:248
  76.8 1.6 %last_bulk.2 = (f32[2,5,128,128]{3,2,1,0:T(8,128)S(1)}, f32[4,5,125,1,128]{4,3,2,1,0:T(1,128)}) custom-call(f32[2,5,128,128]{3,2,1,0:T(8,128)S(1)} %get-tuple-element.117.refs_0_, f32[2,5,32,128]{3,2,1,0:T(8,128)S(1)} %get-tuple-element.118.refs_1_, f32[2,5,32,128]{3,2,1,0:T(8,128)S(1)} %get-tuple-element.119.refs_2_, ...), custom_call_target="tpu_custom_call" | custom-call | flops 1 | bytes 1 | tf_op jit(solution)/shard_map/last_bulk/pallas_call | solution.py:158
  78.4 0.3 collective-permute-done.12.refs_4_
  78.8 1.7 %paired_second.3 = (f32[2,5,128,128]{3,2,1,0:T(8,128)S(1)}, f32[2,5,32,128]{3,2,1,0:T(8,128)S(1)}, f32[2,5,32,128]{3,2,1,0:T(8,128)S(1)}, f32[2,128,128]{2,1,0:T(8,128)S(1)}, f32[2,128,128]{2,1,0:T(8,128)S(1)}) custom-call(f32[2,5,128,128]{3,2,1,0:T(8,128)S(1)} %get-tuple-element.107.refs_0_, f32[2,2,5,32,128]{4,3,2,1,0:T(8,128)S(1)} %get-tuple-element.108.refs_1_, ...), custom_call_target="tpu_custom_call" | custom-call | flops 1 | bytes 1 | tf_op jit(solution)/shard_map/paired_second/pallas_call | solution.py:158
  80.5 1.5 %collective-permute-start.17 = (f32[2,128,128]{2,1,0:T(8,128)S(1)}, f32[2,128,128]{2,1,0:T(8,128)S(1)}, u32[]{:S(2)}, u32[]{:S(2)}) collective-permute-start(f32[2,128,128]{2,1,0:T(8,128)S(1)} %get-tuple-element.138), channel_id=1, source_target_pairs={{0,1},{1,2},{2,3},{3,4},{4,5},{5,6},{6,7},{7,0},{8,9},{9,10},{10,1... | collective-permute-start | bytes 393224 | tf_op jit(solution)/shard_map/ppermute | solution.py:248
  82.0 1.4 %collective-permute-start.18 = (f32[2,128,128]{2,1,0:T(8,128)S(1)}, f32[2,128,128]{2,1,0:T(8,128)S(1)}, u32[]{:S(2)}, u32[]{:S(2)}) collective-permute-start(f32[2,128,128]{2,1,0:T(8,128)S(1)} %get-tuple-element.139), channel_id=1, source_target_pairs={{0,7},{1,0},{2,1},{3,2},{4,3},{5,4},{6,5},{7,6},{8,15},{9,8},{10,9... | collective-permute-start | bytes 393224 | tf_op jit(solution)/shard_map/ppermute | solution.py:248
  83.4 1.2 %last_faces.2.refs_8_ = f32[4,5,125,1,128]{4,3,2,1,0:T(1,128)} custom-call(f32[2,5,128,128]{3,2,1,0:T(8,128)S(1)} %get-tuple-element.126.refs_0_, f32[2,5,32,128]{3,2,1,0:T(8,128)S(1)} %get-tuple-element.118.refs_1_, f32[2,5,32,128]{3,2,1,0:T(8,128)S(1)} %get-tuple-element.119.refs_2_, f32[2,128,128]{2,1,0:T(8,128)S(1)} %collective-permute-done.15.refs_3_, ...), custom_call_target="tpu_custom_call" | custom-call | flops 1 | bytes 1 | tf_op jit(solution)/shard_map/last_faces/pallas_call | solution.py:158
  84.7 1.6 %last_bulk.3 = (f32[2,5,128,128]{3,2,1,0:T(8,128)S(1)}, f32[4,5,125,1,128]{4,3,2,1,0:T(1,128)}) custom-call(f32[2,5,128,128]{3,2,1,0:T(8,128)S(1)} %get-tuple-element.123.refs_0_, f32[2,5,32,128]{3,2,1,0:T(8,128)S(1)} %get-tuple-element.124.refs_1_, f32[2,5,32,128]{3,2,1,0:T(8,128)S(1)} %get-tuple-element.125.refs_2_, ...), custom_call_target="tpu_custom_call", output_to_operand_aliasing={{1}: (7, {})} | custom-call | flops 1 | bytes 1 | tf_op jit(solution)/shard_map/last_bulk/pallas_call | solution.py:158
  86.2 0.3 collective-permute-done.17.refs_3_
  86.5 1.3 %last_faces.3 = f32[4,5,125,1,128]{4,3,2,1,0:T(1,128)} custom-call(f32[2,5,128,128]{3,2,1,0:T(8,128)S(1)} %get-tuple-element.135.refs_0_, f32[2,5,32,128]{3,2,1,0:T(8,128)S(1)} %get-tuple-element.124.refs_1_, f32[2,5,32,128]{3,2,1,0:T(8,128)S(1)} %get-tuple-element.125.refs_2_, ...), custom_call_target="tpu_custom_call", output_to_operand_aliasing={{}: (8, {})} | custom-call | flops 1 | bytes 1 | tf_op jit(solution)/shard_map/last_faces/pallas_call | solution.py:158
  (35 shorter events, 0.2 us)
Async XLA Ops:
  0.6 1.3 %copy-start = (f32[4,5,1,125,128]{4,2,3,1,0:T(1,128)S(1)}, f32[4,5,1,125,128]{4,2,3,1,0:T(1,128)}, u32[]{:S(2)}) copy-start(f32[4,5,1,125,128]{4,2,3,1,0:T(1,128)} %param.13) | copy-start | bytes 3840004
  1.9 11.3 %copy-start.1 = (f32[4,5,1,125,128]{4,2,3,1,0:T(1,128)S(1)}, f32[4,5,1,125,128]{4,2,3,1,0:T(1,128)}, u32[]{:S(2)}) copy-start(f32[4,5,1,125,128]{4,2,3,1,0:T(1,128)} %param.13) | copy-start | bytes 3840004
  1.9 11.3 %copy-start.3 = (f32[5,128,128]{2,1,0:T(8,128)S(1)}, f32[5,128,128]{2,1,0:T(8,128)}, u32[]{:S(2)}) copy-start(f32[5,128,128]{2,1,0:T(8,128)} %constant.22.clone.damp_ref) | copy-start | bytes 983044
  1.9 11.3 %copy-start.5 = (s32[128,128]{1,0:T(8,128)S(1)}, s32[128,128]{1,0:T(8,128)}, u32[]{:S(2)}) copy-start(s32[128,128]{1,0:T(8,128)} %constant.24.clone.mix_ref) | copy-start | bytes 196612
  1.9 11.3 %copy-start.9 = (bf16[128,128]{1,0:T(8,128)(2,1)S(1)}, bf16[128,128]{1,0:T(8,128)(2,1)}, u32[]{:S(2)}) copy-start(bf16[128,128]{1,0:T(8,128)(2,1)} %constant.20.clone.order_ref) | copy-start | bytes 98308
  2.9 20.9 %collective-permute-start = (f32[4,5,32,128]{3,2,1,0:T(8,128)}, f32[4,5,32,128]{3,2,1,0:T(8,128)S(1)}, u32[]{:S(2)}, u32[]{:S(2)}) collective-permute-start(f32[4,5,32,128]{3,2,1,0:T(8,128)} %get-tuple-element.72), channel_id=1, source_target_pairs={{0,8},{8,16},{16,24},{24,0},{1,9},{9,17},{17,25},{25,1},{2,10},{10... | collective-permute-start | bytes 983048 | tf_op jit(solution)/shard_map/ppermute | solution.py:245
  6.0 24.1 %collective-permute-start.1 = (f32[4,5,32,128]{3,2,1,0:T(8,128)}, f32[4,5,32,128]{3,2,1,0:T(8,128)S(1)}, u32[]{:S(2)}, u32[]{:S(2)}) collective-permute-start(f32[4,5,32,128]{3,2,1,0:T(8,128)} %get-tuple-element.73), channel_id=1, source_target_pairs={{0,16},{8,24},{16,0},{24,8},{1,17},{9,25},{17,1},{25,9},{2,18},{10... | collective-permute-start | bytes 983048 | tf_op jit(solution)/shard_map/ppermute | solution.py:245
  8.6 21.5 %collective-permute-start.2 = (f32[4,5,32,128]{3,2,1,0:T(8,128)S(1)}, f32[4,5,32,128]{3,2,1,0:T(8,128)S(1)}, u32[]{:S(2)}, u32[]{:S(2)}) collective-permute-start(f32[4,5,32,128]{3,2,1,0:T(8,128)S(1)} %get-tuple-element.74), channel_id=1, source_target_pairs={{0,24},{8,0},{16,8},{24,16},{1,25},{9,1},{17,9},{25,17},{2,26},{10... | collective-permute-start | bytes 983048 | tf_op jit(solution)/shard_map/ppermute | solution.py:245
  13.3 1.0 %copy-start.4 = (f32[5,128,128]{2,1,0:T(8,128)S(1)}, f32[5,128,128]{2,1,0:T(8,128)}, u32[]{:S(2)}) copy-start(f32[5,128,128]{2,1,0:T(8,128)} %constant.21.clone.flux_ref) | copy-start | bytes 983044
  14.2 0.8 copy-start.6
  15.1 0.8 copy-start.7
  21.2 19.9 %collective-permute-start.6 = (f32[26,32,128]{2,1,0:T(8,128)S(1)}, f32[26,32,128]{2,1,0:T(8,128)S(1)}, u32[]{:S(2)}, u32[]{:S(2)}) collective-permute-start(f32[26,32,128]{2,1,0:T(8,128)S(1)} %get-tuple-element.85.refs_6_), channel_id=1, source_target_pairs={{0,1},{1,2},{2,3},{3,4},{4,5},{5,6},{6,7},{7,0},{8,9},{9,10},{10,1... | collective-permute-start | bytes 1277960 | tf_op jit(solution)/shard_map/ppermute | solution.py:248
  21.2 21.0 %collective-permute-start.7 = (f32[26,32,128]{2,1,0:T(8,128)S(1)}, f32[26,32,128]{2,1,0:T(8,128)S(1)}, u32[]{:S(2)}, u32[]{:S(2)}) collective-permute-start(f32[26,32,128]{2,1,0:T(8,128)S(1)} %get-tuple-element.86.refs_5_), channel_id=1, source_target_pairs={{0,7},{1,0},{2,1},{3,2},{4,3},{5,4},{6,5},{7,6},{8,15},{9,8},{10,9... | collective-permute-start | bytes 1277960 | tf_op jit(solution)/shard_map/ppermute | solution.py:248
  31.0 13.8 %collective-permute-start.3 = (f32[2,5,32,128]{3,2,1,0:T(8,128)S(1)}, f32[2,5,32,128]{3,2,1,0:T(8,128)S(1)}, u32[]{:S(2)}, u32[]{:S(2)}) collective-permute-start(f32[2,5,32,128]{3,2,1,0:T(8,128)S(1)} %get-tuple-element.77), channel_id=1, source_target_pairs={{0,8},{8,16},{16,24},{24,0},{1,9},{9,17},{17,25},{25,1},{2,10},{10... | collective-permute-start | bytes 491528 | tf_op jit(solution)/shard_map/ppermute | solution.py:245
  38.6 13.7 %collective-permute-start.4 = (f32[2,5,32,128]{3,2,1,0:T(8,128)S(1)}, f32[2,5,32,128]{3,2,1,0:T(8,128)S(1)}, u32[]{:S(2)}, u32[]{:S(2)}) collective-permute-start(f32[2,5,32,128]{3,2,1,0:T(8,128)S(1)} %get-tuple-element.78), channel_id=1, source_target_pairs={{0,16},{8,24},{16,0},{24,8},{1,17},{9,25},{17,1},{25,9},{2,18},{10... | collective-permute-start | bytes 491528 | tf_op jit(solution)/shard_map/ppermute | solution.py:245
  40.2 14.1 %collective-permute-start.5 = (f32[2,5,32,128]{3,2,1,0:T(8,128)S(1)}, f32[2,5,32,128]{3,2,1,0:T(8,128)S(1)}, u32[]{:S(2)}, u32[]{:S(2)}) collective-permute-start(f32[2,5,32,128]{3,2,1,0:T(8,128)S(1)} %get-tuple-element.79), channel_id=1, source_target_pairs={{0,24},{8,0},{16,8},{24,16},{1,25},{9,1},{17,9},{25,17},{2,26},{10... | collective-permute-start | bytes 491528 | tf_op jit(solution)/shard_map/ppermute | solution.py:245
  41.0 18.1 %collective-permute-start.8 = (f32[2,5,32,128]{3,2,1,0:T(8,128)S(1)}, f32[2,5,32,128]{3,2,1,0:T(8,128)S(1)}, u32[]{:S(2)}, u32[]{:S(2)}) collective-permute-start(f32[2,5,32,128]{3,2,1,0:T(8,128)S(1)} %get-tuple-element.99), channel_id=1, source_target_pairs={{0,8},{8,16},{16,24},{24,0},{1,9},{9,17},{17,25},{25,1},{2,10},{10... | collective-permute-start | bytes 491528 | tf_op jit(solution)/shard_map/ppermute | solution.py:245
  42.2 16.9 %collective-permute-start.9 = (f32[2,5,32,128]{3,2,1,0:T(8,128)S(1)}, f32[2,5,32,128]{3,2,1,0:T(8,128)S(1)}, u32[]{:S(2)}, u32[]{:S(2)}) collective-permute-start(f32[2,5,32,128]{3,2,1,0:T(8,128)S(1)} %get-tuple-element.100), channel_id=1, source_target_pairs={{0,24},{8,0},{16,8},{24,16},{1,25},{9,1},{17,9},{25,17},{2,26},{10... | collective-permute-start | bytes 491528 | tf_op jit(solution)/shard_map/ppermute | solution.py:245
  44.9 22.7 %collective-permute-start.10 = (f32[2,5,32,128]{3,2,1,0:T(8,128)S(1)}, f32[2,5,32,128]{3,2,1,0:T(8,128)S(1)}, u32[]{:S(2)}, u32[]{:S(2)}) collective-permute-start(f32[2,5,32,128]{3,2,1,0:T(8,128)S(1)} %get-tuple-element.101), channel_id=1, source_target_pairs={{0,16},{8,24},{16,0},{24,8},{1,17},{9,25},{17,1},{25,9},{2,18},{10... | collective-permute-start | bytes 491528 | tf_op jit(solution)/shard_map/ppermute | solution.py:245
  48.1 6.2 %copy-start.8 = (bf16[128,128]{1,0:T(8,128)(2,1)S(1)}, bf16[128,128]{1,0:T(8,128)(2,1)}, u32[]{:S(2)}) copy-start(bf16[128,128]{1,0:T(8,128)(2,1)} %constant.25.clone.refs_9_) | copy-start | bytes 98308
  56.4 16.0 %collective-permute-start.13 = (f32[2,2,128,128]{3,2,1,0:T(8,128)S(1)}, f32[2,2,128,128]{3,2,1,0:T(8,128)S(1)}, u32[]{:S(2)}, u32[]{:S(2)}) collective-permute-start(f32[2,2,128,128]{3,2,1,0:T(8,128)S(1)} %get-tuple-element.114), channel_id=1, source_target_pairs={{0,1},{1,2},{2,3},{3,4},{4,5},{5,6},{6,7},{7,0},{8,9},{9,10},{10,1... | collective-permute-start | bytes 786440 | tf_op jit(solution)/shard_map/ppermute | solution.py:248
  56.4 15.9 %collective-permute-start.14 = (f32[2,2,128,128]{3,2,1,0:T(8,128)S(1)}, f32[2,2,128,128]{3,2,1,0:T(8,128)S(1)}, u32[]{:S(2)}, u32[]{:S(2)}) collective-permute-start(f32[2,2,128,128]{3,2,1,0:T(8,128)S(1)} %get-tuple-element.115), channel_id=1, source_target_pairs={{0,7},{1,0},{2,1},{3,2},{4,3},{5,4},{6,5},{7,6},{8,15},{9,8},{10,9... | collective-permute-start | bytes 786440 | tf_op jit(solution)/shard_map/ppermute | solution.py:248
  69.7 8.7 %collective-permute-start.11 = (f32[2,2,128,128]{3,2,1,0:T(8,128)S(1)}, f32[2,2,128,128]{3,2,1,0:T(8,128)S(1)}, u32[]{:S(2)}, u32[]{:S(2)}) collective-permute-start(f32[2,2,128,128]{3,2,1,0:T(8,128)S(1)} %get-tuple-element.110), channel_id=1, source_target_pairs={{0,1},{1,2},{2,3},{3,4},{4,5},{5,6},{6,7},{7,0},{8,9},{9,10},{10,1... | collective-permute-start | bytes 786440 | tf_op jit(solution)/shard_map/ppermute | solution.py:248
  69.7 9.0 %collective-permute-start.12 = (f32[2,2,128,128]{3,2,1,0:T(8,128)S(1)}, f32[2,2,128,128]{3,2,1,0:T(8,128)S(1)}, u32[]{:S(2)}, u32[]{:S(2)}) collective-permute-start(f32[2,2,128,128]{3,2,1,0:T(8,128)S(1)} %get-tuple-element.111), channel_id=1, source_target_pairs={{0,7},{1,0},{2,1},{3,2},{4,3},{5,4},{6,5},{7,6},{8,15},{9,8},{10,9... | collective-permute-start | bytes 786440 | tf_op jit(solution)/shard_map/ppermute | solution.py:248
  72.4 4.4 %copy-start.2 = (bf16[128,128]{1,0:T(8,128)(2,1)S(1)}, bf16[128,128]{1,0:T(8,128)(2,1)}, u32[]{:S(2)}) copy-start(bf16[128,128]{1,0:T(8,128)(2,1)} %constant.26.clone.refs_6_.refs_7_) | copy-start | bytes 98308
  74.1 9.3 %collective-permute-start.15 = (f32[2,128,128]{2,1,0:T(8,128)S(1)}, f32[2,128,128]{2,1,0:T(8,128)S(1)}, u32[]{:S(2)}, u32[]{:S(2)}) collective-permute-start(f32[2,128,128]{2,1,0:T(8,128)S(1)} %get-tuple-element.129), channel_id=1, source_target_pairs={{0,1},{1,2},{2,3},{3,4},{4,5},{5,6},{6,7},{7,0},{8,9},{9,10},{10,1... | collective-permute-start | bytes 393224 | tf_op jit(solution)/shard_map/ppermute | solution.py:248
  74.2 9.2 %collective-permute-start.16 = (f32[2,128,128]{2,1,0:T(8,128)S(1)}, f32[2,128,128]{2,1,0:T(8,128)S(1)}, u32[]{:S(2)}, u32[]{:S(2)}) collective-permute-start(f32[2,128,128]{2,1,0:T(8,128)S(1)} %get-tuple-element.130), channel_id=1, source_target_pairs={{0,7},{1,0},{2,1},{3,2},{4,3},{5,4},{6,5},{7,6},{8,15},{9,8},{10,9... | collective-permute-start | bytes 393224 | tf_op jit(solution)/shard_map/ppermute | solution.py:248
  80.5 6.0 %collective-permute-start.17 = (f32[2,128,128]{2,1,0:T(8,128)S(1)}, f32[2,128,128]{2,1,0:T(8,128)S(1)}, u32[]{:S(2)}, u32[]{:S(2)}) collective-permute-start(f32[2,128,128]{2,1,0:T(8,128)S(1)} %get-tuple-element.138), channel_id=1, source_target_pairs={{0,1},{1,2},{2,3},{3,4},{4,5},{5,6},{6,7},{7,0},{8,9},{9,10},{10,1... | collective-permute-start | bytes 393224 | tf_op jit(solution)/shard_map/ppermute | solution.py:248
  82.0 4.5 %collective-permute-start.18 = (f32[2,128,128]{2,1,0:T(8,128)S(1)}, f32[2,128,128]{2,1,0:T(8,128)S(1)}, u32[]{:S(2)}, u32[]{:S(2)}) collective-permute-start(f32[2,128,128]{2,1,0:T(8,128)S(1)} %get-tuple-element.139), channel_id=1, source_target_pairs={{0,7},{1,0},{2,1},{3,2},{4,3},{5,4},{6,5},{7,6},{8,15},{9,8},{10,9... | collective-permute-start | bytes 393224 | tf_op jit(solution)/shard_map/ppermute | solution.py:248
